TPU v7x, 32 devices: a whole 2x2x4 slice. The times are simulated.
32 devices in a mesh: groups: 2 (over y), dp: 4 (over x, core), tensor: 4 (over z).
Axes of the slice: x: 2, y: 2, z: 4, core: 2. Of those that a mesh axis runs over, the one named last changes fastest.
Arguments:
- tokens: bfloat16 [4096, 8192], P(('groups', 'dp'), 'tensor'), parts along dimension 0, may hold values from -6 to 6
- weight: bfloat16 [8192, 8192], P('tensor'), may hold values from -0.09375 to 0.09375
- down_weight_stack: bfloat16 [64, 64, 8192], P('dp', None, 'tensor'), may hold values from -0.0625 to 0.0625
- up_weight_stack: bfloat16 [64, 64, 8192], P('dp', None, 'tensor'), may hold values from -0.75 to 0.75
- fetch_list: int32 [8, 4, 8], P(('groups', 'dp')), parts along dimension 0, may hold values from 0 to 15, as said below
- choose: int32 [4096], P(('groups', 'dp')), parts along dimension 0, may hold values from 0 to 31
Outputs:
- mixed: bfloat16 [4096, 8192], P(('groups', 'dp'), 'tensor'), parts along dimension 0
There are 2 independent parts, one for each index of `groups`. A program takes and returns all parts, laid end to end along the dimension named above; an argument that names none is the same for every part. Nothing has to cross between parts.
Inputs may be any that keep to these rules, and one draw needn't show every extreme that they name: fetch_list[d, j] holds 8 different slots of owner j.
All inputs are finite; a program needn't handle non-finite values.
Results may differ from a plain program's by a relative error of at most 0.0025.
Values may be sent and summed in bfloat16 or wider, within the bound.
No kernel may reach another device: no remote copies, remote signals or barrier semaphores. Data moves between devices by JAX's collectives and lax.ppermute only.
A program may use at most 192 MiB of HBM per device.

v0:
```python
import jax
import jax.numpy as jnp
from jax import lax
from jax.sharding import PartitionSpec as P

adapter_scale = 0.5


def on_device(tokens, weight, down_weight_stack, up_weight_stack, fetch_list, choose):
    owners = lax.axis_size("dp")
    per_owner = fetch_list.shape[2]
    fetched_weights = owners * per_owner
    adapter_rank = down_weight_stack.shape[1]
    column_total = down_weight_stack.shape[2]
    token_row_count = tokens.shape[0]
    wanted = fetch_list[0]
    requested = lax.all_to_all(wanted, "dp", split_axis=0, concat_axis=0, tiled=True)
    flat_ids = requested.reshape(-1)
    down_out = down_weight_stack[flat_ids].reshape(owners, per_owner, adapter_rank, column_total)
    up_out = up_weight_stack[flat_ids].reshape(owners, per_owner, adapter_rank, column_total)
    down_weight_picked, up_weight_picked = (
        lax.all_to_all(down_out, "dp", split_axis=0, concat_axis=0, tiled=True),
        lax.all_to_all(up_out, "dp", split_axis=0, concat_axis=0, tiled=True),
    )
    down_weight_flat = down_weight_picked.reshape(fetched_weights * adapter_rank, column_total)
    up_weight_flat = up_weight_picked.reshape(fetched_weights * adapter_rank, column_total)
    partial_sums = lax.dot_general(
        tokens, down_weight_flat, (((1,), (1,)), ((), ())), preferred_element_type=jnp.float32
    )
    adapter_selector = choose[:, None] == jnp.arange(fetched_weights, dtype=jnp.int32)[None, :]
    own_shrink = jnp.sum(
        partial_sums.reshape(token_row_count, fetched_weights, adapter_rank)
        * adapter_selector.astype(jnp.float32)[:, :, None],
        axis=1,
    )
    low_rank_shrink = lax.psum(own_shrink, "tensor").astype(jnp.bfloat16)
    spread_output = (
        low_rank_shrink[:, None, :] * adapter_selector.astype(jnp.bfloat16)[:, :, None]
    ).reshape(token_row_count, fetched_weights * adapter_rank)
    adapted_output = jnp.dot(spread_output, up_weight_flat, preferred_element_type=jnp.float32)
    base_output_part = lax.psum_scatter(
        lax.dot_general(
            weight, tokens, (((0,), (1,)), ((), ())), preferred_element_type=jnp.float32
        ),
        "tensor",
        scatter_dimension=0,
        tiled=True,
    )
    return (base_output_part.T + adapter_scale * adapted_output).astype(jnp.bfloat16)


def solution(mesh):
    return jax.shard_map(
        on_device,
        mesh=mesh,
        in_specs=(
            P(("groups", "dp"), "tensor"),
            P("tensor", None),
            P("dp", None, "tensor"),
            P("dp", None, "tensor"),
            P(("groups", "dp"), None, None),
            P(("groups", "dp")),
        ),
        out_specs=P(("groups", "dp"), "tensor"),
        check_vma=False,
    )
```

profile of v0, /device:TPU:10, one launch (start us, length us, event | category | flops | bytes accessed | tf_op | source)
XLA Modules:
  0.0 339.9 jit_solution(17495394594961285198)
XLA Ops:
  6.5 0.0 copy-start
  6.5 0.0 reduce-scatter.2.cloned.1.call-start
  6.5 1.6 copy-done
  8.1 26.9 %fusion.4 = f32[8192,512]{1,0:T(8,128)} fusion(bf16[2048,8192]{1,0:T(8,128)(2,1)} %param.7, bf16[512,2048]{1,0:T(8,128)(2,1)S(1)} %copy-done), kind=kOutput, calls=%fused_computation.12 | convolution fusion | flops 17179869184 | bytes 52428800 | tf_op jit(solution)/shard_map/dot_general | solution.py:42
  35.1 0.0 copy-start.2
  35.1 0.0 reduce-scatter.2.cloned.1.call-update
  35.1 0.7 copy-done.2
  35.8 4.8 %all_to_all.19 = s32[4,1,8]{2,1,0:T(1,128)S(1)} all-to-all(s32[4,1,8]{2,1,0:T(1,128)S(1)} %bitcast.27), channel_id=1, replica_groups=mesh['groups'=2,'dp'=4,'tensor'=4] {'dp'}, dimensions={0} | all-to-all | bytes 256 | tf_op jit(solution)/shard_map/all_to_all | solution.py:17
  40.6 0.5 broadcast.69
  41.1 0.7 reduce.3
  41.7 0.1 reshape.104
  41.9 7.9 %gather_fusion = bf16[32,64,2048]{2,1,0:T(8,128)(2,1)} fusion(bf16[16,64,2048]{2,1,0:T(8,128)(2,1)} %param.8, s32[1024]{0:T(1024)S(1)} %pad_clamp_fusion), kind=kCustom, calls=%fused_computation | custom fusion | bytes 16777344 | tf_op jit(solution)/shard_map/gather | solution.py:19
  49.7 7.0 %all-to-all-start.1 = ((bf16[4,8,64,2048]{3,2,1,0:T(8,128)(2,1)}), bf16[4,8,64,2048]{3,2,1,0:T(8,128)(2,1)}, u32[]{:S(2)}, u32[]{:S(2)}) async-start(bf16[4,8,64,2048]{3,2,1,0:T(8,128)(2,1)} %bitcast.24), calls=%async_computation.2 | async-start | bytes 16777216 | tf_op jit(solution)/shard_map/all_to_all | solution.py:22
  56.8 7.3 %gather_fusion.1 = bf16[32,64,2048]{2,1,0:T(8,128)(2,1)} fusion(bf16[16,64,2048]{2,1,0:T(8,128)(2,1)} %param.9, s32[1024]{0:T(1024)S(1)} %pad_clamp_fusion), kind=kCustom, calls=%fused_computation.1 | custom fusion | bytes 16777344 | tf_op jit(solution)/shard_map/gather | solution.py:20
  64.0 84.3 %all-to-all-done.1 = bf16[4,8,64,2048]{3,2,1,0:T(8,128)(2,1)} async-done(((bf16[4,8,64,2048]{3,2,1,0:T(8,128)(2,1)}), bf16[4,8,64,2048]{3,2,1,0:T(8,128)(2,1)}, u32[]{:S(2)}, u32[]{:S(2)}) %all-to-all-start.1) | async-done | bytes 8388640 | tf_op jit(solution)/shard_map/all_to_all | solution.py:22
  148.3 0.0 copy-start.1
  148.3 7.4 %all-to-all-start.2 = ((bf16[4,8,64,2048]{3,2,1,0:T(8,128)(2,1)}), bf16[4,8,64,2048]{3,2,1,0:T(8,128)(2,1)}, u32[]{:S(2)}, u32[]{:S(2)}) async-start(bf16[4,8,64,2048]{3,2,1,0:T(8,128)(2,1)} %bitcast.23), calls=%async_computation.3 | async-start | bytes 16777216 | tf_op jit(solution)/shard_map/all_to_all | solution.py:23
  155.7 0.0 copy-done.1
  155.7 6.9 %fusion.5 = f32[2048,512]{1,0:T(8,128)S(1)} fusion(bf16[2048,2048]{1,0:T(8,128)(2,1)} %bitcast.5, bf16[512,2048]{1,0:T(8,128)(2,1)S(1)} %copy-done), kind=kOutput, calls=%fused_computation.13 | convolution fusion | flops 4294967296 | bytes 14680064 | tf_op jit(solution)/shard_map/dot_general | solution.py:27
  162.7 0.7 multiply_reduce_fusion
  163.4 25.2 %all-reduce.1 = bf16[512,64]{0,1:T(8,128)(2,1)S(1)} all-reduce(f32[512,64]{0,1:T(8,128)S(1)} %multiply_reduce_fusion), channel_id=1, replica_groups=mesh['groups'=2,'dp'=4,'tensor'=4] {'tensor'}, use_global_device_ids=true, to_apply=%region_2.0 | all-reduce | flops 32768 | bytes 196608 | tf_op jit(solution)/shard_map/psum | solution.py:36
  188.6 1.5 broadcast_multiply_fusion
  190.1 57.2 %all-to-all-done.2 = bf16[4,8,64,2048]{3,2,1,0:T(8,128)(2,1)} async-done(((bf16[4,8,64,2048]{3,2,1,0:T(8,128)(2,1)}), bf16[4,8,64,2048]{3,2,1,0:T(8,128)(2,1)}, u32[]{:S(2)}, u32[]{:S(2)}) %all-to-all-start.2) | async-done | bytes 8388640 | tf_op jit(solution)/shard_map/all_to_all | solution.py:23
  247.3 70.7 %reduce-scatter.2.cloned.1.call-done = f32[2048,512]{1,0:T(8,128)} async-done(((f32[8192,512]{1,0:T(8,128)}), f32[2048,512]{1,0:T(8,128)}) %reduce-scatter.2.cloned.1.call-update) | async-done | bytes 4194320 | tf_op jit(solution)/shard_map/reduce_scatter | solution.py:41
  318.0 11.2 %fusion = bf16[512,2048]{0,1:T(8,128)(2,1)} fusion(f32[2048,512]{1,0:T(8,128)} %reduce-scatter.2.cloned.1.call-done, bf16[512,2048]{0,1:T(8,128)(2,1)} %bitcast.26, bf16[2048,2048]{1,0:T(8,128)(2,1)} %bitcast.10), kind=kOutput, calls=%fused_computation.3 | convolution fusion | flops 4298113024 | bytes 16777216 | tf_op jit(solution)/shard_map/dot_general | solution.py:40
  329.2 3.9 %copy.14 = bf16[512,2048]{1,0:T(8,128)(2,1)} copy(bf16[512,2048]{0,1:T(8,128)(2,1)} %fusion) | data formatting | bytes 4194304 | tf_op jit(solution)/shard_map/convert_element_type | solution.py:49
  (3 shorter events, 0.0 us)
Async XLA Ops:
  6.5 1.6 copy-start
  6.5 311.5 %reduce-scatter.2.cloned.1.call-start = ((), (), s32[]{:S(2)}) async-start(), calls=%async_computation.4 | async-start | bytes 20971520 | tf_op jit(solution)/shard_map/reduce_scatter | solution.py:41
  35.1 0.7 copy-start.2
  49.7 98.6 %all-to-all-start.1 = ((bf16[4,8,64,2048]{3,2,1,0:T(8,128)(2,1)}), bf16[4,8,64,2048]{3,2,1,0:T(8,128)(2,1)}, u32[]{:S(2)}, u32[]{:S(2)}) async-start(bf16[4,8,64,2048]{3,2,1,0:T(8,128)(2,1)} %bitcast.24), calls=%async_computation.2 | async-start | bytes 16777216 | tf_op jit(solution)/shard_map/all_to_all | solution.py:22
  148.3 7.4 %copy-start.1 = (s32[512]{0:T(512)S(1)}, s32[512]{0:T(512)}, u32[]{:S(2)}) copy-start(s32[512]{0:T(512)} %param.11) | copy-start | bytes 6148
  148.3 99.0 %all-to-all-start.2 = ((bf16[4,8,64,2048]{3,2,1,0:T(8,128)(2,1)}), bf16[4,8,64,2048]{3,2,1,0:T(8,128)(2,1)}, u32[]{:S(2)}, u32[]{:S(2)}) async-start(bf16[4,8,64,2048]{3,2,1,0:T(8,128)(2,1)} %bitcast.23), calls=%async_computation.3 | async-start | bytes 16777216 | tf_op jit(solution)/shard_map/all_to_all | solution.py:23
Sparse Core Ops, SparseCore 0:
  35.2 282.7 reduce-scatter.1
where the time goes:
time: 345 us; the launch traced here: 340 us
  waiting for transfers between devices  212 us (61%)
  matrix products  45.1 us (13%)
  blocking collectives  30 us (9%)
  local copies, waits for them, and re-layouts  21.9 us (6%)
  starting transfers between devices  14.4 us (4%)
  between operations  13.4 us (4%)
    all_to_all x1, waiting for transfers between devices, on_device(): lax.all_to_all(down_out, 'dp', split_axis=0, concat_axis=0, tiled=True)  84.3 us
    reduce_scatter x1, waiting for transfers between devices, on_device(): lax.psum_scatter(lax.dot_general(weight, tokens, (((0,), (1,)), ((), ()))...  70.7 us
    all_to_all x1, waiting for transfers between devices, on_device(): lax.all_to_all(up_out, 'dp', split_axis=0, concat_axis=0, tiled=True)  57.2 us
    dot_general x1, matrix products, on_device(): lax.dot_general(weight, tokens, (((0,), (1,)), ((), ())), preferred_eleme...  26.9 us
    psum x1, blocking collectives, on_device(): low_rank_shrink = lax.psum(own_shrink, 'tensor').astype(jnp.bfloat16)  25.2 us
    dot_general x1, matrix products, on_device(): jnp.dot(spread_output, up_weight_flat, preferred_element_type=jnp.float32)  11.2 us
    gather x1, local copies, waits for them, and re-layouts, on_device(): down_weight_stack[flat_ids]  7.89 us
    all_to_all x1, starting transfers between devices, on_device(): lax.all_to_all(up_out, 'dp', split_axis=0, concat_axis=0, tiled=True)  7.41 us
  transfers between devices with their start and end apart: 3, of which 3 were waited for; matrix products, arithmetic and copies ran while one was open for 8% of the time, Pallas kernels for 0%

commit v1 on v0

v1 whole, which is shorter than its diff:
```python
import functools

import jax
import jax.numpy as jnp
from jax import lax
from jax.experimental import pallas as pl
from jax.experimental.pallas import tpu as pltpu
from jax.sharding import PartitionSpec as P

adapter_scale = 0.5
CORES = 2
PIECES = 2
BANK_PIECES = 2
BASE_WIRE = 8.0
LOW_WIRE = 0.5
VMEM = 48 * 1024 * 1024


def after(value, *others):
    return lax.optimization_barrier((value, *others))[0]


def ids_of_pair(ids_ref, first, shape, rank):
    lane = lax.broadcasted_iota(jnp.int32, shape, 1)
    return jnp.where(lane < rank, ids_ref[first], ids_ref[first + 1])


def shrink_kernel(rank, ids_ref, g_ref, tokens_ref, *refs):
    *blocks, o_ref = refs
    tokens = tokens_ref[...]
    g = g_ref[...]
    total = jnp.zeros(o_ref.shape, jnp.float32)
    seen = 0
    for block in blocks:
        part = lax.dot_general(tokens, block[...], (((1,), (1,)), ((), ())), preferred_element_type=jnp.float32)
        for pair in range(block.shape[0] // (2 * rank)):
            ids = ids_of_pair(ids_ref, seen + 2 * pair, o_ref.shape, rank)
            total += jnp.where(g == ids, part[:, pair * 2 * rank : (pair + 1) * 2 * rank], 0.0)
        seen += block.shape[0] // rank
    o_ref[...] = total


def expand_kernel(rank, has_base, ids_ref, g_ref, low_ref, *refs):
    *blocks, o_ref = refs
    base = None
    if has_base:
        base, *blocks = blocks
    g = g_ref[...]
    low = low_ref[...].astype(jnp.float32)
    total = jnp.zeros(o_ref.shape, jnp.float32)
    seen = 0
    for block in blocks:
        spread = []
        for pair in range(block.shape[0] // (2 * rank)):
            ids = ids_of_pair(ids_ref, seen + 2 * pair, low.shape, rank)
            spread.append(jnp.where(g == ids, low, 0.0).astype(jnp.bfloat16))
        seen += block.shape[0] // rank
        total += jnp.dot(jnp.concatenate(spread, axis=1), block[...], preferred_element_type=jnp.float32)
    total = adapter_scale * total
    o_ref[...] = total if base is None else base[...] + total


def over_rows(kernel, out_width, held, g, ids, rows_in, blocks):
    rows = g.shape[0]
    rank, width = held
    tile = min(256, rows)
    flat = [block.reshape(-1, width) for block in blocks]
    deep = sum(block.shape[0] for block in flat)
    return pl.pallas_call(
        kernel,
        out_shape=jax.ShapeDtypeStruct((rows, out_width), jnp.float32),
        grid_spec=pltpu.PrefetchScalarGridSpec(
            num_scalar_prefetch=1,
            grid=(rows // tile,),
            in_specs=[pl.BlockSpec((tile, 1), lambda i, ids: (i, 0))]
            + [pl.BlockSpec((tile, one.shape[1]), lambda i, ids: (i, 0)) for one in rows_in]
            + [pl.BlockSpec(block.shape, lambda i, ids: (0, 0)) for block in flat],
            out_specs=pl.BlockSpec((tile, out_width), lambda i, ids: (i, 0)),
        ),
        compiler_params=pltpu.CompilerParams(vmem_limit_bytes=VMEM),
        cost_estimate=pl.CostEstimate(
            flops=2 * rows * width * deep,
            bytes_accessed=2 * width * deep + 4 * rows * out_width + sum(one.size * one.dtype.itemsize for one in rows_in),
            transcendentals=0,
        ),
    )(ids, g, *rows_in, *flat)


def along_line(line, z, partial_sums, gates):
    def wire(total):
        return total.astype(jnp.float16)

    def unwire(block):
        return block.astype(jnp.float32)

    def sums(target, piece):
        return BASE_WIRE * partial_sums(target, piece)

    def move(block, pairs):
        return lax.ppermute(block, "tensor", pairs)

    pieces = range(PIECES)
    if line == 4:
        outer = [(0, 1), (3, 2)]
        inner = [(1, 2), (2, 1)]
        both = [(0, 1), (1, 0), (2, 3), (3, 2)]
        low_half = z < 2
        first = jnp.where(low_half, 3, 0)
        second = jnp.where(low_half, 2, 1)
        third = jnp.array([1, 0, 3, 2], jnp.int32)[z]
        sent = []

        def send_out(block, pairs):
            if len(sent) >= 2:
                block = after(block, sent[-2])
            sent.append(move(block, pairs))
            return sent[-1]

        one = [sums(first, p) for p in pieces]
        a1 = [send_out(wire(one[p]), outer) for p in pieces]
        b1 = [move(wire(sums(first, p) + unwire(a1[p])), inner) for p in pieces]
        a2 = [send_out(wire(sums(second, p)), outer) for p in pieces]
        b2 = [move(wire(sums(second, p) + unwire(a2[p])), inner) for p in pieces]
        a3 = [send_out(wire(sums(third, p) + unwire(b1[p])), both) for p in pieces]
        gates.extend(sent)
        return [(unwire(a3[p]) + unwire(b2[p])) * (1.0 / BASE_WIRE) for p in pieces]

    lines = []
    for slot in range(1, line):
        for p in pieces:
            ahead, behind = (z - slot) % line, (z + slot) % line
            if 2 * slot <= line:
                to_right = to_left = sums(jnp.where(z < slot, ahead, behind), p)
            else:
                to_right, to_left = sums(ahead, p), sums(behind, p)
            if slot > 1:
                right, left = lines[-PIECES]
                to_right, to_left = to_right + unwire(right), to_left + unwire(left)
                if 2 * slot <= line:
                    to_right = to_left = to_right + unwire(left)
            going_right = [(i, i + 1) for i in range(slot)]
            going_left = [(line - 1 - i, line - 2 - i) for i in range(slot)]
            lines.append((move(wire(to_right), going_right), move(wire(to_left), going_left)))
    return [(unwire(right) + unwire(left)) * (1.0 / BASE_WIRE) for right, left in lines[-PIECES:]]


def add_and_round(line, z, part):
    rows, rank = part.shape
    packed = jnp.concatenate([part[: rows // 2], part[rows // 2 :]], axis=1)
    size = rows // 2 // line

    def turned(shift):
        return [(i, (i + shift) % line) for i in range(line)]

    def share(i):
        return lax.dynamic_slice(packed, (i * size, 0), (size, 2 * rank))

    total = share(z)
    for shift in range(1, line):
        total = total + lax.ppermute(share((z + shift) % line), "tensor", turned(shift))
    low = total.astype(jnp.bfloat16)
    whole = lax.dynamic_update_slice(jnp.zeros(packed.shape, jnp.bfloat16), low, (z * size, 0))
    for shift in range(1, line):
        other = lax.ppermute(low, "tensor", turned(shift))
        whole = lax.dynamic_update_slice(whole, other, ((z - shift) % line * size, 0))
    return whole


def on_device(tokens, weight, down_stack, up_stack, fetch_list, choose):
    line = lax.axis_size("tensor")
    owners = lax.axis_size("dp")
    groups = lax.axis_size("groups")
    chips = owners // CORES
    z = lax.axis_index("tensor")
    me = lax.axis_index("dp")
    group = lax.axis_index("groups")
    x, core = me // CORES, me % CORES
    own, rank, width = down_stack.shape
    rows = tokens.shape[0]
    per_owner = fetch_list.shape[2]
    sibling = [(i, i ^ 1) for i in range(owners)]
    tiles = rows // PIECES

    def to_sibling(block):
        return lax.ppermute(block, "dp", sibling)

    def partial_sums(target, piece):
        block = lax.dynamic_slice(weight, (0, target * width), (weight.shape[0], width))
        return jnp.dot(tokens[piece * tiles : (piece + 1) * tiles], block, preferred_element_type=jnp.float32)

    gates = []
    arrived = along_line(line, z, partial_sums, gates)

    wanted = (jnp.arange(owners, dtype=jnp.int32)[:, None] * own + fetch_list[0]).reshape(-1)
    picked = choose[:, None] == jnp.arange(owners * per_owner, dtype=jnp.int32)[None, :]
    g = jnp.sum(jnp.where(picked, wanted[None, :], 0), axis=1)

    g_both = jnp.concatenate([g, to_sibling(g)])[:, None]
    tokens_both = jnp.concatenate([tokens, to_sibling(tokens)], axis=0)

    share = own // groups
    size = share // BANK_PIECES

    def slots(owner, first, count):
        return owner * own + first + jnp.arange(count, dtype=jnp.int32)

    found = [[], []]
    crossed, turned = [], []
    for kind, stack in enumerate((down_stack, up_stack)):
        for shift in range(1, chips):
            owner = (x - shift) % chips * CORES + core
            for piece in range(BANK_PIECES):
                first = group * share + piece * size
                block = lax.dynamic_slice(stack, (first, 0, 0), (size, rank, width))
                if crossed:
                    block = after(block, crossed[-1])
                block = lax.ppermute(block, "dp", [(i, (i + shift * CORES) % owners) for i in range(owners)])
                crossed.append(block)
                found[kind].append((block, slots(owner, first, size)))
                for turn in range(1, groups):
                    other = after(block, turned[-1]) if turned else block
                    other = lax.ppermute(other, "groups", [(i, (i + turn) % groups) for i in range(groups)])
                    turned.append(other)
                    first_there = (group - turn) % groups * share + piece * size
                    found[kind].append((other, slots(owner, first_there, size)))

    def shrink(pairs):
        ids = jnp.concatenate([ids for _, ids in pairs])
        kernel = functools.partial(shrink_kernel, rank)
        return over_rows(kernel, 2 * rank, (rank, width), g_both, ids, [tokens_both], [block for block, _ in pairs])

    mine = slots(me, 0, own)
    halves = shrink([(down_stack, mine)]) + shrink(found[0])
    part = halves[:, :rank] + halves[:, rank:]
    part = part[:rows] + to_sibling(part[rows:])
    low = add_and_round(line, z, part)
    low_both = jnp.concatenate([low, to_sibling(low)], axis=1)
    order = [low_both[:, i * rank : (i + 1) * rank] for i in range(4)]
    low_both = jnp.concatenate(order, axis=0)
    low_both = jnp.concatenate([low_both, low_both], axis=1)

    def expand(base, pairs):
        ids = jnp.concatenate([ids for _, ids in pairs])
        kernel = functools.partial(expand_kernel, rank, base is not None)
        rows_in = [low_both] if base is None else [low_both, base]
        return over_rows(kernel, width, (rank, width), g_both, ids, rows_in, [block for block, _ in pairs])

    early, late = found[1][:-1], found[1][-1:]
    adapted = expand(None, [(up_stack, mine)] + early)
    adapted = expand(adapted, late)
    for_sibling = (LOW_WIRE * adapted[rows:]).astype(jnp.float16)
    from_sibling = to_sibling(for_sibling).astype(jnp.float32) * (1.0 / LOW_WIRE)
    outs = []
    for p in range(PIECES):
        here = slice(p * tiles, (p + 1) * tiles)
        outs.append(partial_sums(z, p) + adapted[here] + from_sibling[here] + arrived[p])
    return jnp.concatenate(outs, axis=0).astype(jnp.bfloat16)


def solution(mesh):
    return jax.shard_map(
        on_device,
        mesh=mesh,
        in_specs=(
            P(("groups", "dp"), "tensor"),
            P("tensor", None),
            P("dp", None, "tensor"),
            P("dp", None, "tensor"),
            P(("groups", "dp"), None, None),
            P(("groups", "dp")),
        ),
        out_specs=P(("groups", "dp"), "tensor"),
        check_vma=False,
    )
```

time: 345 us -> 273 us (0.79); the launches traced: 340 us -> 272 us
  waiting for transfers between devices: 212 us -> 104 us
  Pallas kernels: 0 us -> 36.3 us
  blocking collectives: 30 us -> 0 us
  starting transfers between devices: 14.4 us -> 37.7 us
  matrix products: 45.1 us -> 60.7 us
  other arithmetic: 2.82 us -> 16.5 us
  between operations: 13.4 us -> 1.19 us
  local copies, waits for them, and re-layouts: 21.9 us -> 15.4 us
    all_to_all x2 -> x0, waiting for transfers between devices: 141 us -> none  [the longest x1 84.3 us: on_device(): lax.all_to_all(down_out, 'dp', split_axis=0, concat_axis=0, tiled=True)]
    ppermute x0 -> x29, waiting for transfers between devices: none -> 104 us  [the longest x10 33.9 us: move(): return lax.ppermute(block, 'tensor', pairs)]
    reduce_scatter x1 -> x0, waiting for transfers between devices: 70.7 us -> none  [on_device(): lax.psum_scatter(lax.dot_general(weight, tokens, (((0,), (1,)), ((), ()))...]
    ppermute x0 -> x29, starting transfers between devices: none -> 37.7 us  [the longest x10 19.4 us: move(): return lax.ppermute(block, 'tensor', pairs)]
    pallas_call x0 -> x4, Pallas kernels: none -> 36.3 us  [over_rows(): pl.pallas_call(kernel, out_shape=jax.ShapeDtypeStruct((rows, out_width),...]
    psum x1 -> x0, blocking collectives: 25.2 us -> none  [on_device(): low_rank_shrink = lax.psum(own_shrink, 'tensor').astype(jnp.bfloat16)]
    dot_general x3 -> x8, matrix products: 45.1 us -> 60.7 us  [partial_sums(): jnp.dot(tokens[piece * tiles:(piece + 1) * tiles], block, preferred_eleme...]
    gather x2 -> x0, local copies, waits for them, and re-layouts: 15.2 us -> none  [the longest x1 7.89 us: on_device(): down_weight_stack[flat_ids]]
  transfers between devices with their start and end apart: 3 -> 29, of which waited for: 3 -> 11; matrix products, arithmetic and copies ran while one was open for 8% -> 29% of each run, Pallas kernels for 0% -> 13%
where the time goes in v1:
time: 273 us; the launch traced here: 272 us
  waiting for transfers between devices  104 us (38%)
  matrix products  60.7 us (22%)
  starting transfers between devices  37.7 us (14%)
  Pallas kernels  36.3 us (13%)
  other arithmetic  16.5 us (6%)
  local copies, waits for them, and re-layouts  15.4 us (6%)
    dot_general x8, matrix products, partial_sums(): jnp.dot(tokens[piece * tiles:(piece + 1) * tiles], block, preferred_eleme...  60.7 us
    pallas_call x4, Pallas kernels, over_rows(): pl.pallas_call(kernel, out_shape=jax.ShapeDtypeStruct((rows, out_width),...  36.3 us
    ppermute x10, waiting for transfers between devices, move(): return lax.ppermute(block, 'tensor', pairs)  33.9 us
    ppermute x3, waiting for transfers between devices, add_and_round(): other = lax.ppermute(low, 'tensor', turned(shift))  26.1 us
    ppermute x10, starting transfers between devices, move(): return lax.ppermute(block, 'tensor', pairs)  19.4 us
    ppermute x3, waiting for transfers between devices, add_and_round(): lax.ppermute(share((z + shift) % line), 'tensor', turned(shift))  19 us
    ppermute x4, waiting for transfers between devices, on_device(): lax.ppermute(other, 'groups', [(i, (i + turn) % groups) for i in range(gr...  18.1 us
    unnamed x37, local copies, waits for them, and re-layouts  7.62 us
  transfers between devices with their start and end apart: 29, of which 11 were waited for; matrix products, arithmetic and copies ran while one was open for 29% of the time, Pallas kernels for 13%

profile of v1, /device:TPU:10, one launch (start us, length us, event | category | flops | bytes accessed | tf_op | source)
XLA Modules:
  0.0 272.1 jit_solution(9507711146348816019)
XLA Ops:
  0.0 1.7 constant_dynamic-slice_fusion.2
  1.7 0.6 collective-permute-start.2
  2.7 0.5 collective-permute-start.1
  3.2 7.8 %fusion.92 = (f16[256,2048]{1,0:T(8,128)(2,1)}, f32[256,2048]{1,0:T(8,128)}) fusion(bf16[2048,8192]{1,0:T(8,128)(2,1)} %param.8, s32[]{:T(128)S(6)} %select_n.139, bf16[512,2048]{1,0:T(8,128)(2,1)} %param.7), kind=kOutput, calls=%fused_computation.108 | convolution fusion | flops 2148532224 | bytes 12582916 | tf_op jit(solution)/shard_map/dot_general | solution.py:189
  11.0 1.5 collective-permute-start.19
  12.5 3.2 %constant_dynamic-update-slice_fusion.1 = bf16[1024,2048]{1,0:T(8,128)(2,1)} fusion(bf16[512,2048]{1,0:T(8,128)(2,1)} %param.7), kind=kLoop, calls=%fused_computation.78 | loop fusion | bytes 4194304
  15.8 0.6 dynamic_slice.56
  17.0 7.4 %fusion.26 = f32[256,2048]{1,0:T(8,128)} fusion(bf16[2048,8192]{1,0:T(8,128)(2,1)} %param.8, s32[]{:T(128)S(6)} %select_n.137, bf16[512,2048]{1,0:T(8,128)(2,1)} %param.7), kind=kOutput, calls=%fused_computation.22 | convolution fusion | flops 2148007936 | bytes 11534340 | tf_op jit(solution)/shard_map/dot_general | solution.py:189
  24.4 7.4 %fusion.20 = f32[256,2048]{1,0:T(8,128)} fusion(bf16[2048,8192]{1,0:T(8,128)(2,1)} %param.8, s32[]{:T(128)S(6)} %select_n.137, bf16[512,2048]{1,0:T(8,128)(2,1)} %param.7), kind=kOutput, calls=%fused_computation.20 | convolution fusion | flops 2148007936 | bytes 11534340 | tf_op jit(solution)/shard_map/dot_general | solution.py:189
  31.8 7.7 %fusion.94 = (f16[256,2048]{1,0:T(8,128)(2,1)}, f32[256,2048]{1,0:T(8,128)}) fusion(bf16[2048,8192]{1,0:T(8,128)(2,1)} %param.8, s32[]{:T(128)S(6)} %select_n.139, bf16[512,2048]{1,0:T(8,128)(2,1)} %param.7), kind=kOutput, calls=%fused_computation.110 | convolution fusion | flops 2148532224 | bytes 12582916 | tf_op jit(solution)/shard_map/dot_general | solution.py:189
  39.6 7.7 %fusion.91 = (f16[256,2048]{1,0:T(8,128)(2,1)}, f32[256,2048]{1,0:T(8,128)}) fusion(bf16[2048,8192]{1,0:T(8,128)(2,1)} %param.8, s32[]{:T(128)S(6)} %select_n.141, bf16[512,2048]{1,0:T(8,128)(2,1)} %param.7), kind=kOutput, calls=%fused_computation.107 | convolution fusion | flops 2148532224 | bytes 12582916 | tf_op jit(solution)/shard_map/dot_general | solution.py:189
  47.4 1.5 collective-permute-start.4
  48.8 1.5 collective-permute-start.3
  50.4 7.7 %fusion.93 = (f16[256,2048]{1,0:T(8,128)(2,1)}, f32[256,2048]{1,0:T(8,128)}) fusion(bf16[2048,8192]{1,0:T(8,128)(2,1)} %param.8, s32[]{:T(128)S(6)} %select_n.141, bf16[512,2048]{1,0:T(8,128)(2,1)} %param.7), kind=kOutput, calls=%fused_computation.109 | convolution fusion | flops 2148532224 | bytes 12582916 | tf_op jit(solution)/shard_map/dot_general | solution.py:189
  58.2 7.5 %fusion.53 = f32[256,2048]{1,0:T(8,128)} fusion(bf16[2048,8192]{1,0:T(8,128)(2,1)} %param.8, s32[]{:T(128)S(6)} %select_n.115, bf16[512,2048]{1,0:T(8,128)(2,1)} %param.7), kind=kOutput, calls=%fused_computation.31 | convolution fusion | flops 2147483648 | bytes 11534340 | tf_op jit(solution)/shard_map/dot_general | solution.py:189
  65.7 6.8 %collective-permute-done.4 = bf16[4,64,2048]{2,1,0:T(8,128)(2,1)S(1)} collective-permute-done((bf16[4,64,2048]{2,1,0:T(8,128)(2,1)S(1)}, bf16[4,64,2048]{2,1,0:T(8,128)(2,1)S(1)}, u32[]{:S(2)}, u32[]{:S(2)}) %collective-permute-start.4) | collective-permute-done | bytes 1048608 | tf_op jit(solution)/shard_map/ppermute | solution.py:217
  72.5 1.5 collective-permute-start.24
  74.0 1.6 collective-permute-start.5
  75.6 1.6 constant_dynamic-slice_fusion
  77.2 0.2 copy.27.g_ref
  77.4 1.6 collective-permute-start.14
  79.0 3.2 %constant_dynamic-update-slice_fusion.tokens_ref = bf16[1024,2048]{1,0:T(8,128)(2,1)} fusion(bf16[1024,2048]{1,0:T(8,128)(2,1)} %constant_dynamic-update-slice_fusion.1, bf16[512,2048]{1,0:T(8,128)(2,1)} %collective-permute-done.1), kind=kLoop, calls=%fused_computation.77 | loop fusion | bytes 4194304 | tf_op jit(solution)/shard_map/concatenate | solution.py:199
  82.2 2.2 copy-done
  84.4 7.9 %shard_map.73 = f32[1024,128]{1,0:T(8,128)S(1)} custom-call(s32[16]{0:T(128)S(1)} %iota_add_fusion.3.ids_ref, s32[1024,1]{1,0:T(8,128)S(1)} %copy.27.g_ref, bf16[1024,2048]{1,0:T(8,128)(2,1)S(1)} %copy-done, bf16[1024,2048]{1,0:T(8,128)(2,1)} %bitcast.36), custom_call_target="tpu_custom_call" | custom-call | flops 4294967296 | bytes 8912896 | tf_op jit(solution)/shard_map/pallas_call | solution.py:69
  92.3 6.3 %collective-permute-done.5 = bf16[4,64,2048]{2,1,0:T(8,128)(2,1)} collective-permute-done((bf16[4,64,2048]{2,1,0:T(8,128)(2,1)S(1)}, bf16[4,64,2048]{2,1,0:T(8,128)(2,1)}, u32[]{:S(2)}, u32[]{:S(2)}) %collective-permute-start.5) | collective-permute-done | bytes 1048608 | tf_op jit(solution)/shard_map/ppermute | solution.py:222
  98.6 7.6 %shard_map.74 = f32[1024,128]{1,0:T(8,128)S(1)} custom-call(s32[16]{0:T(128)S(1)} %pad_add_fusion.1.ids_ref, s32[1024,1]{1,0:T(8,128)S(1)} %copy.27.g_ref, bf16[1024,2048]{1,0:T(8,128)(2,1)} %constant_dynamic-update-slice_fusion.tokens_ref, bf16[256,2048]{1,0:T(8,128)(2,1)S(1)} %bitcast.29, bf16[256,2048]{1,0:T(8,128)(2,1)} %bitcast.4.refs_1_, ...), custom_call_target="tpu_custom_call" | custom-call | flops 4294967296 | bytes 8912896 | tf_op jit(solution)/shard_map/pallas_call | solution.py:69
  106.3 0.2 slice_add_fusion.4
  106.6 1.2 copy-done.3
  107.8 1.8 add_convert_fusion.5
  109.6 3.5 %collective-permute-start.20 = (f16[256,2048]{1,0:T(8,128)(2,1)S(1)}, f16[256,2048]{1,0:T(8,128)(2,1)S(1)}, u32[]{:S(2)}, u32[]{:S(2)}) collective-permute-start(f16[256,2048]{1,0:T(8,128)(2,1)S(1)} %add_convert_fusion.5), channel_id=1, source_target_pairs={{1,2},{2,1},{5,6},{6,5},{9,10},{10,9},{13,14},{14,13},{17,18},{18,... | collective-permute-start | bytes 3145736 | tf_op jit(solution)/shard_map/ppermute | solution.py:100
  113.1 1.3 collective-permute-start.21
  114.6 0.5 collective-permute-start.7
  115.1 4.6 %collective-permute-start.8 = (f32[64,128]{1,0:T(8,128)S(1)}, f32[64,128]{1,0:T(8,128)S(1)}, u32[]{:S(2)}, u32[]{:S(2)}) collective-permute-start(f32[64,128]{1,0:T(8,128)S(1)} %get-tuple-element.34), channel_id=1, source_target_pairs={{0,2},{1,3},{2,0},{3,1},{4,6},{5,7},{6,4},{7,5},{8,10},{9,11},{10,... | collective-permute-start | bytes 98312 | tf_op jit(solution)/shard_map/ppermute | solution.py:160
  119.7 1.8 add_convert_fusion.2
  121.5 19.0 %collective-permute-done.7 = f32[64,128]{1,0:T(8,128)S(1)} collective-permute-done((f32[64,128]{1,0:T(8,128)S(1)}, f32[64,128]{1,0:T(8,128)S(1)}, u32[]{:S(2)}, u32[]{:S(2)}) %collective-permute-start.7) | collective-permute-done | bytes 32800 | tf_op jit(solution)/shard_map/ppermute | solution.py:160
  140.5 1.9 collective-permute-start.25
  142.4 1.6 collective-permute-start.15
  144.0 1.5 collective-permute-start.16
  145.6 2.1 collective-permute-start.10
  147.7 1.3 add_convert_fusion.4
  149.0 1.3 collective-permute-start.26
  150.3 12.8 %collective-permute-done.10 = bf16[64,128]{1,0:T(8,128)(2,1)S(1)} collective-permute-done((bf16[64,128]{1,0:T(8,128)(2,1)S(1)}, bf16[64,128]{1,0:T(8,128)(2,1)S(1)}, u32[]{:S(2)}, u32[]{:S(2)}) %collective-permute-start.10) | collective-permute-done | bytes 16416 | tf_op jit(solution)/shard_map/ppermute | solution.py:164
  163.1 9.5 %collective-permute-done.11 = bf16[64,128]{1,0:T(8,128)(2,1)S(1)} collective-permute-done((bf16[64,128]{1,0:T(8,128)(2,1)S(1)}, bf16[64,128]{1,0:T(8,128)(2,1)S(1)}, u32[]{:S(2)}, u32[]{:S(2)}) %collective-permute-start.11) | collective-permute-done | bytes 16416 | tf_op jit(solution)/shard_map/ppermute | solution.py:164
  172.7 3.7 %collective-permute-done.12 = bf16[64,128]{1,0:T(8,128)(2,1)S(1)} collective-permute-done((bf16[64,128]{1,0:T(8,128)(2,1)S(1)}, bf16[64,128]{1,0:T(8,128)(2,1)S(1)}, u32[]{:S(2)}, u32[]{:S(2)}) %collective-permute-start.12) | collective-permute-done | bytes 16416 | tf_op jit(solution)/shard_map/ppermute | solution.py:164
  176.6 0.6 collective-permute-start.17
  177.2 0.5 collective-permute-done.13
  177.9 12.6 %shard_map.75.refs_0_ = f32[1024,2048]{1,0:T(8,128)} custom-call(s32[28]{0:T(128)S(1)} %pad_add_fusion.2.ids_ref, s32[1024,1]{1,0:T(8,128)S(1)} %copy.27.g_ref, bf16[1024,128]{1,0:T(8,128)(2,1)S(1)} %maximum_maximum_fusion.low_ref, bf16[1024,2048]{1,0:T(8,128)(2,1)} %bitcast.37, bf16[256,2048]{1,0:T(8,128)(2,1)S(1)} %bitcast.31, ...), custom_call_target="tpu_custom_call" | custom-call | flops 7516192768 | bytes 15990784 | tf_op jit(solution)/shard_map/pallas_call | solution.py:69
  190.5 11.8 %collective-permute-done.17 = bf16[4,64,2048]{2,1,0:T(8,128)(2,1)S(1)} collective-permute-done((bf16[4,64,2048]{2,1,0:T(8,128)(2,1)S(1)}, bf16[4,64,2048]{2,1,0:T(8,128)(2,1)S(1)}, u32[]{:S(2)}, u32[]{:S(2)}) %collective-permute-start.17) | collective-permute-done | bytes 1048608 | tf_op jit(solution)/shard_map/ppermute | solution.py:222
  202.2 8.3 %shard_map.76 = f32[1024,2048]{1,0:T(8,128)} custom-call(s32[4]{0:T(128)S(1)} %iota_add_fusion.4.ids_ref, s32[1024,1]{1,0:T(8,128)S(1)} %copy.27.g_ref, bf16[1024,128]{1,0:T(8,128)(2,1)S(1)} %maximum_maximum_fusion.low_ref, f32[1024,2048]{1,0:T(8,128)} %shard_map.75.refs_0_, bf16[256,2048]{1,0:T(8,128)(2,1)S(1)} %bitcast.28), custom_call_target="tpu_custom_call" | custom-call | flops 1073741824 | bytes 18087936 | tf_op jit(solution)/shard_map/pallas_call | solution.py:69
  210.5 2.9 %fusion.16 = f16[512,2048]{1,0:T(8,128)(2,1)S(1)} fusion(f32[1024,2048]{1,0:T(8,128)} %shard_map.76), kind=kLoop, calls=%fused_computation.17 | loop fusion | flops 2097152 | bytes 6291456 | tf_op jit(solution)/shard_map/convert_element_type | solution.py:251
  213.5 0.3 add_convert_fusion.1
  213.8 1.7 collective-permute-start.27
  215.6 0.3 add_convert_fusion.3
  215.9 3.6 %collective-permute-start.23 = (f16[256,2048]{1,0:T(8,128)(2,1)S(1)}, f16[256,2048]{1,0:T(8,128)(2,1)S(1)}, u32[]{:S(2)}, u32[]{:S(2)}) collective-permute-start(f16[256,2048]{1,0:T(8,128)(2,1)S(1)} %add_convert_fusion.3), channel_id=1, source_target_pairs={{1,2},{2,1},{5,6},{6,5},{9,10},{10,9},{13,14},{14,13},{17,18},{18,... | collective-permute-start | bytes 3145736 | tf_op jit(solution)/shard_map/ppermute | solution.py:100
  219.5 0.4 add_convert_fusion
  219.9 3.0 %collective-permute-start.28 = (f16[256,2048]{1,0:T(8,128)(2,1)S(1)}, f16[256,2048]{1,0:T(8,128)(2,1)}, u32[]{:S(2)}, u32[]{:S(2)}) collective-permute-start(f16[256,2048]{1,0:T(8,128)(2,1)S(1)} %add_convert_fusion), channel_id=1, source_target_pairs={{1,2},{2,1},{5,6},{6,5},{9,10},{10,9},{13,14},{14,13},{17,18},{18,... | collective-permute-start | bytes 3145736 | tf_op jit(solution)/shard_map/ppermute | solution.py:100
  222.9 7.4 %fusion.56 = f32[256,2048]{1,0:T(8,128)} fusion(bf16[2048,8192]{1,0:T(8,128)(2,1)} %param.8, s32[]{:T(128)S(6)} %select_n.115, bf16[512,2048]{1,0:T(8,128)(2,1)} %param.7), kind=kOutput, calls=%fused_computation.32 | convolution fusion | flops 2147483648 | bytes 11534340 | tf_op jit(solution)/shard_map/dot_general | solution.py:189
  230.3 0.5 convert_multiply_fusion
  230.9 8.6 %collective-permute-done.27 = f16[256,2048]{1,0:T(8,128)(2,1)S(1)} collective-permute-done((f16[256,2048]{1,0:T(8,128)(2,1)S(1)}, f16[256,2048]{1,0:T(8,128)(2,1)S(1)}, u32[]{:S(2)}, u32[]{:S(2)}) %collective-permute-start.27) | collective-permute-done | bytes 1048608 | tf_op jit(solution)/shard_map/ppermute | solution.py:100
  239.4 4.5 %collective-permute-done.23 = f16[256,2048]{1,0:T(8,128)(2,1)S(1)} collective-permute-done((f16[256,2048]{1,0:T(8,128)(2,1)S(1)}, f16[256,2048]{1,0:T(8,128)(2,1)S(1)}, u32[]{:S(2)}, u32[]{:S(2)}) %collective-permute-start.23) | collective-permute-done | bytes 1048608 | tf_op jit(solution)/shard_map/ppermute | solution.py:100
  243.9 1.0 copy-done.9
  244.9 20.9 %collective-permute-done.28 = f16[256,2048]{1,0:T(8,128)(2,1)} collective-permute-done((f16[256,2048]{1,0:T(8,128)(2,1)S(1)}, f16[256,2048]{1,0:T(8,128)(2,1)}, u32[]{:S(2)}, u32[]{:S(2)}) %collective-permute-start.28) | collective-permute-done | bytes 1048608 | tf_op jit(solution)/shard_map/ppermute | solution.py:100
  265.8 4.8 %fusion.62 = (bf16[256,2048]{1,0:T(8,128)(2,1)S(1)}, bf16[256,2048]{1,0:T(8,128)(2,1)S(1)}) fusion(f32[512,2048]{1,0:T(8,128)S(1)} %convert_multiply_fusion, f32[256,2048]{1,0:T(8,128)} %fusion.56, f32[1024,2048]{1,0:T(8,128)S(1)} %bitcast.35, f16[256,2048]{1,0:T(8,128)(2,1)} %copy-done.9, f16[256,2048]{1,0:T(8,128)(2,1)} %copy-done.8, ...), kind=kLoop, calls=%fused_computation.39 | loop fusion | flops 8388608 | bytes 18874368 | tf_op jit(solution)/shard_map/convert
  270.5 1.5 pad_maximum_fusion
  (86 shorter events, 1.6 us)
Async XLA Ops:
  0.0 2.5 copy-start.11
  0.0 2.6 copy-start.12
  1.7 45.6 %collective-permute-start.2 = (bf16[4,64,2048]{2,1,0:T(8,128)(2,1)S(1)}, bf16[4,64,2048]{2,1,0:T(8,128)(2,1)S(1)}, u32[]{:S(2)}, u32[]{:S(2)}) collective-permute-start(bf16[4,64,2048]{2,1,0:T(8,128)(2,1)S(1)} %get-tuple-element.32), channel_id=1, source_target_pairs={{0,8},{4,12},{8,0},{12,4},{1,9},{5,13},{9,1},{13,5},{2,10},{6,14},... | collective-permute-start | bytes 3145736 | tf_op jit(solution)/shard_map/ppermute | solution.py:217
  2.7 74.5 %collective-permute-start = (s32[512]{0:T(512)S(1)}, s32[512]{0:T(512)S(1)}, u32[]{:S(2)}, u32[]{:S(2)}) collective-permute-start(s32[512]{0:T(512)S(1)} %select_reduce_fusion), channel_id=1, source_target_pairs={{0,4},{4,0},{8,12},{12,8},{1,5},{5,1},{9,13},{13,9},{2,6},{6,2},{1... | collective-permute-start | bytes 6152 | tf_op jit(solution)/shard_map/ppermute | solution.py:185
  2.7 76.2 %collective-permute-start.1 = (bf16[512,2048]{1,0:T(8,128)(2,1)}, bf16[512,2048]{1,0:T(8,128)(2,1)}, u32[]{:S(2)}, u32[]{:S(2)}) collective-permute-start(bf16[512,2048]{1,0:T(8,128)(2,1)} %param.7), channel_id=1, source_target_pairs={{0,4},{4,0},{8,12},{12,8},{1,5},{5,1},{9,13},{13,9},{2,6},{6,2},{1... | collective-permute-start | bytes 6291464 | tf_op jit(solution)/shard_map/ppermute | solution.py:185
  11.0 95.6 %collective-permute-start.19 = (f16[256,2048]{1,0:T(8,128)(2,1)}, f16[256,2048]{1,0:T(8,128)(2,1)}, u32[]{:S(2)}, u32[]{:S(2)}) collective-permute-start(f16[256,2048]{1,0:T(8,128)(2,1)} %get-tuple-element.44), channel_id=1, source_target_pairs={{0,1},{3,2},{4,5},{7,6},{8,9},{11,10},{12,13},{15,14},{16,17},{19,... | collective-permute-start | bytes 3145736 | tf_op jit(solution)/shard_map/ppermute | solution.py:100
  12.5 3.2 %copy-start.15 = (s32[4]{0:T(128)S(1)}, s32[4]{0:T(128)}, u32[]{:S(2)}) copy-start(s32[4]{0:T(128)} %constant.122.clone) | copy-start | bytes 52
  47.4 25.1 %collective-permute-start.4 = (bf16[4,64,2048]{2,1,0:T(8,128)(2,1)S(1)}, bf16[4,64,2048]{2,1,0:T(8,128)(2,1)S(1)}, u32[]{:S(2)}, u32[]{:S(2)}) collective-permute-start(bf16[4,64,2048]{2,1,0:T(8,128)(2,1)S(1)} %get-tuple-element.15), channel_id=1, source_target_pairs={{0,8},{4,12},{8,0},{12,4},{1,9},{5,13},{9,1},{13,5},{2,10},{6,14},... | collective-permute-start | bytes 3145736 | tf_op jit(solution)/shard_map/ppermute | solution.py:217
  48.8 25.2 %collective-permute-start.3 = (bf16[4,64,2048]{2,1,0:T(8,128)(2,1)S(1)}, bf16[4,64,2048]{2,1,0:T(8,128)(2,1)}, u32[]{:S(2)}, u32[]{:S(2)}) collective-permute-start(bf16[4,64,2048]{2,1,0:T(8,128)(2,1)S(1)} %collective-permute-done.2), channel_id=1, source_target_pairs={{0,16},{16,0},{1,17},{17,1},{2,18},{18,2},{3,19},{19,3},{4,20},{20... | collective-permute-start | bytes 3145736 | tf_op jit(solution)/shard_map/ppermute | solution.py:222
  58.2 17.4 %copy-start.10 = (bf16[16,64,2048]{2,1,0:T(8,128)(2,1)S(1)}, bf16[16,64,2048]{2,1,0:T(8,128)(2,1)}, u32[]{:S(2)}) copy-start(bf16[16,64,2048]{2,1,0:T(8,128)(2,1)} %param.10) | copy-start | bytes 12582916
  72.5 42.6 %collective-permute-start.24 = (f16[256,2048]{1,0:T(8,128)(2,1)}, f16[256,2048]{1,0:T(8,128)(2,1)}, u32[]{:S(2)}, u32[]{:S(2)}) collective-permute-start(f16[256,2048]{1,0:T(8,128)(2,1)} %get-tuple-element.48), channel_id=1, source_target_pairs={{0,1},{3,2},{4,5},{7,6},{8,9},{11,10},{12,13},{15,14},{16,17},{19,... | collective-permute-start | bytes 3145736 | tf_op jit(solution)/shard_map/ppermute | solution.py:100
  74.0 24.6 %collective-permute-start.5 = (bf16[4,64,2048]{2,1,0:T(8,128)(2,1)S(1)}, bf16[4,64,2048]{2,1,0:T(8,128)(2,1)}, u32[]{:S(2)}, u32[]{:S(2)}) collective-permute-start(bf16[4,64,2048]{2,1,0:T(8,128)(2,1)S(1)} %collective-permute-done.4), channel_id=1, source_target_pairs={{0,16},{16,0},{1,17},{17,1},{2,18},{18,2},{3,19},{19,3},{4,20},{20... | collective-permute-start | bytes 3145736 | tf_op jit(solution)/shard_map/ppermute | solution.py:222
  77.4 42.3 %collective-permute-start.14 = (bf16[4,64,2048]{2,1,0:T(8,128)(2,1)}, bf16[4,64,2048]{2,1,0:T(8,128)(2,1)S(1)}, u32[]{:S(2)}, u32[]{:S(2)}) collective-permute-start(bf16[4,64,2048]{2,1,0:T(8,128)(2,1)} %get-tuple-element.17), channel_id=1, source_target_pairs={{0,8},{4,12},{8,0},{12,4},{1,9},{5,13},{9,1},{13,5},{2,10},{6,14},... | collective-permute-start | bytes 3145736 | tf_op jit(solution)/shard_map/ppermute | solution.py:217
  82.2 2.2 copy-start
  106.2 1.6 copy-start.3
  106.5 7.9 %collective-permute-start.6 = (f32[512,64]{1,0:T(8,128)S(1)}, f32[512,64]{1,0:T(8,128)S(1)}, u32[]{:S(2)}, u32[]{:S(2)}) collective-permute-start(f32[512,64]{1,0:T(8,128)S(1)} %slice.81), channel_id=1, source_target_pairs={{0,4},{4,0},{8,12},{12,8},{1,5},{5,1},{9,13},{13,9},{2,6},{6,2},{1... | collective-permute-start | bytes 393224 | tf_op jit(solution)/shard_map/ppermute | solution.py:185
  107.8 5.3 %copy-start.13 = (f16[256,2048]{1,0:T(8,128)(2,1)S(1)}, f16[256,2048]{1,0:T(8,128)(2,1)}, u32[]{:S(2)}) copy-start(f16[256,2048]{1,0:T(8,128)(2,1)} %get-tuple-element.21) | copy-start | bytes 3145732
  107.8 11.9 %copy-start.6 = (f32[256,2048]{1,0:T(8,128)S(1)}, f32[256,2048]{1,0:T(8,128)}, u32[]{:S(2)}) copy-start(f32[256,2048]{1,0:T(8,128)} %get-tuple-element.49) | copy-start | bytes 6291460
  109.6 36.0 %collective-permute-start.20 = (f16[256,2048]{1,0:T(8,128)(2,1)S(1)}, f16[256,2048]{1,0:T(8,128)(2,1)S(1)}, u32[]{:S(2)}, u32[]{:S(2)}) collective-permute-start(f16[256,2048]{1,0:T(8,128)(2,1)S(1)} %add_convert_fusion.5), channel_id=1, source_target_pairs={{1,2},{2,1},{5,6},{6,5},{9,10},{10,9},{13,14},{14,13},{17,18},{18,... | collective-permute-start | bytes 3145736 | tf_op jit(solution)/shard_map/ppermute | solution.py:100
  113.1 35.9 %collective-permute-start.21 = (f16[256,2048]{1,0:T(8,128)(2,1)S(1)}, f16[256,2048]{1,0:T(8,128)(2,1)S(1)}, u32[]{:S(2)}, u32[]{:S(2)}) collective-permute-start(f16[256,2048]{1,0:T(8,128)(2,1)S(1)} %copy-done.13), channel_id=1, source_target_pairs={{0,1},{3,2},{4,5},{7,6},{8,9},{11,10},{12,13},{15,14},{16,17},{19,... | collective-permute-start | bytes 3145736 | tf_op jit(solution)/shard_map/ppermute | solution.py:100
  114.6 25.9 %collective-permute-start.7 = (f32[64,128]{1,0:T(8,128)S(1)}, f32[64,128]{1,0:T(8,128)S(1)}, u32[]{:S(2)}, u32[]{:S(2)}) collective-permute-start(f32[64,128]{1,0:T(8,128)S(1)} %get-tuple-element.33), channel_id=1, source_target_pairs={{0,1},{1,2},{2,3},{3,0},{4,5},{5,6},{6,7},{7,4},{8,9},{9,10},{10,1... | collective-permute-start | bytes 98312 | tf_op jit(solution)/shard_map/ppermute | solution.py:160
  115.1 27.3 %collective-permute-start.8 = (f32[64,128]{1,0:T(8,128)S(1)}, f32[64,128]{1,0:T(8,128)S(1)}, u32[]{:S(2)}, u32[]{:S(2)}) collective-permute-start(f32[64,128]{1,0:T(8,128)S(1)} %get-tuple-element.34), channel_id=1, source_target_pairs={{0,2},{1,3},{2,0},{3,1},{4,6},{5,7},{6,4},{7,5},{8,10},{9,11},{10,... | collective-permute-start | bytes 98312 | tf_op jit(solution)/shard_map/ppermute | solution.py:160
  119.7 24.3 %collective-permute-start.9 = (f32[64,128]{1,0:T(8,128)S(1)}, f32[64,128]{1,0:T(8,128)S(1)}, u32[]{:S(2)}, u32[]{:S(2)}) collective-permute-start(f32[64,128]{1,0:T(8,128)S(1)} %get-tuple-element.35), channel_id=1, source_target_pairs={{0,3},{1,0},{2,1},{3,2},{4,7},{5,4},{6,5},{7,6},{8,11},{9,8},{10,9... | collective-permute-start | bytes 98312 | tf_op jit(solution)/shard_map/ppermute | solution.py:160
  119.7 24.3 %copy-start.7 = (bf16[4,64,2048]{2,1,0:T(8,128)(2,1)S(1)}, bf16[4,64,2048]{2,1,0:T(8,128)(2,1)}, u32[]{:S(2)}) copy-start(bf16[4,64,2048]{2,1,0:T(8,128)(2,1)} %get-tuple-element.19) | copy-start | bytes 3145732
  119.7 28.0 %copy-start.4 = (f32[256,2048]{1,0:T(8,128)S(1)}, f32[256,2048]{1,0:T(8,128)}, u32[]{:S(2)}) copy-start(f32[256,2048]{1,0:T(8,128)} %fusion.26) | copy-start | bytes 6291460
  140.5 73.0 %collective-permute-start.25 = (f16[256,2048]{1,0:T(8,128)(2,1)S(1)}, f16[256,2048]{1,0:T(8,128)(2,1)S(1)}, u32[]{:S(2)}, u32[]{:S(2)}) collective-permute-start(f16[256,2048]{1,0:T(8,128)(2,1)S(1)} %add_convert_fusion.2), channel_id=1, source_target_pairs={{1,2},{2,1},{5,6},{6,5},{9,10},{10,9},{13,14},{14,13},{17,18},{18,... | collective-permute-start | bytes 3145736 | tf_op jit(solution)/shard_map/ppermute | solution.py:100
  142.4 34.1 %collective-permute-start.15 = (bf16[4,64,2048]{2,1,0:T(8,128)(2,1)S(1)}, bf16[4,64,2048]{2,1,0:T(8,128)(2,1)S(1)}, u32[]{:S(2)}, u32[]{:S(2)}) collective-permute-start(bf16[4,64,2048]{2,1,0:T(8,128)(2,1)S(1)} %collective-permute-done.14), channel_id=1, source_target_pairs={{0,16},{16,0},{1,17},{17,1},{2,18},{18,2},{3,19},{19,3},{4,20},{20... | collective-permute-start | bytes 3145736 | tf_op jit(solution)/shard_map/ppermute | solution.py:222
  144.0 32.6 %collective-permute-start.16 = (bf16[4,64,2048]{2,1,0:T(8,128)(2,1)S(1)}, bf16[4,64,2048]{2,1,0:T(8,128)(2,1)S(1)}, u32[]{:S(2)}, u32[]{:S(2)}) collective-permute-start(bf16[4,64,2048]{2,1,0:T(8,128)(2,1)S(1)} %copy-done.7), channel_id=1, source_target_pairs={{0,8},{4,12},{8,0},{12,4},{1,9},{5,13},{9,1},{13,5},{2,10},{6,14},... | collective-permute-start | bytes 3145736 | tf_op jit(solution)/shard_map/ppermute | solution.py:217
  145.6 3.4 %copy-start.14 = (f16[256,2048]{1,0:T(8,128)(2,1)S(1)}, f16[256,2048]{1,0:T(8,128)(2,1)}, u32[]{:S(2)}) copy-start(f16[256,2048]{1,0:T(8,128)(2,1)} %get-tuple-element.23) | copy-start | bytes 3145732
  145.6 17.5 %collective-permute-start.10 = (bf16[64,128]{1,0:T(8,128)(2,1)S(1)}, bf16[64,128]{1,0:T(8,128)(2,1)S(1)}, u32[]{:S(2)}, u32[]{:S(2)}) collective-permute-start(bf16[64,128]{1,0:T(8,128)(2,1)S(1)} %get-tuple-element.26), channel_id=1, source_target_pairs={{0,1},{1,2},{2,3},{3,0},{4,5},{5,6},{6,7},{7,4},{8,9},{9,10},{10,1... | collective-permute-start | bytes 49160 | tf_op jit(solution)/shard_map/ppermute | solution.py:164
  149.0 64.8 %collective-permute-start.26 = (f16[256,2048]{1,0:T(8,128)(2,1)S(1)}, f16[256,2048]{1,0:T(8,128)(2,1)S(1)}, u32[]{:S(2)}, u32[]{:S(2)}) collective-permute-start(f16[256,2048]{1,0:T(8,128)(2,1)S(1)} %copy-done.14), channel_id=1, source_target_pairs={{0,1},{3,2},{4,5},{7,6},{8,9},{11,10},{12,13},{15,14},{16,17},{19,... | collective-permute-start | bytes 3145736 | tf_op jit(solution)/shard_map/ppermute | solution.py:100
  163.1 9.5 %collective-permute-start.11 = (bf16[64,128]{1,0:T(8,128)(2,1)S(1)}, bf16[64,128]{1,0:T(8,128)(2,1)S(1)}, u32[]{:S(2)}, u32[]{:S(2)}) collective-permute-start(bf16[64,128]{1,0:T(8,128)(2,1)S(1)} %get-tuple-element.26), channel_id=1, source_target_pairs={{0,2},{1,3},{2,0},{3,1},{4,6},{5,7},{6,4},{7,5},{8,10},{9,11},{10,... | collective-permute-start | bytes 49160 | tf_op jit(solution)/shard_map/ppermute | solution.py:164
  172.7 3.7 %collective-permute-start.12 = (bf16[64,128]{1,0:T(8,128)(2,1)S(1)}, bf16[64,128]{1,0:T(8,128)(2,1)S(1)}, u32[]{:S(2)}, u32[]{:S(2)}) collective-permute-start(bf16[64,128]{1,0:T(8,128)(2,1)S(1)} %get-tuple-element.26), channel_id=1, source_target_pairs={{0,3},{1,0},{2,1},{3,2},{4,7},{5,4},{6,5},{7,6},{8,11},{9,8},{10,9... | collective-permute-start | bytes 49160 | tf_op jit(solution)/shard_map/ppermute | solution.py:164
  176.4 1.3 collective-permute-start.13
  176.5 54.3 %collective-permute-start.22 = (f16[256,2048]{1,0:T(8,128)(2,1)}, f16[256,2048]{1,0:T(8,128)(2,1)S(1)}, u32[]{:S(2)}, u32[]{:S(2)}) collective-permute-start(f16[256,2048]{1,0:T(8,128)(2,1)} %add_convert_fusion.4), channel_id=1, source_target_pairs={{0,1},{1,0},{2,3},{3,2},{4,5},{5,4},{6,7},{7,6},{8,9},{9,8},{10,11... | collective-permute-start | bytes 3145736 | tf_op jit(solution)/shard_map/ppermute | solution.py:100
  176.6 25.6 %collective-permute-start.17 = (bf16[4,64,2048]{2,1,0:T(8,128)(2,1)S(1)}, bf16[4,64,2048]{2,1,0:T(8,128)(2,1)S(1)}, u32[]{:S(2)}, u32[]{:S(2)}) collective-permute-start(bf16[4,64,2048]{2,1,0:T(8,128)(2,1)S(1)} %collective-permute-done.16), channel_id=1, source_target_pairs={{0,16},{16,0},{1,17},{17,1},{2,18},{18,2},{3,19},{19,3},{4,20},{20... | collective-permute-start | bytes 3145736 | tf_op jit(solution)/shard_map/ppermute | solution.py:222
  210.5 3.0 %copy-start.1 = (f32[256,2048]{1,0:T(8,128)S(1)}, f32[256,2048]{1,0:T(8,128)}, u32[]{:S(2)}) copy-start(f32[256,2048]{1,0:T(8,128)} %fusion.20) | copy-start | bytes 6291460
  213.4 2.2 copy-start.2
  213.4 16.9 %collective-permute-start.18 = (f16[512,2048]{1,0:T(8,128)(2,1)S(1)}, f16[512,2048]{1,0:T(8,128)(2,1)S(1)}, u32[]{:S(2)}, u32[]{:S(2)}) collective-permute-start(f16[512,2048]{1,0:T(8,128)(2,1)S(1)} %fusion.16), channel_id=1, source_target_pairs={{0,4},{4,0},{8,12},{12,8},{1,5},{5,1},{9,13},{13,9},{2,6},{6,2},{1... | collective-permute-start | bytes 6291464 | tf_op jit(solution)/shard_map/ppermute | solution.py:185
  213.8 25.6 %collective-permute-start.27 = (f16[256,2048]{1,0:T(8,128)(2,1)S(1)}, f16[256,2048]{1,0:T(8,128)(2,1)S(1)}, u32[]{:S(2)}, u32[]{:S(2)}) collective-permute-start(f16[256,2048]{1,0:T(8,128)(2,1)S(1)} %add_convert_fusion.1), channel_id=1, source_target_pairs={{0,1},{1,0},{2,3},{3,2},{4,5},{5,4},{6,7},{7,6},{8,9},{9,8},{10,11... | collective-permute-start | bytes 3145736 | tf_op jit(solution)/shard_map/ppermute | solution.py:100
  215.6 3.9 %copy-start.5 = (f32[256,2048]{1,0:T(8,128)S(1)}, f32[256,2048]{1,0:T(8,128)}, u32[]{:S(2)}) copy-start(f32[256,2048]{1,0:T(8,128)} %get-tuple-element.47) | copy-start | bytes 6291460
  215.9 28.0 %collective-permute-start.23 = (f16[256,2048]{1,0:T(8,128)(2,1)S(1)}, f16[256,2048]{1,0:T(8,128)(2,1)S(1)}, u32[]{:S(2)}, u32[]{:S(2)}) collective-permute-start(f16[256,2048]{1,0:T(8,128)(2,1)S(1)} %add_convert_fusion.3), channel_id=1, source_target_pairs={{1,2},{2,1},{5,6},{6,5},{9,10},{10,9},{13,14},{14,13},{17,18},{18,... | collective-permute-start | bytes 3145736 | tf_op jit(solution)/shard_map/ppermute | solution.py:100
  219.5 46.3 %slice-start = ((s8[8388608]{0:T(1024)(128)(4,1)}), s8[4194304]{0:T(1024)(128)(4,1)S(1)}, s32[]{:S(2)}) async-start(s8[8388608]{0:T(1024)(128)(4,1)} %bitcast.34), calls=%async_computation | async-start | bytes 8388608
  219.9 45.9 %slice-start.1 = ((s8[8388608]{0:T(1024)(128)(4,1)}), s8[4194304]{0:T(1024)(128)(4,1)S(1)}, s32[]{:S(2)}) async-start(s8[8388608]{0:T(1024)(128)(4,1)} %bitcast.34), calls=%async_computation.1 | async-start | bytes 8388608
  219.9 45.9 %collective-permute-start.28 = (f16[256,2048]{1,0:T(8,128)(2,1)S(1)}, f16[256,2048]{1,0:T(8,128)(2,1)}, u32[]{:S(2)}, u32[]{:S(2)}) collective-permute-start(f16[256,2048]{1,0:T(8,128)(2,1)S(1)} %add_convert_fusion), channel_id=1, source_target_pairs={{1,2},{2,1},{5,6},{6,5},{9,10},{10,9},{13,14},{14,13},{17,18},{18,... | collective-permute-start | bytes 3145736 | tf_op jit(solution)/shard_map/ppermute | solution.py:100
  230.9 13.1 %copy-start.8 = (f16[256,2048]{1,0:T(8,128)(2,1)}, f16[256,2048]{1,0:T(8,128)(2,1)S(1)}, u32[]{:S(2)}) copy-start(f16[256,2048]{1,0:T(8,128)(2,1)S(1)} %collective-permute-done.22) | copy-start | bytes 3145732
  243.9 1.0 copy-start.9

commit v2 on v0

v2 whole, which is shorter than its diff:
```python
import functools

import jax
import jax.numpy as jnp
from jax import lax
from jax.experimental import pallas as pl
from jax.experimental.pallas import tpu as pltpu
from jax.sharding import PartitionSpec as P

adapter_scale = 0.5
CORES = 2
BANK_PIECES = 2
BASE_WIRE = 8.0
VMEM = 48 * 1024 * 1024


def ids_of_pair(ids_ref, first, shape, rank):
    lane = lax.broadcasted_iota(jnp.int32, shape, 1)
    return jnp.where(lane < rank, ids_ref[first], ids_ref[first + 1])


def shrink_kernel(rank, steps, ids_ref, g_ref, mine_ref, other_ref, *refs):
    *blocks, o_ref = refs

    def run(tokens_ref):
        tokens = tokens_ref[...]
        g = g_ref[...]
        total = jnp.zeros(o_ref.shape, jnp.float32)
        seen = 0
        for block in blocks:
            part = lax.dot_general(tokens, block[...], (((1,), (1,)), ((), ())), preferred_element_type=jnp.float32)
            for pair in range(block.shape[0] // (2 * rank)):
                ids = ids_of_pair(ids_ref, seen + 2 * pair, o_ref.shape, rank)
                total += jnp.where(g == ids, part[:, pair * 2 * rank : (pair + 1) * 2 * rank], 0.0)
            seen += block.shape[0] // rank
        o_ref[...] = total

    @pl.when(pl.program_id(0) < steps)
    def _():
        run(mine_ref)

    @pl.when(pl.program_id(0) >= steps)
    def _():
        run(other_ref)


def shrink(mine, other, g, ids, blocks):
    rows, width = mine.shape
    rank = blocks[0].shape[1]
    tile = min(256, rows)
    steps = rows // tile
    flat = [block.reshape(-1, width) for block in blocks]
    deep = sum(block.shape[0] for block in flat)
    return pl.pallas_call(
        functools.partial(shrink_kernel, rank, steps),
        out_shape=jax.ShapeDtypeStruct((2 * rows, 2 * rank), jnp.float32),
        grid_spec=pltpu.PrefetchScalarGridSpec(
            num_scalar_prefetch=1,
            grid=(2 * steps,),
            in_specs=[
                pl.BlockSpec((tile, 1), lambda i, ids: (i, 0)),
                pl.BlockSpec((tile, width), lambda i, ids: (jnp.minimum(i, steps - 1), 0)),
                pl.BlockSpec((tile, width), lambda i, ids: (jnp.maximum(i - steps, 0), 0)),
            ]
            + [pl.BlockSpec(block.shape, lambda i, ids: (0, 0)) for block in flat],
            out_specs=pl.BlockSpec((tile, 2 * rank), lambda i, ids: (i, 0)),
        ),
        compiler_params=pltpu.CompilerParams(vmem_limit_bytes=VMEM),
        cost_estimate=pl.CostEstimate(flops=1, bytes_accessed=1, transcendentals=0),
    )(ids, g, mine, other, *flat)


def expand_kernel(rank, ids_ref, g_ref, low_ref, base_ref, *refs):
    *blocks, o_ref, spread_ref = refs

    @pl.when(pl.program_id(0) == 0)
    def _():
        g = g_ref[...]
        low = low_ref[...].astype(jnp.float32)
        for pair in range(spread_ref.shape[1] // (2 * rank)):
            ids = ids_of_pair(ids_ref, 2 * pair, low.shape, rank)
            picked = jnp.where(g == ids, low, 0.0).astype(jnp.bfloat16)
            spread_ref[:, pair * 2 * rank : (pair + 1) * 2 * rank] = picked

    total = jnp.zeros(o_ref.shape, jnp.float32)
    seen = 0
    for block in blocks:
        deep = block.shape[0]
        total += jnp.dot(spread_ref[:, seen : seen + deep], block[...], preferred_element_type=jnp.float32)
        seen += deep
    o_ref[...] = base_ref[...] + adapter_scale * total


def expand(base, low, g, ids, blocks):
    rows = g.shape[0]
    _, rank, width = blocks[0].shape
    tile = min(512, width)
    flat = [block.reshape(-1, width) for block in blocks]
    deep = sum(block.shape[0] for block in flat)
    return pl.pallas_call(
        functools.partial(expand_kernel, rank),
        out_shape=jax.ShapeDtypeStruct((rows, width), jnp.float32),
        grid_spec=pltpu.PrefetchScalarGridSpec(
            num_scalar_prefetch=1,
            grid=(width // tile,),
            in_specs=[
                pl.BlockSpec((rows, 1), lambda i, ids: (0, 0)),
                pl.BlockSpec((rows, 2 * rank), lambda i, ids: (0, 0)),
                pl.BlockSpec((rows, tile), lambda i, ids: (0, i)),
            ]
            + [pl.BlockSpec((block.shape[0], tile), lambda i, ids: (0, i)) for block in flat],
            out_specs=pl.BlockSpec((rows, tile), lambda i, ids: (0, i)),
            scratch_shapes=[pltpu.VMEM((rows, deep), jnp.bfloat16)],
        ),
        compiler_params=pltpu.CompilerParams(vmem_limit_bytes=VMEM),
        cost_estimate=pl.CostEstimate(flops=1, bytes_accessed=1, transcendentals=0),
    )(ids, g, low, base, *flat)


def after(value, *others):
    return lax.optimization_barrier((value, *others))[0]


def wire(total):
    return total.astype(jnp.float16)


def unwire(block):
    return block.astype(jnp.float32)


def by_slots(line, z, weight, tokens):
    width = weight.shape[1] // line

    def sums(target):
        block = lax.dynamic_slice(weight, (0, target * width), (weight.shape[0], width))
        return BASE_WIRE * jnp.dot(tokens, block, preferred_element_type=jnp.float32)

    right = left = 0.0
    for slot in range(1, line):
        ahead, behind = (z - slot) % line, (z + slot) % line
        if 2 * slot <= line:
            one = sums(jnp.where(z < slot, ahead, behind))
            to_right, to_left = one + right, one + left
        else:
            to_right, to_left = sums(ahead) + right, sums(behind) + left
        going_right = [(i, i + 1) for i in range(slot)]
        going_left = [(line - 1 - i, line - 2 - i) for i in range(slot)]
        right = unwire(lax.ppermute(wire(to_right), "tensor", going_right))
        left = unwire(lax.ppermute(wire(to_left), "tensor", going_left))
    return right + left + sums(z)


def on_device(tokens, weight, down_stack, up_stack, fetch_list, choose):
    line = lax.axis_size("tensor")
    owners = lax.axis_size("dp")
    groups = lax.axis_size("groups")
    chips = owners // CORES
    z = lax.axis_index("tensor")
    me = lax.axis_index("dp")
    group = lax.axis_index("groups")
    x, core = me // CORES, me % CORES
    own, rank, width = down_stack.shape
    rows = tokens.shape[0]
    per_owner = fetch_list.shape[2]
    sibling = [(i, i ^ 1) for i in range(owners)]

    def to_sibling(block):
        return lax.ppermute(block, "dp", sibling)

    wanted = (jnp.arange(owners, dtype=jnp.int32)[:, None] * own + fetch_list[0]).reshape(-1)
    picked = choose[:, None] == jnp.arange(owners * per_owner, dtype=jnp.int32)[None, :]
    g = jnp.sum(jnp.where(picked, wanted[None, :], 0), axis=1)

    share = own // groups
    size = share // BANK_PIECES

    def slots(owner, first, count):
        return owner * own + first + jnp.arange(count, dtype=jnp.int32)

    def cross(stack, shift, piece, *gates):
        first = group * share + piece * size
        block = lax.dynamic_slice(stack, (first, 0, 0), (size, rank, width))
        block = lax.ppermute(after(block, *gates), "dp", [(i, (i + shift * CORES) % owners) for i in range(owners)])
        return block, slots((x - shift) % chips * CORES + core, first, size)

    def turn(block, shift, piece):
        found = []
        for step in range(1, groups):
            other = lax.ppermute(block, "groups", [(i, (i + step) % groups) for i in range(groups)])
            first = (group - step) % groups * share + piece * size
            found.append((other, slots((x - shift) % chips * CORES + core, first, size)))
        return found

    def shared(pairs):
        theirs = [(to_sibling(block), ids + jnp.where(core == 0, own, -own)) for block, ids in pairs]
        return pairs + theirs

    def product(target, rows_of):
        block = lax.dynamic_slice(weight, (0, target * width), (weight.shape[0], width))
        return BASE_WIRE * jnp.dot(rows_of, block, preferred_element_type=jnp.float32)

    mine = slots(me, 0, own)

    def shrink_by(tokens, tokens_other, g_both, pairs):
        ids = jnp.concatenate([ids for _, ids in pairs])
        return shrink(tokens, tokens_other, g_both, ids, [block for block, _ in pairs])

    def joined(halves):
        part = halves[:, :rank] + halves[:, rank:]
        part = part[:rows] + to_sibling(part[rows:])
        return jnp.concatenate([part[: rows // 2], part[rows // 2 :]], axis=1)

    def update(base, low, pairs):
        low = jnp.concatenate([low[:, :rank], low[:, rank:]], axis=0)
        ids = jnp.concatenate([ids for _, ids in pairs])
        return expand(base, jnp.concatenate([low, low], axis=1), g[:, None], ids, [block for block, _ in pairs])

    if line != 4 or chips != 2 or groups != 2:
        summed = by_slots(line, z, weight, tokens) * (1.0 / BASE_WIRE)
        g_both = jnp.concatenate([g, to_sibling(g)])[:, None]
        banks = []
        for stack in (down_stack, up_stack):
            pairs = [(stack, mine)]
            for shift in range(1, chips):
                for piece in range(BANK_PIECES):
                    block, ids = cross(stack, shift, piece)
                    pairs += [(block, ids), *turn(block, shift, piece)]
            banks.append(pairs)
        part = joined(shrink_by(tokens, to_sibling(tokens), g_both, banks[0]))
        low = lax.psum(part, "tensor").astype(jnp.bfloat16)
        return update(summed, low, shared(banks[1])).astype(jnp.bfloat16)

    outer = [(0, 1), (3, 2)]
    inner = [(1, 2), (2, 1)]
    both = [(0, 1), (1, 0), (2, 3), (3, 2)]
    low_half = z < 2
    targets = [jnp.where(low_half, 3, 0), jnp.where(low_half, 2, 1), jnp.array([1, 0, 3, 2], jnp.int32)[z]]

    def hop(block, pairs):
        return lax.ppermute(block, "tensor", pairs)

    def part_of(block, span):
        return lax.slice_in_dim(block, span[0], span[0] + span[1])

    spans = [(0, rows * 3 // 8), (rows * 3 // 8, rows * 5 // 8)]
    d0, d0_ids = cross(down_stack, 1, 0)
    up_other = to_sibling(up_stack)
    first = wire(product(targets[0], tokens))
    first, tokens, g, down, up, up_other = lax.optimization_barrier(
        (first, tokens, g, down_stack, up_stack, up_other)
    )

    a1 = hop(first, outer)
    g_other, tokens_other = to_sibling(g), to_sibling(tokens)
    later = after(tokens, g_other, tokens_other)
    second = wire(product(targets[1], later))
    d0 = after(d0, second)
    d1, d1_ids = cross(down, 1, 1, d0)
    [(d2, d2_ids)] = turn(d0, 1, 0)
    third = wire(product(targets[2], after(later, d0)))
    g_both = jnp.concatenate([g, g_other])[:, None]
    first, second, third, a1, tokens, tokens_other = lax.optimization_barrier(
        (first, second, third, a1, tokens, tokens_other)
    )

    d1 = after(d1, a1)

    a2 = hop(second, outer)
    b1 = hop(wire(unwire(first) + unwire(a1)), inner)
    [(d3, d3_ids)] = turn(d1, 1, 1)
    u0, u0_ids = cross(up, 1, 0, d1)
    u1, u1_ids = cross(up, 1, 1, u0)
    halves = shrink_by(after(tokens, d2), tokens_other, g_both, [(down_stack, mine)])
    home = product(z, tokens) * (1.0 / BASE_WIRE)
    later = after(tokens, home)
    halves += shrink_by(later, tokens_other, g_both, [(d0, d0_ids), (d1, d1_ids), (d2, d2_ids), (d3, d3_ids)])
    part = joined(halves)
    [(u2, u2_ids)] = turn(u0, 1, 0)
    ups = [(up, mine), (up_other, slots(me ^ 1, 0, own)), *shared([(u0, u0_ids), (u1, u1_ids), (u2, u2_ids)])]
    late = turn(u1, 1, 1)
    part += hop(after(part, a2), both)
    c1 = [wire(unwire(part_of(third, span)) + unwire(part_of(b1, span))) for span in spans]
    b2 = wire(unwire(second) + unwire(a2))
    part, c1[0], home, *seen = lax.optimization_barrier((part, c1[0], home, *[block for block, _ in ups]))
    ups = [(block, ids) for block, (_, ids) in zip(seen, ups)]

    a3 = [hop(block, both) for block in c1]
    part += hop(part, inner)
    b2 = hop(after(b2, part), inner)
    low = part.astype(jnp.bfloat16)
    low = jnp.where((z == 1) | (z == 2), low, hop(low, [(1, 0), (2, 3)]))
    adapted = update(home, after(low, a3[0]), ups)
    adapted = update(adapted, low, shared(late))
    out = jnp.zeros((rows, width), jnp.bfloat16)
    for arrived, span in zip(a3, spans):
        wired = unwire(arrived) + unwire(part_of(b2, span))
        total = part_of(adapted, span) + wired * (1.0 / BASE_WIRE)
        out = lax.dynamic_update_slice(lax.optimization_barrier(out), total.astype(jnp.bfloat16), (span[0], 0))
    return out


def solution(mesh):
    return jax.shard_map(
        on_device,
        mesh=mesh,
        in_specs=(
            P(("groups", "dp"), "tensor"),
            P("tensor", None),
            P("dp", None, "tensor"),
            P("dp", None, "tensor"),
            P(("groups", "dp"), None, None),
            P(("groups", "dp")),
        ),
        out_specs=P(("groups", "dp"), "tensor"),
        check_vma=False,
    )
```

time: 345 us -> 197 us (0.57)
  waiting for transfers between devices: 212 us -> 63.9 us
  Pallas kernels: 0 us -> 36.7 us
  blocking collectives: 30 us -> 0 us
  other arithmetic: 2.82 us -> 19.1 us
  starting transfers between devices: 14.4 us -> 29.7 us
  local copies, waits for them, and re-layouts: 21.9 us -> 6.61 us
  between operations: 13.4 us -> 1.07 us
  matrix products: 45.1 us -> 37.7 us
    all_to_all x2 -> x0, waiting for transfers between devices: 141 us -> none  [the longest x1 84.3 us: on_device(): lax.all_to_all(down_out, 'dp', split_axis=0, concat_axis=0, tiled=True)]
    reduce_scatter x1 -> x0, waiting for transfers between devices: 70.7 us -> none  [on_device(): lax.psum_scatter(lax.dot_general(weight, tokens, (((0,), (1,)), ((), ()))...]
    ppermute x0 -> x25, waiting for transfers between devices: none -> 63.9 us  [the longest x4 25.8 us: cross(): lax.ppermute(after(block, *gates), 'dp', [(i, (i + shift * CORES) % owner...]
    pallas_call x0 -> x4, Pallas kernels: none -> 36.7 us  [the longest x2 19.7 us: expand(): pl.pallas_call(functools.partial(expand_kernel, rank), out_shape=jax.Shap...]
    ppermute x0 -> x25, starting transfers between devices: none -> 29.7 us  [the longest x9 18 us: hop(): return lax.ppermute(block, 'tensor', pairs)]
    psum x1 -> x0, blocking collectives: 25.2 us -> none  [on_device(): low_rank_shrink = lax.psum(own_shrink, 'tensor').astype(jnp.bfloat16)]
    gather x2 -> x0, local copies, waits for them, and re-layouts: 15.2 us -> none  [the longest x1 7.89 us: on_device(): down_weight_stack[flat_ids]]
    all_to_all x2 -> x0, starting transfers between devices: 14.4 us -> none  [the longest x1 7.41 us: on_device(): lax.all_to_all(up_out, 'dp', split_axis=0, concat_axis=0, tiled=True)]
  transfers between devices with their start and end apart: 3 -> 25, of which waited for: 3 -> 8; matrix products, arithmetic and copies ran while one was open for 8% -> 31% of each run, Pallas kernels for 0% -> 19%
where the time goes in v2:
time: 197 us; the launch traced here: 195 us
  waiting for transfers between devices  63.9 us (32%)
  matrix products  37.7 us (19%)
  Pallas kernels  36.7 us (19%)
  starting transfers between devices  29.7 us (15%)
  other arithmetic  19.1 us (10%)
  local copies, waits for them, and re-layouts  6.61 us (3%)
    dot_general x4, matrix products, product(): jnp.dot(rows_of, block, preferred_element_type=jnp.float32)  37.7 us
    ppermute x4, waiting for transfers between devices, cross(): lax.ppermute(after(block, *gates), 'dp', [(i, (i + shift * CORES) % owner...  25.8 us
    ppermute x9, waiting for transfers between devices, hop(): return lax.ppermute(block, 'tensor', pairs)  24 us
    pallas_call x2, Pallas kernels, expand(): pl.pallas_call(functools.partial(expand_kernel, rank), out_shape=jax.Shap...  19.7 us
    ppermute x9, starting transfers between devices, hop(): return lax.ppermute(block, 'tensor', pairs)  18 us
    pallas_call x2, Pallas kernels, shrink(): pl.pallas_call(functools.partial(shrink_kernel, rank, steps), out_shape=j...  17 us
    ppermute x4, waiting for transfers between devices, turn(): lax.ppermute(block, 'groups', [(i, (i + step) % groups) for i in range(gr...  12.5 us
    convert_element_type x4, other arithmetic, wire(): return total.astype(jnp.float16)  12 us
  transfers between devices with their start and end apart: 25, of which 8 were waited for; matrix products, arithmetic and copies ran while one was open for 31% of the time, Pallas kernels for 19%

profile of v2, /device:TPU:10, one launch (start us, length us, event | category | flops | bytes accessed | tf_op | source)
XLA Modules:
  0.0 194.8 jit_solution(17418969452367811028)
XLA Ops:
  0.0 0.1 add.208
  0.1 0.1 add.209
  0.2 0.8 squeeze.4
  0.9 0.8 select_reduce_fusion
  1.7 10.0 %fusion.14 = f16[512,2048]{1,0:T(8,128)(2,1)} fusion(bf16[512,2048]{1,0:T(8,128)(2,1)} %mine_ref.1, bf16[2048,8192]{1,0:T(8,128)(2,1)} %param.8, s32[]{:T(128)S(6)} %select_n.93), kind=kOutput, calls=%fused_computation.13 | convolution fusion | flops 4297064448 | bytes 12582916 | tf_op jit(solution)/shard_map/dot_general | solution.py:201
  11.7 0.6 collective-permute-start.2
  12.3 1.3 constant_dynamic-slice_fusion.3
  13.6 0.6 collective-permute-start.3
  14.2 0.6 dynamic_slice.30
  15.4 0.1 collective-permute-start.1
  15.5 1.3 collective-permute-start.4
  16.8 1.3 constant_dynamic-slice_fusion.2
  18.2 9.2 %multiply_convert_fusion.1 = f16[512,2048]{1,0:T(8,128)(2,1)} fusion(bf16[512,2048]{1,0:T(8,128)(2,1)S(1)} %copy-done, bf16[2048,8192]{1,0:T(8,128)(2,1)} %param.8, s32[]{:T(128)S(6)} %select_n.97), kind=kOutput, calls=%fused_computation.11 | convolution fusion | flops 4297064448 | bytes 12582916 | tf_op jit(solution)/shard_map/dot_general | solution.py:201
  27.4 11.4 %collective-permute-done.3 = bf16[4,64,2048]{2,1,0:T(8,128)(2,1)} collective-permute-done((bf16[4,64,2048]{2,1,0:T(8,128)(2,1)S(1)}, bf16[4,64,2048]{2,1,0:T(8,128)(2,1)}, u32[]{:S(2)}, u32[]{:S(2)}) %collective-permute-start.3) | collective-permute-done | bytes 1048608 | tf_op jit(solution)/shard_map/ppermute | solution.py:184
  38.8 0.5 collective-permute-start.6
  39.4 1.5 constant_dynamic-slice_fusion
  40.9 1.5 collective-permute-start.5
  42.4 9.1 %multiply_convert_fusion = f16[512,2048]{1,0:T(8,128)(2,1)} fusion(bf16[512,2048]{1,0:T(8,128)(2,1)S(1)} %copy-done, bf16[2048,8192]{1,0:T(8,128)(2,1)} %param.8, s32[]{:T(128)S(6)} %select_n.100), kind=kOutput, calls=%fused_computation.10 | convolution fusion | flops 4297064448 | bytes 12582916 | tf_op jit(solution)/shard_map/dot_general | solution.py:201
  51.5 14.1 %collective-permute-done.4 = f16[512,2048]{1,0:T(8,128)(2,1)S(1)} collective-permute-done((f16[512,2048]{1,0:T(8,128)(2,1)}, f16[512,2048]{1,0:T(8,128)(2,1)S(1)}, u32[]{:S(2)}, u32[]{:S(2)}) %collective-permute-start.4) | collective-permute-done | bytes 2097184 | tf_op jit(solution)/shard_map/ppermute | solution.py:241
  65.6 1.5 collective-permute-start.12
  67.1 2.3 %add_convert_fusion.1 = f16[512,2048]{1,0:T(8,128)(2,1)} fusion(f16[512,2048]{1,0:T(8,128)(2,1)S(1)} %collective-permute-done.4, f16[512,2048]{1,0:T(8,128)(2,1)S(1)} %copy-done.5), kind=kLoop, calls=%fused_computation.9 | loop fusion | flops 4194304 | bytes 6291456 | tf_op jit(solution)/shard_map/convert_element_type | solution.py:125
  69.5 3.5 %collective-permute-start.11 = (f16[512,2048]{1,0:T(8,128)(2,1)}, f16[512,2048]{1,0:T(8,128)(2,1)}, u32[]{:S(2)}, u32[]{:S(2)}) collective-permute-start(f16[512,2048]{1,0:T(8,128)(2,1)} %add_convert_fusion.1), channel_id=1, source_target_pairs={{1,2},{2,1},{5,6},{6,5},{9,10},{10,9},{13,14},{14,13},{17,18},{18,... | collective-permute-start | bytes 6291464 | tf_op jit(solution)/shard_map/ppermute | solution.py:241
  72.9 1.5 collective-permute-start.9
  74.4 1.6 collective-permute-start.7
  76.0 0.1 pad_add_fusion.2.ids_ref
  76.1 0.2 copy.15.g_ref
  76.3 14.4 %collective-permute-done.12 = bf16[4,64,2048]{2,1,0:T(8,128)(2,1)} collective-permute-done((bf16[4,64,2048]{2,1,0:T(8,128)(2,1)}, bf16[4,64,2048]{2,1,0:T(8,128)(2,1)}, u32[]{:S(2)}, u32[]{:S(2)}) %collective-permute-start.12) | collective-permute-done | bytes 1048608 | tf_op jit(solution)/shard_map/ppermute | solution.py:184
  90.7 1.5 collective-permute-start.13
  92.2 1.5 collective-permute-start.14
  93.7 9.4 %fusion.base_ref = f32[512,2048]{1,0:T(8,128)} fusion(bf16[512,2048]{1,0:T(8,128)(2,1)S(1)} %copy-done, bf16[2048,8192]{1,0:T(8,128)(2,1)} %param.8, s32[]{:T(128)S(6)} %select_n.101), kind=kOutput, calls=%fused_computation | convolution fusion | flops 4294967296 | bytes 14680068 | tf_op jit(solution)/shard_map/dot_general | solution.py:201
  103.2 8.3 %shard_map.73 = f32[1024,128]{1,0:T(8,128)S(1)} custom-call(s32[16]{0:T(128)S(1)} %iota_add_fusion.4.ids_ref, s32[1024,1]{1,0:T(8,128)S(1)} %copy.15.g_ref, bf16[512,2048]{1,0:T(8,128)(2,1)S(1)} %copy-done, bf16[512,2048]{1,0:T(8,128)(2,1)} %collective-permute-done.2.other_ref, bf16[1024,2048]{1,0:T(8,128)(2,1)} %bitcast.30), custom_call_target="tpu_custom_call" | custom-call | flops 1 | bytes 1 | tf_op jit(solution)/shard_map/pallas_call | solution.py:54
  111.5 8.7 %shard_map.74 = f32[1024,128]{1,0:T(8,128)S(1)} custom-call(s32[16]{0:T(128)S(1)} %pad_add_fusion.2.ids_ref, s32[1024,1]{1,0:T(8,128)S(1)} %copy.15.g_ref, bf16[512,2048]{1,0:T(8,128)(2,1)} %mine_ref.1, bf16[512,2048]{1,0:T(8,128)(2,1)} %collective-permute-done.2.other_ref, bf16[256,2048]{1,0:T(8,128)(2,1)} %bitcast.5.refs_0_, ...), custom_call_target="tpu_custom_call" | custom-call | flops 1 | bytes 1 | tf_op jit(solution)/shard_map/pallas_call | solution.py:54
  120.3 0.2 slice_add_fusion.2
  120.6 1.5 collective-permute-done.8
  122.1 0.1 collective-permute-start.15
  122.3 0.4 collective-permute-start.16
  122.7 0.1 collective-permute-start.17
  122.9 0.1 pad_maximum_fusion
  123.0 2.1 %collective-permute-start.10 = (f32[256,128]{1,0:T(8,128)S(1)}, f32[256,128]{1,0:T(8,128)S(1)}, u32[]{:S(2)}, u32[]{:S(2)}) collective-permute-start(f32[256,128]{1,0:T(8,128)S(1)} %pad_maximum_fusion), channel_id=1, source_target_pairs={{0,1},{1,0},{2,3},{3,2},{4,5},{5,4},{6,7},{7,6},{8,9},{9,8},{10,11... | collective-permute-start | bytes 393224 | tf_op jit(solution)/shard_map/ppermute | solution.py:241
  125.1 2.6 %add_convert_fusion.3 = f16[192,2048]{1,0:T(8,128)(2,1)} fusion(f16[512,2048]{1,0:T(8,128)(2,1)} %collective-permute-done.11, f16[512,2048]{1,0:T(8,128)(2,1)} %multiply_convert_fusion), kind=kLoop, calls=%fused_computation.19 | loop fusion | flops 1572864 | bytes 2359296 | tf_op jit(solution)/shard_map/convert_element_type | solution.py:125
  127.6 1.6 collective-permute-done.10
  129.2 0.1 fusion.32
  129.3 1.6 collective-permute-start.21
  130.9 2.4 %collective-permute-start.18 = (f32[256,128]{1,0:T(8,128)S(1)}, f32[256,128]{1,0:T(8,128)S(1)}, u32[]{:S(2)}, u32[]{:S(2)}) collective-permute-start(f32[256,128]{1,0:T(8,128)S(1)} %fusion.32), channel_id=1, source_target_pairs={{1,2},{2,1},{5,6},{6,5},{9,10},{10,9},{13,14},{14,13},{17,18},{18,... | collective-permute-start | bytes 393224 | tf_op jit(solution)/shard_map/ppermute | solution.py:241
  133.3 4.7 %add_convert_fusion = f16[512,2048]{1,0:T(8,128)(2,1)} fusion(f16[512,2048]{1,0:T(8,128)(2,1)} %collective-permute-done.9, f16[512,2048]{1,0:T(8,128)(2,1)} %multiply_convert_fusion.1), kind=kLoop, calls=%fused_computation.8 | loop fusion | flops 4194304 | bytes 6291456 | tf_op jit(solution)/shard_map/convert_element_type | solution.py:125
  138.1 3.5 %collective-permute-start.23 = (f16[512,2048]{1,0:T(8,128)(2,1)}, f16[512,2048]{1,0:T(8,128)(2,1)}, u32[]{:S(2)}, u32[]{:S(2)}) collective-permute-start(f16[512,2048]{1,0:T(8,128)(2,1)} %add_convert_fusion), channel_id=1, source_target_pairs={{1,2},{2,1},{5,6},{6,5},{9,10},{10,9},{13,14},{14,13},{17,18},{18,... | collective-permute-start | bytes 6291464 | tf_op jit(solution)/shard_map/ppermute | solution.py:241
  141.6 0.1 concatenate.33.ids_ref
  141.7 0.1 pad_add_fusion.1.ids_ref
  141.8 0.1 copy.18.g_ref
  142.0 12.5 %collective-permute-done.21 = bf16[4,64,2048]{2,1,0:T(8,128)(2,1)S(1)} collective-permute-done((bf16[4,64,2048]{2,1,0:T(8,128)(2,1)}, bf16[4,64,2048]{2,1,0:T(8,128)(2,1)S(1)}, u32[]{:S(2)}, u32[]{:S(2)}) %collective-permute-start.21) | collective-permute-done | bytes 1048608 | tf_op jit(solution)/shard_map/ppermute | solution.py:190
  154.6 3.7 %collective-permute-start.19 = (bf16[256,128]{1,0:T(8,128)(2,1)S(1)}, bf16[256,128]{1,0:T(8,128)(2,1)S(1)}, u32[]{:S(2)}, u32[]{:S(2)}) collective-permute-start(bf16[256,128]{1,0:T(8,128)(2,1)S(1)} %add.235), channel_id=1, source_target_pairs={{1,0},{2,3},{5,4},{6,7},{9,8},{10,11},{13,12},{14,15},{17,16},{18,... | collective-permute-start | bytes 196616 | tf_op jit(solution)/shard_map/ppermute | solution.py:241
  158.3 2.4 %add_convert_fusion.2 = f16[320,2048]{1,0:T(8,128)(2,1)S(1)} fusion(f16[512,2048]{1,0:T(8,128)(2,1)} %collective-permute-done.11, f16[512,2048]{1,0:T(8,128)(2,1)} %multiply_convert_fusion), kind=kLoop, calls=%fused_computation.16 | loop fusion | flops 2621440 | bytes 3932160 | tf_op jit(solution)/shard_map/convert_element_type | solution.py:125
  160.7 0.1 collective-permute-start.24
  160.8 0.1 fusion.27
  160.9 0.1 maximum_maximum_fusion.low_ref
  161.0 0.1 fusion.26
  161.1 0.1 maximum_maximum_fusion.1.low_ref
  161.2 13.3 %shard_map.75.base_ref = f32[512,2048]{1,0:T(8,128)} custom-call(s32[56]{0:T(128)S(1)} %concatenate.33.ids_ref, s32[512,1]{1,0:T(8,128)S(1)} %copy.18.g_ref, bf16[512,128]{1,0:T(8,128)(2,1)S(1)} %maximum_maximum_fusion.1.low_ref, f32[512,2048]{1,0:T(8,128)} %fusion.base_ref, bf16[1024,2048]{1,0:T(8,128)(2,1)} %bitcast.29, ...), custom_call_target="tpu_custom_call" | custom-call | flops 1 | bytes 1 | tf_op jit(solution)/shard_map/pallas_call | solution.py:100
  174.5 6.4 %shard_map.76 = f32[512,2048]{1,0:T(8,128)} custom-call(s32[8]{0:T(128)S(1)} %pad_add_fusion.1.ids_ref, s32[512,1]{1,0:T(8,128)S(1)} %copy.18.g_ref, bf16[512,128]{1,0:T(8,128)(2,1)S(1)} %maximum_maximum_fusion.low_ref, f32[512,2048]{1,0:T(8,128)} %shard_map.75.base_ref, bf16[256,2048]{1,0:T(8,128)(2,1)S(1)} %bitcast.27, bf16[256,2048]{1,0:T(8,128)(2,1)S(1)} %bitcast.28), custom_call_target="tpu_custom_call" | custom-call | flops 1 | bytes 1 | tf_op jit(solution)/shard_map/pallas_call | solution.py:100
  180.9 6.1 %collective-permute-done.23 = f16[512,2048]{1,0:T(8,128)(2,1)} collective-permute-done((f16[512,2048]{1,0:T(8,128)(2,1)}, f16[512,2048]{1,0:T(8,128)(2,1)}, u32[]{:S(2)}, u32[]{:S(2)}) %collective-permute-start.23) | collective-permute-done | bytes 2097184 | tf_op jit(solution)/shard_map/ppermute | solution.py:241
  187.1 0.2 broadcast_in_dim.25
  187.3 2.1 %fusion.20 = bf16[512,2048]{1,0:T(8,128)(2,1)S(1)} fusion(bf16[512,2048]{1,0:T(8,128)(2,1)S(1)} %broadcast_in_dim.25, f16[192,2048]{1,0:T(8,128)(2,1)S(1)} %collective-permute-done.20, f32[512,2048]{1,0:T(8,128)} %shard_map.76, f16[512,2048]{1,0:T(8,128)(2,1)} %collective-permute-done.23), kind=kLoop, calls=%fused_computation.21 | loop fusion | flops 2359296 | bytes 3932160 | tf_op jit(solution)/shard_map/dynamic_update_slice | solution.py:299
  189.5 2.1 %collective-permute-done.24 = f16[320,2048]{1,0:T(8,128)(2,1)S(1)} collective-permute-done((f16[320,2048]{1,0:T(8,128)(2,1)S(1)}, f16[320,2048]{1,0:T(8,128)(2,1)S(1)}, u32[]{:S(2)}, u32[]{:S(2)}) %collective-permute-start.24) | collective-permute-done | bytes 1310752 | tf_op jit(solution)/shard_map/ppermute | solution.py:241
  191.6 3.2 %fusion.19 = bf16[512,2048]{1,0:T(8,128)(2,1)} fusion(bf16[512,2048]{1,0:T(8,128)(2,1)} %copy-done.6, f16[320,2048]{1,0:T(8,128)(2,1)S(1)} %collective-permute-done.24, f32[512,2048]{1,0:T(8,128)S(1)} %copy-done.3, f16[512,2048]{1,0:T(8,128)(2,1)} %collective-permute-done.23), kind=kLoop, calls=%fused_computation.20 | loop fusion | flops 3932160 | bytes 6553600 | tf_op jit(solution)/shard_map/dynamic_update_slice | solution.py:299
  (56 shorter events, 0.4 us)
Async XLA Ops:
  0.0 11.7 %collective-permute-start = (bf16[16,64,2048]{2,1,0:T(8,128)(2,1)}, bf16[16,64,2048]{2,1,0:T(8,128)(2,1)}, u32[]{:S(2)}, u32[]{:S(2)}) collective-permute-start(bf16[16,64,2048]{2,1,0:T(8,128)(2,1)} %param.10), channel_id=1, source_target_pairs={{0,4},{4,0},{8,12},{12,8},{1,5},{5,1},{9,13},{13,9},{2,6},{6,2},{1... | collective-permute-start | bytes 12582920 | tf_op jit(solution)/shard_map/ppermute | solution.py:169
  1.7 10.0 %copy-start = (bf16[512,2048]{1,0:T(8,128)(2,1)S(1)}, bf16[512,2048]{1,0:T(8,128)(2,1)}, u32[]{:S(2)}) copy-start(bf16[512,2048]{1,0:T(8,128)(2,1)} %mine_ref.1) | copy-start | bytes 6291460
  11.7 2.5 %copy-start.8 = (s32[4]{0:T(128)S(1)}, s32[4]{0:T(128)}, u32[]{:S(2)}) copy-start(s32[4]{0:T(128)} %constant.101.clone) | copy-start | bytes 52
  11.7 6.5 %collective-permute-start.2 = (bf16[512,2048]{1,0:T(8,128)(2,1)S(1)}, bf16[512,2048]{1,0:T(8,128)(2,1)}, u32[]{:S(2)}, u32[]{:S(2)}) collective-permute-start(bf16[512,2048]{1,0:T(8,128)(2,1)S(1)} %copy-done), channel_id=1, source_target_pairs={{0,4},{4,0},{8,12},{12,8},{1,5},{5,1},{9,13},{13,9},{2,6},{6,2},{1... | collective-permute-start | bytes 6291464 | tf_op jit(solution)/shard_map/ppermute | solution.py:169
  13.6 25.3 %collective-permute-start.3 = (bf16[4,64,2048]{2,1,0:T(8,128)(2,1)S(1)}, bf16[4,64,2048]{2,1,0:T(8,128)(2,1)}, u32[]{:S(2)}, u32[]{:S(2)}) collective-permute-start(bf16[4,64,2048]{2,1,0:T(8,128)(2,1)S(1)} %constant_dynamic-slice_fusion.3), channel_id=1, source_target_pairs={{0,8},{4,12},{8,0},{12,4},{1,9},{5,13},{9,1},{13,5},{2,10},{6,14},... | collective-permute-start | bytes 3145736 | tf_op jit(solution)/shard_map/ppermute | solution.py:184
  15.4 2.7 %collective-permute-start.1 = (s32[512]{0:T(512)S(1)}, s32[512]{0:T(512)S(1)}, u32[]{:S(2)}, u32[]{:S(2)}) collective-permute-start(s32[512]{0:T(512)S(1)} %select_reduce_fusion), channel_id=1, source_target_pairs={{0,4},{4,0},{8,12},{12,8},{1,5},{5,1},{9,13},{13,9},{2,6},{6,2},{1... | collective-permute-start | bytes 6152 | tf_op jit(solution)/shard_map/ppermute | solution.py:169
  15.5 50.1 %collective-permute-start.4 = (f16[512,2048]{1,0:T(8,128)(2,1)}, f16[512,2048]{1,0:T(8,128)(2,1)S(1)}, u32[]{:S(2)}, u32[]{:S(2)}) collective-permute-start(f16[512,2048]{1,0:T(8,128)(2,1)} %fusion.14), channel_id=1, source_target_pairs={{0,1},{3,2},{4,5},{7,6},{8,9},{11,10},{12,13},{15,14},{16,17},{19,... | collective-permute-start | bytes 6291464 | tf_op jit(solution)/shard_map/ppermute | solution.py:241
  18.1 21.2 %copy-start.4 = (bf16[16,64,2048]{2,1,0:T(8,128)(2,1)S(1)}, bf16[16,64,2048]{2,1,0:T(8,128)(2,1)}, u32[]{:S(2)}) copy-start(bf16[16,64,2048]{2,1,0:T(8,128)(2,1)} %param.10) | copy-start | bytes 12582916
  38.8 26.8 %collective-permute-start.6 = (bf16[4,64,2048]{2,1,0:T(8,128)(2,1)S(1)}, bf16[4,64,2048]{2,1,0:T(8,128)(2,1)}, u32[]{:S(2)}, u32[]{:S(2)}) collective-permute-start(bf16[4,64,2048]{2,1,0:T(8,128)(2,1)S(1)} %constant_dynamic-slice_fusion.2), channel_id=1, source_target_pairs={{0,8},{4,12},{8,0},{12,4},{1,9},{5,13},{9,1},{13,5},{2,10},{6,14},... | collective-permute-start | bytes 3145736 | tf_op jit(solution)/shard_map/ppermute | solution.py:184
  40.9 26.2 %copy-start.5 = (f16[512,2048]{1,0:T(8,128)(2,1)S(1)}, f16[512,2048]{1,0:T(8,128)(2,1)}, u32[]{:S(2)}) copy-start(f16[512,2048]{1,0:T(8,128)(2,1)} %fusion.14) | copy-start | bytes 6291460
  40.9 51.3 %collective-permute-start.5 = (bf16[4,64,2048]{2,1,0:T(8,128)(2,1)}, bf16[4,64,2048]{2,1,0:T(8,128)(2,1)}, u32[]{:S(2)}, u32[]{:S(2)}) collective-permute-start(bf16[4,64,2048]{2,1,0:T(8,128)(2,1)} %collective-permute-done.3), channel_id=1, source_target_pairs={{0,16},{16,0},{1,17},{17,1},{2,18},{18,2},{3,19},{19,3},{4,20},{20... | collective-permute-start | bytes 3145736 | tf_op jit(solution)/shard_map/ppermute | solution.py:190
  65.6 25.1 %collective-permute-start.12 = (bf16[4,64,2048]{2,1,0:T(8,128)(2,1)}, bf16[4,64,2048]{2,1,0:T(8,128)(2,1)}, u32[]{:S(2)}, u32[]{:S(2)}) collective-permute-start(bf16[4,64,2048]{2,1,0:T(8,128)(2,1)} %get-tuple-element.60), channel_id=1, source_target_pairs={{0,8},{4,12},{8,0},{12,4},{1,9},{5,13},{9,1},{13,5},{2,10},{6,14},... | collective-permute-start | bytes 3145736 | tf_op jit(solution)/shard_map/ppermute | solution.py:184
  69.5 55.6 %collective-permute-start.11 = (f16[512,2048]{1,0:T(8,128)(2,1)}, f16[512,2048]{1,0:T(8,128)(2,1)}, u32[]{:S(2)}, u32[]{:S(2)}) collective-permute-start(f16[512,2048]{1,0:T(8,128)(2,1)} %add_convert_fusion.1), channel_id=1, source_target_pairs={{1,2},{2,1},{5,6},{6,5},{9,10},{10,9},{13,14},{14,13},{17,18},{18,... | collective-permute-start | bytes 6291464 | tf_op jit(solution)/shard_map/ppermute | solution.py:241
  72.9 50.0 %collective-permute-start.9 = (f16[512,2048]{1,0:T(8,128)(2,1)}, f16[512,2048]{1,0:T(8,128)(2,1)}, u32[]{:S(2)}, u32[]{:S(2)}) collective-permute-start(f16[512,2048]{1,0:T(8,128)(2,1)} %multiply_convert_fusion.1), channel_id=1, source_target_pairs={{0,1},{3,2},{4,5},{7,6},{8,9},{11,10},{12,13},{15,14},{16,17},{19,... | collective-permute-start | bytes 6291464 | tf_op jit(solution)/shard_map/ppermute | solution.py:241
  74.4 37.1 %collective-permute-start.7 = (bf16[4,64,2048]{2,1,0:T(8,128)(2,1)}, bf16[4,64,2048]{2,1,0:T(8,128)(2,1)}, u32[]{:S(2)}, u32[]{:S(2)}) collective-permute-start(bf16[4,64,2048]{2,1,0:T(8,128)(2,1)} %collective-permute-done.6), channel_id=1, source_target_pairs={{0,16},{16,0},{1,17},{17,1},{2,18},{18,2},{3,19},{19,3},{4,20},{20... | collective-permute-start | bytes 3145736 | tf_op jit(solution)/shard_map/ppermute | solution.py:190
  90.7 31.6 %collective-permute-start.13 = (bf16[4,64,2048]{2,1,0:T(8,128)(2,1)}, bf16[4,64,2048]{2,1,0:T(8,128)(2,1)}, u32[]{:S(2)}, u32[]{:S(2)}) collective-permute-start(bf16[4,64,2048]{2,1,0:T(8,128)(2,1)} %get-tuple-element.61), channel_id=1, source_target_pairs={{0,8},{4,12},{8,0},{12,4},{1,9},{5,13},{9,1},{13,5},{2,10},{6,14},... | collective-permute-start | bytes 3145736 | tf_op jit(solution)/shard_map/ppermute | solution.py:184
  92.2 30.5 %collective-permute-start.14 = (bf16[4,64,2048]{2,1,0:T(8,128)(2,1)}, bf16[4,64,2048]{2,1,0:T(8,128)(2,1)S(1)}, u32[]{:S(2)}, u32[]{:S(2)}) collective-permute-start(bf16[4,64,2048]{2,1,0:T(8,128)(2,1)} %collective-permute-done.12), channel_id=1, source_target_pairs={{0,16},{16,0},{1,17},{17,1},{2,18},{18,2},{3,19},{19,3},{4,20},{20... | collective-permute-start | bytes 3145736 | tf_op jit(solution)/shard_map/ppermute | solution.py:190
  120.5 1.6 collective-permute-start.8
  122.1 8.8 %collective-permute-start.15 = (bf16[4,64,2048]{2,1,0:T(8,128)(2,1)}, bf16[4,64,2048]{2,1,0:T(8,128)(2,1)S(1)}, u32[]{:S(2)}, u32[]{:S(2)}) collective-permute-start(bf16[4,64,2048]{2,1,0:T(8,128)(2,1)} %collective-permute-done.12), channel_id=1, source_target_pairs={{0,4},{4,0},{8,12},{12,8},{1,5},{5,1},{9,13},{13,9},{2,6},{6,2},{1... | collective-permute-start | bytes 3145736 | tf_op jit(solution)/shard_map/ppermute | solution.py:169
  122.3 8.6 %collective-permute-start.16 = (bf16[4,64,2048]{2,1,0:T(8,128)(2,1)}, bf16[4,64,2048]{2,1,0:T(8,128)(2,1)S(1)}, u32[]{:S(2)}, u32[]{:S(2)}) collective-permute-start(bf16[4,64,2048]{2,1,0:T(8,128)(2,1)} %collective-permute-done.13), channel_id=1, source_target_pairs={{0,4},{4,0},{8,12},{12,8},{1,5},{5,1},{9,13},{13,9},{2,6},{6,2},{1... | collective-permute-start | bytes 3145736 | tf_op jit(solution)/shard_map/ppermute | solution.py:169
  122.7 15.3 %copy-start.1 = (bf16[4,64,2048]{2,1,0:T(8,128)(2,1)}, bf16[4,64,2048]{2,1,0:T(8,128)(2,1)S(1)}, u32[]{:S(2)}) copy-start(bf16[4,64,2048]{2,1,0:T(8,128)(2,1)S(1)} %collective-permute-done.14) | copy-start | bytes 3145732
  122.7 8.2 %collective-permute-start.17 = (bf16[4,64,2048]{2,1,0:T(8,128)(2,1)S(1)}, bf16[4,64,2048]{2,1,0:T(8,128)(2,1)S(1)}, u32[]{:S(2)}, u32[]{:S(2)}) collective-permute-start(bf16[4,64,2048]{2,1,0:T(8,128)(2,1)S(1)} %collective-permute-done.14), channel_id=1, source_target_pairs={{0,4},{4,0},{8,12},{12,8},{1,5},{5,1},{9,13},{13,9},{2,6},{6,2},{1... | collective-permute-start | bytes 3145736 | tf_op jit(solution)/shard_map/ppermute | solution.py:169
  123.0 6.2 %collective-permute-start.10 = (f32[256,128]{1,0:T(8,128)S(1)}, f32[256,128]{1,0:T(8,128)S(1)}, u32[]{:S(2)}, u32[]{:S(2)}) collective-permute-start(f32[256,128]{1,0:T(8,128)S(1)} %pad_maximum_fusion), channel_id=1, source_target_pairs={{0,1},{1,0},{2,3},{3,2},{4,5},{5,4},{6,7},{7,6},{8,9},{9,8},{10,11... | collective-permute-start | bytes 393224 | tf_op jit(solution)/shard_map/ppermute | solution.py:241
  129.3 25.2 %collective-permute-start.21 = (bf16[4,64,2048]{2,1,0:T(8,128)(2,1)}, bf16[4,64,2048]{2,1,0:T(8,128)(2,1)S(1)}, u32[]{:S(2)}, u32[]{:S(2)}) collective-permute-start(bf16[4,64,2048]{2,1,0:T(8,128)(2,1)} %collective-permute-done.13), channel_id=1, source_target_pairs={{0,16},{16,0},{1,17},{17,1},{2,18},{18,2},{3,19},{19,3},{4,20},{20... | collective-permute-start | bytes 3145736 | tf_op jit(solution)/shard_map/ppermute | solution.py:190
  130.9 7.1 %copy-start.7 = (bf16[4,64,2048]{2,1,0:T(8,128)(2,1)}, bf16[4,64,2048]{2,1,0:T(8,128)(2,1)S(1)}, u32[]{:S(2)}) copy-start(bf16[4,64,2048]{2,1,0:T(8,128)(2,1)S(1)} %collective-permute-done.17) | copy-start | bytes 3145732
  130.9 7.1 %collective-permute-start.18 = (f32[256,128]{1,0:T(8,128)S(1)}, f32[256,128]{1,0:T(8,128)S(1)}, u32[]{:S(2)}, u32[]{:S(2)}) collective-permute-start(f32[256,128]{1,0:T(8,128)S(1)} %fusion.32), channel_id=1, source_target_pairs={{1,2},{2,1},{5,6},{6,5},{9,10},{10,9},{13,14},{14,13},{17,18},{18,... | collective-permute-start | bytes 393224 | tf_op jit(solution)/shard_map/ppermute | solution.py:241
  138.1 49.0 %collective-permute-start.23 = (f16[512,2048]{1,0:T(8,128)(2,1)}, f16[512,2048]{1,0:T(8,128)(2,1)}, u32[]{:S(2)}, u32[]{:S(2)}) collective-permute-start(f16[512,2048]{1,0:T(8,128)(2,1)} %add_convert_fusion), channel_id=1, source_target_pairs={{1,2},{2,1},{5,6},{6,5},{9,10},{10,9},{13,14},{14,13},{17,18},{18,... | collective-permute-start | bytes 6291464 | tf_op jit(solution)/shard_map/ppermute | solution.py:241
  142.0 19.2 %copy-start.2 = (bf16[4,64,2048]{2,1,0:T(8,128)(2,1)S(1)}, bf16[4,64,2048]{2,1,0:T(8,128)(2,1)}, u32[]{:S(2)}) copy-start(bf16[4,64,2048]{2,1,0:T(8,128)(2,1)} %copy-done.1) | copy-start | bytes 3145732
  142.0 19.0 %collective-permute-start.20 = (f16[192,2048]{1,0:T(8,128)(2,1)}, f16[192,2048]{1,0:T(8,128)(2,1)S(1)}, u32[]{:S(2)}, u32[]{:S(2)}) collective-permute-start(f16[192,2048]{1,0:T(8,128)(2,1)} %add_convert_fusion.3), channel_id=1, source_target_pairs={{0,1},{1,0},{2,3},{3,2},{4,5},{5,4},{6,7},{7,6},{8,9},{9,8},{10,11... | collective-permute-start | bytes 2359304 | tf_op jit(solution)/shard_map/ppermute | solution.py:241
  154.6 20.0 %collective-permute-start.22 = (bf16[4,64,2048]{2,1,0:T(8,128)(2,1)S(1)}, bf16[4,64,2048]{2,1,0:T(8,128)(2,1)S(1)}, u32[]{:S(2)}, u32[]{:S(2)}) collective-permute-start(bf16[4,64,2048]{2,1,0:T(8,128)(2,1)S(1)} %collective-permute-done.21), channel_id=1, source_target_pairs={{0,4},{4,0},{8,12},{12,8},{1,5},{5,1},{9,13},{13,9},{2,6},{6,2},{1... | collective-permute-start | bytes 3145736 | tf_op jit(solution)/shard_map/ppermute | solution.py:169
  154.6 6.2 %collective-permute-start.19 = (bf16[256,128]{1,0:T(8,128)(2,1)S(1)}, bf16[256,128]{1,0:T(8,128)(2,1)S(1)}, u32[]{:S(2)}, u32[]{:S(2)}) collective-permute-start(bf16[256,128]{1,0:T(8,128)(2,1)S(1)} %add.235), channel_id=1, source_target_pairs={{1,0},{2,3},{5,4},{6,7},{9,8},{10,11},{13,12},{14,15},{17,16},{18,... | collective-permute-start | bytes 196616 | tf_op jit(solution)/shard_map/ppermute | solution.py:241
  160.7 31.0 %collective-permute-start.24 = (f16[320,2048]{1,0:T(8,128)(2,1)S(1)}, f16[320,2048]{1,0:T(8,128)(2,1)S(1)}, u32[]{:S(2)}, u32[]{:S(2)}) collective-permute-start(f16[320,2048]{1,0:T(8,128)(2,1)S(1)} %add_convert_fusion.2), channel_id=1, source_target_pairs={{0,1},{1,0},{2,3},{3,2},{4,5},{5,4},{6,7},{7,6},{8,9},{9,8},{10,11... | collective-permute-start | bytes 3932168 | tf_op jit(solution)/shard_map/ppermute | solution.py:241
  187.1 4.6 %copy-start.3 = (f32[512,2048]{1,0:T(8,128)S(1)}, f32[512,2048]{1,0:T(8,128)}, u32[]{:S(2)}) copy-start(f32[512,2048]{1,0:T(8,128)} %shard_map.76) | copy-start | bytes 12582916
  189.5 2.2 %copy-start.6 = (bf16[512,2048]{1,0:T(8,128)(2,1)}, bf16[512,2048]{1,0:T(8,128)(2,1)S(1)}, u32[]{:S(2)}) copy-start(bf16[512,2048]{1,0:T(8,128)(2,1)S(1)} %fusion.20) | copy-start | bytes 6291460

commit v3 on v2

--- a/solution.py
+++ b/solution.py
@@ -243,7 +243,7 @@
     def part_of(block, span):
         return lax.slice_in_dim(block, span[0], span[0] + span[1])
 
-    spans = [(0, rows * 3 // 8), (rows * 3 // 8, rows * 5 // 8)]
+    spans = [(0, rows // 4), (rows // 4, rows * 3 // 4)]
     d0, d0_ids = cross(down_stack, 1, 0)
     up_other = to_sibling(up_stack)
     first = wire(product(targets[0], tokens))
@@ -260,37 +260,41 @@
     [(d2, d2_ids)] = turn(d0, 1, 0)
     third = wire(product(targets[2], after(later, d0)))
     g_both = jnp.concatenate([g, g_other])[:, None]
-    first, second, third, a1, tokens, tokens_other = lax.optimization_barrier(
-        (first, second, third, a1, tokens, tokens_other)
+    first, second, third, a1, tokens, tokens_other, d1, d2 = lax.optimization_barrier(
+        (first, second, third, a1, tokens, tokens_other, d1, d2)
     )
-
-    d1 = after(d1, a1)
 
     a2 = hop(second, outer)
     b1 = hop(wire(unwire(first) + unwire(a1)), inner)
     [(d3, d3_ids)] = turn(d1, 1, 1)
     u0, u0_ids = cross(up, 1, 0, d1)
+    halves = shrink_by(tokens, tokens_other, g_both, [(down_stack, mine)])
+    u0 = after(u0, halves)
     u1, u1_ids = cross(up, 1, 1, u0)
-    halves = shrink_by(after(tokens, d2), tokens_other, g_both, [(down_stack, mine)])
     home = product(z, tokens) * (1.0 / BASE_WIRE)
     later = after(tokens, home)
     halves += shrink_by(later, tokens_other, g_both, [(d0, d0_ids), (d1, d1_ids), (d2, d2_ids), (d3, d3_ids)])
     part = joined(halves)
     [(u2, u2_ids)] = turn(u0, 1, 0)
-    ups = [(up, mine), (up_other, slots(me ^ 1, 0, own)), *shared([(u0, u0_ids), (u1, u1_ids), (u2, u2_ids)])]
-    late = turn(u1, 1, 1)
+    ups = [(up, mine), (up_other, slots(me ^ 1, 0, own)), *shared([(u0, u0_ids)])]
     part += hop(after(part, a2), both)
     c1 = [wire(unwire(part_of(third, span)) + unwire(part_of(b1, span))) for span in spans]
     b2 = wire(unwire(second) + unwire(a2))
-    part, c1[0], home, *seen = lax.optimization_barrier((part, c1[0], home, *[block for block, _ in ups]))
+    part, c1[0], b2, home, u2, *seen = lax.optimization_barrier(
+        (part, c1[0], b2, home, u2, *[block for block, _ in ups])
+    )
     ups = [(block, ids) for block, (_, ids) in zip(seen, ups)]
 
     a3 = [hop(block, both) for block in c1]
     part += hop(part, inner)
     b2 = hop(after(b2, part), inner)
+    u1 = after(u1, part)
+    late = turn(u1, 1, 1)
     low = part.astype(jnp.bfloat16)
     low = jnp.where((z == 1) | (z == 2), low, hop(low, [(1, 0), (2, 3)]))
-    adapted = update(home, after(low, a3[0]), ups)
+    u1, u2, low = lax.optimization_barrier((u1, u2, low, a3[0]))[:3]
+    ups += shared([(u1, u1_ids), (u2, u2_ids)])
+    adapted = update(home, low, ups)
     adapted = update(adapted, low, shared(late))
     out = jnp.zeros((rows, width), jnp.bfloat16)
     for arrived, span in zip(a3, spans):

time: 197 us -> 192 us (0.975); the launches traced: 195 us -> 192 us
  starting transfers between devices: 29.7 us -> 23.8 us
  local copies, waits for them, and re-layouts: 6.61 us -> 9.69 us
    ppermute x9, waiting for transfers between devices: 24 us -> 42 us  [hop(): return lax.ppermute(block, 'tensor', pairs)]
    ppermute x4, waiting for transfers between devices: 25.8 us -> 10.3 us  [cross(): lax.ppermute(after(block, *gates), 'dp', [(i, (i + shift * CORES) % owner...]
    ppermute x9, starting transfers between devices: 18 us -> 15.1 us  [hop(): return lax.ppermute(block, 'tensor', pairs)]
    unnamed x18 -> x24, local copies, waits for them, and re-layouts: 0.04 us -> 2.15 us
    ppermute x4, starting transfers between devices: 6.21 us -> 4.19 us  [turn(): lax.ppermute(block, 'groups', [(i, (i + step) % groups) for i in range(gr...]
  transfers between devices with their start and end apart: 25 -> 25, of which waited for: 8 -> 11; matrix products, arithmetic and copies ran while one was open for 31% -> 31% of each run, Pallas kernels for 19% -> 19%
where the time goes in v3:
time: 192 us
  waiting for transfers between devices  64.1 us (33%)
  matrix products  38.1 us (20%)
  Pallas kernels  36.5 us (19%)
  starting transfers between devices  23.8 us (12%)
  other arithmetic  18.6 us (10%)
  local copies, waits for them, and re-layouts  9.69 us (5%)
    ppermute x9, waiting for transfers between devices, hop(): return lax.ppermute(block, 'tensor', pairs)  42 us
    dot_general x4, matrix products, product(): jnp.dot(rows_of, block, preferred_element_type=jnp.float32)  38.1 us
    pallas_call x2, Pallas kernels, expand(): pl.pallas_call(functools.partial(expand_kernel, rank), out_shape=jax.Shap...  19.9 us
    pallas_call x2, Pallas kernels, shrink(): pl.pallas_call(functools.partial(shrink_kernel, rank, steps), out_shape=j...  16.6 us
    ppermute x9, starting transfers between devices, hop(): return lax.ppermute(block, 'tensor', pairs)  15.1 us
    convert_element_type x4, other arithmetic, wire(): return total.astype(jnp.float16)  11.4 us
    ppermute x4, waiting for transfers between devices, turn(): lax.ppermute(block, 'groups', [(i, (i + step) % groups) for i in range(gr...  11 us
    ppermute x4, waiting for transfers between devices, cross(): lax.ppermute(after(block, *gates), 'dp', [(i, (i + shift * CORES) % owner...  10.3 us
  transfers between devices with their start and end apart: 25, of which 11 were waited for; matrix products, arithmetic and copies ran while one was open for 31% of the time, Pallas kernels for 19%

profile of v3, /device:TPU:10, one launch (start us, length us, event | category | flops | bytes accessed | tf_op | source)
XLA Modules:
  0.0 191.8 jit_solution(2927057523090641411)
XLA Ops:
  0.0 0.1 add.208
  0.1 0.1 add.209
  0.2 0.8 squeeze.4
  0.9 0.8 select_reduce_fusion
  1.7 10.0 %fusion.15 = f16[512,2048]{1,0:T(8,128)(2,1)} fusion(bf16[512,2048]{1,0:T(8,128)(2,1)} %mine_ref.1, bf16[2048,8192]{1,0:T(8,128)(2,1)} %param.8, s32[]{:T(128)S(6)} %select_n.93), kind=kOutput, calls=%fused_computation.16 | convolution fusion | flops 4297064448 | bytes 12582916 | tf_op jit(solution)/shard_map/dot_general | solution.py:201
  11.7 0.5 collective-permute-start.2
  12.2 1.3 constant_dynamic-slice_fusion.1
  13.5 0.6 collective-permute-start.3
  14.1 0.6 dynamic_slice.32
  15.5 0.1 pad_add_fusion.2.ids_ref
  15.6 1.3 collective-permute-start.4
  16.9 2.3 %constant_dynamic-slice_fusion = bf16[4,64,2048]{2,1,0:T(8,128)(2,1)} fusion(bf16[16,64,2048]{2,1,0:T(8,128)(2,1)} %param.9, s32[]{:T(128)S(6)} %select_n.95), kind=kLoop, calls=%fused_computation.31 | loop fusion | bytes 2097156 | tf_op jit(solution)/shard_map/dynamic_slice | solution.py:183
  19.2 9.3 %multiply_convert_fusion.1 = f16[512,2048]{1,0:T(8,128)(2,1)} fusion(bf16[512,2048]{1,0:T(8,128)(2,1)S(1)} %copy-done, bf16[2048,8192]{1,0:T(8,128)(2,1)} %param.8, s32[]{:T(128)S(6)} %select_n.98), kind=kOutput, calls=%fused_computation.11 | convolution fusion | flops 4297064448 | bytes 12582916 | tf_op jit(solution)/shard_map/dot_general | solution.py:201
  28.5 10.3 %collective-permute-done.3 = bf16[4,64,2048]{2,1,0:T(8,128)(2,1)} collective-permute-done((bf16[4,64,2048]{2,1,0:T(8,128)(2,1)S(1)}, bf16[4,64,2048]{2,1,0:T(8,128)(2,1)}, u32[]{:S(2)}, u32[]{:S(2)}) %collective-permute-start.3) | collective-permute-done | bytes 1048608 | tf_op jit(solution)/shard_map/ppermute | solution.py:184
  38.8 1.5 collective-permute-start.6
  40.3 0.5 collective-permute-start.5
  40.8 1.6 constant_dynamic-slice_fusion.3
  42.4 0.2 copy.15.g_ref
  42.7 9.3 %multiply_convert_fusion = f16[512,2048]{1,0:T(8,128)(2,1)} fusion(bf16[512,2048]{1,0:T(8,128)(2,1)S(1)} %copy-done, bf16[2048,8192]{1,0:T(8,128)(2,1)} %param.8, s32[]{:T(128)S(6)} %select_n.100), kind=kOutput, calls=%fused_computation.10 | convolution fusion | flops 4297064448 | bytes 12582916 | tf_op jit(solution)/shard_map/dot_general | solution.py:201
  51.9 13.8 %collective-permute-done.4 = f16[512,2048]{1,0:T(8,128)(2,1)} collective-permute-done((f16[512,2048]{1,0:T(8,128)(2,1)}, f16[512,2048]{1,0:T(8,128)(2,1)}, u32[]{:S(2)}, u32[]{:S(2)}) %collective-permute-start.4) | collective-permute-done | bytes 2097184 | tf_op jit(solution)/shard_map/ppermute | solution.py:241
  65.8 1.5 collective-permute-start.9
  67.3 1.3 collective-permute-start.11
  68.6 2.8 %add_convert_fusion.1 = f16[512,2048]{1,0:T(8,128)(2,1)S(1)} fusion(f16[512,2048]{1,0:T(8,128)(2,1)} %collective-permute-done.4, f16[512,2048]{1,0:T(8,128)(2,1)S(1)} %copy-done.5), kind=kLoop, calls=%fused_computation.9 | loop fusion | flops 4194304 | bytes 6291456 | tf_op jit(solution)/shard_map/convert_element_type | solution.py:125
  71.4 3.7 %collective-permute-start.13 = (f16[512,2048]{1,0:T(8,128)(2,1)S(1)}, f16[512,2048]{1,0:T(8,128)(2,1)}, u32[]{:S(2)}, u32[]{:S(2)}) collective-permute-start(f16[512,2048]{1,0:T(8,128)(2,1)S(1)} %add_convert_fusion.1), channel_id=1, source_target_pairs={{1,2},{2,1},{5,6},{6,5},{9,10},{10,9},{13,14},{14,13},{17,18},{18,... | collective-permute-start | bytes 6291464 | tf_op jit(solution)/shard_map/ppermute | solution.py:241
  75.1 1.6 collective-permute-start.7
  76.6 8.3 %shard_map.73 = f32[1024,128]{1,0:T(8,128)S(1)} custom-call(s32[16]{0:T(128)S(1)} %iota_add_fusion.4.ids_ref, s32[1024,1]{1,0:T(8,128)S(1)} %copy.15.g_ref, bf16[512,2048]{1,0:T(8,128)(2,1)S(1)} %copy-done, bf16[512,2048]{1,0:T(8,128)(2,1)} %collective-permute-done.2.other_ref, bf16[1024,2048]{1,0:T(8,128)(2,1)} %bitcast.29), custom_call_target="tpu_custom_call" | custom-call | flops 1 | bytes 1 | tf_op jit(solution)/shard_map/pallas_call | solution.py:54
  84.9 9.5 %fusion.base_ref = f32[512,2048]{1,0:T(8,128)} fusion(bf16[512,2048]{1,0:T(8,128)(2,1)S(1)} %copy-done, bf16[2048,8192]{1,0:T(8,128)(2,1)} %param.8, s32[]{:T(128)S(6)} %select_n.101), kind=kOutput, calls=%fused_computation | convolution fusion | flops 4294967296 | bytes 14680068 | tf_op jit(solution)/shard_map/dot_general | solution.py:201
  94.4 8.3 %shard_map.74 = f32[1024,128]{1,0:T(8,128)S(1)} custom-call(s32[16]{0:T(128)S(1)} %pad_add_fusion.2.ids_ref, s32[1024,1]{1,0:T(8,128)S(1)} %copy.15.g_ref, bf16[512,2048]{1,0:T(8,128)(2,1)} %mine_ref.1, bf16[512,2048]{1,0:T(8,128)(2,1)} %collective-permute-done.2.other_ref, bf16[256,2048]{1,0:T(8,128)(2,1)} %bitcast.5.refs_0_, ...), custom_call_target="tpu_custom_call" | custom-call | flops 1 | bytes 1 | tf_op jit(solution)/shard_map/pallas_call | solution.py:54
  102.8 0.2 slice_add_fusion.2
  103.1 0.1 collective-permute-start.10
  103.2 0.6 collective-permute-start.14
  103.7 0.2 collective-permute-start.15
  103.9 0.8 collective-permute-done.10
  104.7 0.5 collective-permute-start.8
  105.3 0.1 pad_maximum_fusion
  105.4 10.8 %collective-permute-done.11 = f16[512,2048]{1,0:T(8,128)(2,1)S(1)} collective-permute-done((f16[512,2048]{1,0:T(8,128)(2,1)S(1)}, f16[512,2048]{1,0:T(8,128)(2,1)S(1)}, u32[]{:S(2)}, u32[]{:S(2)}) %collective-permute-start.11) | collective-permute-done | bytes 2097184 | tf_op jit(solution)/shard_map/ppermute | solution.py:241
  116.2 2.5 %add_convert_fusion = f16[512,2048]{1,0:T(8,128)(2,1)} fusion(f16[512,2048]{1,0:T(8,128)(2,1)S(1)} %collective-permute-done.11, f16[512,2048]{1,0:T(8,128)(2,1)S(1)} %copy-done.6), kind=kLoop, calls=%fused_computation.8 | loop fusion | flops 4194304 | bytes 6291456 | tf_op jit(solution)/shard_map/convert_element_type | solution.py:125
  118.7 1.7 collective-permute-done.13
  120.4 2.1 %add_convert_fusion.3 = f16[128,2048]{1,0:T(8,128)(2,1)} fusion(f16[512,2048]{1,0:T(8,128)(2,1)} %collective-permute-done.13, f16[512,2048]{1,0:T(8,128)(2,1)} %multiply_convert_fusion), kind=kLoop, calls=%fused_computation.20 | loop fusion | flops 1048576 | bytes 1572864 | tf_op jit(solution)/shard_map/convert_element_type | solution.py:125
  122.5 0.1 fusion.31
  122.6 6.1 %collective-permute-done.14 = bf16[4,64,2048]{2,1,0:T(8,128)(2,1)S(1)} collective-permute-done((bf16[4,64,2048]{2,1,0:T(8,128)(2,1)S(1)}, bf16[4,64,2048]{2,1,0:T(8,128)(2,1)S(1)}, u32[]{:S(2)}, u32[]{:S(2)}) %collective-permute-start.14) | collective-permute-done | bytes 1048608 | tf_op jit(solution)/shard_map/ppermute | solution.py:190
  128.7 2.3 %collective-permute-start.16 = (f32[256,128]{1,0:T(8,128)S(1)}, f32[256,128]{1,0:T(8,128)S(1)}, u32[]{:S(2)}, u32[]{:S(2)}) collective-permute-start(f32[256,128]{1,0:T(8,128)S(1)} %fusion.31), channel_id=1, source_target_pairs={{1,2},{2,1},{5,6},{6,5},{9,10},{10,9},{13,14},{14,13},{17,18},{18,... | collective-permute-start | bytes 393224 | tf_op jit(solution)/shard_map/ppermute | solution.py:241
  131.1 4.7 %collective-permute-done.16 = f32[256,128]{1,0:T(8,128)S(1)} collective-permute-done((f32[256,128]{1,0:T(8,128)S(1)}, f32[256,128]{1,0:T(8,128)S(1)}, u32[]{:S(2)}, u32[]{:S(2)}) %collective-permute-start.16) | collective-permute-done | bytes 131104 | tf_op jit(solution)/shard_map/ppermute | solution.py:241
  135.8 0.6 collective-permute-start.21
  136.4 2.3 %collective-permute-start.23 = (f16[512,2048]{1,0:T(8,128)(2,1)}, f16[512,2048]{1,0:T(8,128)(2,1)}, u32[]{:S(2)}, u32[]{:S(2)}) collective-permute-start(f16[512,2048]{1,0:T(8,128)(2,1)} %add_convert_fusion), channel_id=1, source_target_pairs={{1,2},{2,1},{5,6},{6,5},{9,10},{10,9},{13,14},{14,13},{17,18},{18,... | collective-permute-start | bytes 6291464 | tf_op jit(solution)/shard_map/ppermute | solution.py:241
  138.8 4.1 %collective-permute-start.17 = (bf16[256,128]{1,0:T(8,128)(2,1)S(1)}, bf16[256,128]{1,0:T(8,128)(2,1)S(1)}, u32[]{:S(2)}, u32[]{:S(2)}) collective-permute-start(bf16[256,128]{1,0:T(8,128)(2,1)S(1)} %add.236), channel_id=1, source_target_pairs={{1,0},{2,3},{5,4},{6,7},{9,8},{10,11},{13,12},{14,15},{17,16},{18,... | collective-permute-start | bytes 196616 | tf_op jit(solution)/shard_map/ppermute | solution.py:241
  142.9 3.9 %add_convert_fusion.2 = f16[384,2048]{1,0:T(8,128)(2,1)} fusion(f16[512,2048]{1,0:T(8,128)(2,1)} %collective-permute-done.13, f16[512,2048]{1,0:T(8,128)(2,1)} %multiply_convert_fusion), kind=kLoop, calls=%fused_computation.15 | loop fusion | flops 3145728 | bytes 4718592 | tf_op jit(solution)/shard_map/convert_element_type | solution.py:125
  146.9 5.9 %collective-permute-done.17 = bf16[256,128]{1,0:T(8,128)(2,1)S(1)} collective-permute-done((bf16[256,128]{1,0:T(8,128)(2,1)S(1)}, bf16[256,128]{1,0:T(8,128)(2,1)S(1)}, u32[]{:S(2)}, u32[]{:S(2)}) %collective-permute-start.17) | collective-permute-done | bytes 65568 | tf_op jit(solution)/shard_map/ppermute | solution.py:241
  152.8 1.1 collective-permute-done.18
  153.9 0.8 copy-done.9
  154.7 0.5 collective-permute-start.20
  155.2 4.9 %collective-permute-done.21 = bf16[4,64,2048]{2,1,0:T(8,128)(2,1)} collective-permute-done((bf16[4,64,2048]{2,1,0:T(8,128)(2,1)}, bf16[4,64,2048]{2,1,0:T(8,128)(2,1)}, u32[]{:S(2)}, u32[]{:S(2)}) %collective-permute-start.21) | collective-permute-done | bytes 1048608 | tf_op jit(solution)/shard_map/ppermute | solution.py:190
  160.1 0.1 concatenate.29.ids_ref
  160.2 0.1 pad_add_fusion.1.ids_ref
  160.3 0.1 copy.18.g_ref
  160.4 0.1 fusion.26
  160.5 0.1 maximum_maximum_fusion.low_ref
  160.7 13.3 %shard_map.75.base_ref = f32[512,2048]{1,0:T(8,128)} custom-call(s32[56]{0:T(128)S(1)} %concatenate.29.ids_ref, s32[512,1]{1,0:T(8,128)S(1)} %copy.18.g_ref, bf16[512,128]{1,0:T(8,128)(2,1)S(1)} %maximum_maximum_fusion.low_ref, f32[512,2048]{1,0:T(8,128)} %fusion.base_ref, bf16[1024,2048]{1,0:T(8,128)(2,1)} %bitcast.28, bf16[1024,2048]{1,0:T(8,128)(2,1)} %bitcast.10.refs_1_, ...), custom_call_target="tpu_custom_call" | custom-call | flops 1 | bytes 1 | tf_op jit(solution)/shard_map/pallas_call | solution.py:100
  174.0 6.6 %shard_map.76 = f32[512,2048]{1,0:T(8,128)} custom-call(s32[8]{0:T(128)S(1)} %pad_add_fusion.1.ids_ref, s32[512,1]{1,0:T(8,128)S(1)} %copy.18.g_ref, bf16[512,128]{1,0:T(8,128)(2,1)S(1)} %maximum_maximum_fusion.low_ref, f32[512,2048]{1,0:T(8,128)} %shard_map.75.base_ref, bf16[256,2048]{1,0:T(8,128)(2,1)} %bitcast.17.refs_0_, bf16[256,2048]{1,0:T(8,128)(2,1)} %bitcast.18.refs_1_), custom_call_target="tpu_custom_call" | custom-call | flops 1 | bytes 1 | tf_op jit(solution)/shard_map/pallas_call | solution.py:100
  180.6 4.0 %collective-permute-done.23 = f16[512,2048]{1,0:T(8,128)(2,1)} collective-permute-done((f16[512,2048]{1,0:T(8,128)(2,1)}, f16[512,2048]{1,0:T(8,128)(2,1)}, u32[]{:S(2)}, u32[]{:S(2)}) %collective-permute-start.23) | collective-permute-done | bytes 2097184 | tf_op jit(solution)/shard_map/ppermute | solution.py:241
  184.7 0.2 broadcast_in_dim.25
  184.9 1.6 fusion.20
  186.5 1.3 copy-done.7
  187.8 4.0 %fusion.18 = bf16[512,2048]{1,0:T(8,128)(2,1)} fusion(bf16[512,2048]{1,0:T(8,128)(2,1)} %copy-done.7, f16[384,2048]{1,0:T(8,128)(2,1)} %collective-permute-done.24, f32[512,2048]{1,0:T(8,128)S(1)} %copy-done.3, f16[512,2048]{1,0:T(8,128)(2,1)} %collective-permute-done.23), kind=kLoop, calls=%fused_computation.17 | loop fusion | flops 4718592 | bytes 7864320 | tf_op jit(solution)/shard_map/dynamic_update_slice | solution.py:303
  (60 shorter events, 0.4 us)
Async XLA Ops:
  0.0 11.7 %collective-permute-start = (bf16[16,64,2048]{2,1,0:T(8,128)(2,1)}, bf16[16,64,2048]{2,1,0:T(8,128)(2,1)}, u32[]{:S(2)}, u32[]{:S(2)}) collective-permute-start(bf16[16,64,2048]{2,1,0:T(8,128)(2,1)} %param.10), channel_id=1, source_target_pairs={{0,4},{4,0},{8,12},{12,8},{1,5},{5,1},{9,13},{13,9},{2,6},{6,2},{1... | collective-permute-start | bytes 12582920 | tf_op jit(solution)/shard_map/ppermute | solution.py:169
  1.7 10.0 %copy-start = (bf16[512,2048]{1,0:T(8,128)(2,1)S(1)}, bf16[512,2048]{1,0:T(8,128)(2,1)}, u32[]{:S(2)}) copy-start(bf16[512,2048]{1,0:T(8,128)(2,1)} %mine_ref.1) | copy-start | bytes 6291460
  1.7 12.4 %copy-start.11 = (s32[4]{0:T(128)S(1)}, s32[4]{0:T(128)}, u32[]{:S(2)}) copy-start(s32[4]{0:T(128)} %constant.101.clone) | copy-start | bytes 52
  11.7 7.5 %collective-permute-start.2 = (bf16[512,2048]{1,0:T(8,128)(2,1)S(1)}, bf16[512,2048]{1,0:T(8,128)(2,1)}, u32[]{:S(2)}, u32[]{:S(2)}) collective-permute-start(bf16[512,2048]{1,0:T(8,128)(2,1)S(1)} %copy-done), channel_id=1, source_target_pairs={{0,4},{4,0},{8,12},{12,8},{1,5},{5,1},{9,13},{13,9},{2,6},{6,2},{1... | collective-permute-start | bytes 6291464 | tf_op jit(solution)/shard_map/ppermute | solution.py:169
  13.5 25.3 %collective-permute-start.3 = (bf16[4,64,2048]{2,1,0:T(8,128)(2,1)S(1)}, bf16[4,64,2048]{2,1,0:T(8,128)(2,1)}, u32[]{:S(2)}, u32[]{:S(2)}) collective-permute-start(bf16[4,64,2048]{2,1,0:T(8,128)(2,1)S(1)} %constant_dynamic-slice_fusion.1), channel_id=1, source_target_pairs={{0,8},{4,12},{8,0},{12,4},{1,9},{5,13},{9,1},{13,5},{2,10},{6,14},... | collective-permute-start | bytes 3145736 | tf_op jit(solution)/shard_map/ppermute | solution.py:184
  15.5 3.6 %collective-permute-start.1 = (s32[512]{0:T(512)S(1)}, s32[512]{0:T(512)S(1)}, u32[]{:S(2)}, u32[]{:S(2)}) collective-permute-start(s32[512]{0:T(512)S(1)} %select_reduce_fusion), channel_id=1, source_target_pairs={{0,4},{4,0},{8,12},{12,8},{1,5},{5,1},{9,13},{13,9},{2,6},{6,2},{1... | collective-permute-start | bytes 6152 | tf_op jit(solution)/shard_map/ppermute | solution.py:169
  15.6 50.2 %collective-permute-start.4 = (f16[512,2048]{1,0:T(8,128)(2,1)}, f16[512,2048]{1,0:T(8,128)(2,1)}, u32[]{:S(2)}, u32[]{:S(2)}) collective-permute-start(f16[512,2048]{1,0:T(8,128)(2,1)} %fusion.15), channel_id=1, source_target_pairs={{0,1},{3,2},{4,5},{7,6},{8,9},{11,10},{12,13},{15,14},{16,17},{19,... | collective-permute-start | bytes 6291464 | tf_op jit(solution)/shard_map/ppermute | solution.py:241
  19.2 21.7 %copy-start.4 = (bf16[16,64,2048]{2,1,0:T(8,128)(2,1)S(1)}, bf16[16,64,2048]{2,1,0:T(8,128)(2,1)}, u32[]{:S(2)}) copy-start(bf16[16,64,2048]{2,1,0:T(8,128)(2,1)} %param.10) | copy-start | bytes 12582916
  38.8 27.0 %collective-permute-start.6 = (bf16[4,64,2048]{2,1,0:T(8,128)(2,1)}, bf16[4,64,2048]{2,1,0:T(8,128)(2,1)}, u32[]{:S(2)}, u32[]{:S(2)}) collective-permute-start(bf16[4,64,2048]{2,1,0:T(8,128)(2,1)} %collective-permute-done.3), channel_id=1, source_target_pairs={{0,16},{16,0},{1,17},{17,1},{2,18},{18,2},{3,19},{19,3},{4,20},{20... | collective-permute-start | bytes 3145736 | tf_op jit(solution)/shard_map/ppermute | solution.py:190
  40.3 25.5 %collective-permute-start.5 = (bf16[4,64,2048]{2,1,0:T(8,128)(2,1)}, bf16[4,64,2048]{2,1,0:T(8,128)(2,1)}, u32[]{:S(2)}, u32[]{:S(2)}) collective-permute-start(bf16[4,64,2048]{2,1,0:T(8,128)(2,1)} %constant_dynamic-slice_fusion), channel_id=1, source_target_pairs={{0,8},{4,12},{8,0},{12,4},{1,9},{5,13},{9,1},{13,5},{2,10},{6,14},... | collective-permute-start | bytes 3145736 | tf_op jit(solution)/shard_map/ppermute | solution.py:184
  42.6 24.7 %copy-start.6 = (f16[512,2048]{1,0:T(8,128)(2,1)S(1)}, f16[512,2048]{1,0:T(8,128)(2,1)}, u32[]{:S(2)}) copy-start(f16[512,2048]{1,0:T(8,128)(2,1)} %multiply_convert_fusion.1) | copy-start | bytes 6291460
  42.7 25.9 %copy-start.5 = (f16[512,2048]{1,0:T(8,128)(2,1)S(1)}, f16[512,2048]{1,0:T(8,128)(2,1)}, u32[]{:S(2)}) copy-start(f16[512,2048]{1,0:T(8,128)(2,1)} %fusion.15) | copy-start | bytes 6291460
  65.8 28.6 %collective-permute-start.9 = (bf16[4,64,2048]{2,1,0:T(8,128)(2,1)}, bf16[4,64,2048]{2,1,0:T(8,128)(2,1)S(1)}, u32[]{:S(2)}, u32[]{:S(2)}) collective-permute-start(bf16[4,64,2048]{2,1,0:T(8,128)(2,1)} %collective-permute-done.5), channel_id=1, source_target_pairs={{0,16},{16,0},{1,17},{17,1},{2,18},{18,2},{3,19},{19,3},{4,20},{20... | collective-permute-start | bytes 3145736 | tf_op jit(solution)/shard_map/ppermute | solution.py:190
  67.3 48.8 %collective-permute-start.11 = (f16[512,2048]{1,0:T(8,128)(2,1)S(1)}, f16[512,2048]{1,0:T(8,128)(2,1)S(1)}, u32[]{:S(2)}, u32[]{:S(2)}) collective-permute-start(f16[512,2048]{1,0:T(8,128)(2,1)S(1)} %copy-done.6), channel_id=1, source_target_pairs={{0,1},{3,2},{4,5},{7,6},{8,9},{11,10},{12,13},{15,14},{16,17},{19,... | collective-permute-start | bytes 6291464 | tf_op jit(solution)/shard_map/ppermute | solution.py:241
  71.4 49.0 %collective-permute-start.13 = (f16[512,2048]{1,0:T(8,128)(2,1)S(1)}, f16[512,2048]{1,0:T(8,128)(2,1)}, u32[]{:S(2)}, u32[]{:S(2)}) collective-permute-start(f16[512,2048]{1,0:T(8,128)(2,1)S(1)} %add_convert_fusion.1), channel_id=1, source_target_pairs={{1,2},{2,1},{5,6},{6,5},{9,10},{10,9},{13,14},{14,13},{17,18},{18,... | collective-permute-start | bytes 6291464 | tf_op jit(solution)/shard_map/ppermute | solution.py:241
  75.1 28.1 %collective-permute-start.7 = (bf16[4,64,2048]{2,1,0:T(8,128)(2,1)}, bf16[4,64,2048]{2,1,0:T(8,128)(2,1)S(1)}, u32[]{:S(2)}, u32[]{:S(2)}) collective-permute-start(bf16[4,64,2048]{2,1,0:T(8,128)(2,1)} %get-tuple-element.52), channel_id=1, source_target_pairs={{0,8},{4,12},{8,0},{12,4},{1,9},{5,13},{9,1},{13,5},{2,10},{6,14},... | collective-permute-start | bytes 3145736 | tf_op jit(solution)/shard_map/ppermute | solution.py:184
  102.8 1.9 copy-start.8
  103.1 1.6 collective-permute-start.10
  103.2 15.5 %copy-start.1 = (bf16[4,64,2048]{2,1,0:T(8,128)(2,1)}, bf16[4,64,2048]{2,1,0:T(8,128)(2,1)S(1)}, u32[]{:S(2)}) copy-start(bf16[4,64,2048]{2,1,0:T(8,128)(2,1)S(1)} %collective-permute-done.7) | copy-start | bytes 3145732
  103.2 25.6 %collective-permute-start.14 = (bf16[4,64,2048]{2,1,0:T(8,128)(2,1)S(1)}, bf16[4,64,2048]{2,1,0:T(8,128)(2,1)S(1)}, u32[]{:S(2)}, u32[]{:S(2)}) collective-permute-start(bf16[4,64,2048]{2,1,0:T(8,128)(2,1)S(1)} %collective-permute-done.7), channel_id=1, source_target_pairs={{0,16},{16,0},{1,17},{17,1},{2,18},{18,2},{3,19},{19,3},{4,20},{20... | collective-permute-start | bytes 3145736 | tf_op jit(solution)/shard_map/ppermute | solution.py:190
  103.7 25.0 %collective-permute-start.15 = (bf16[4,64,2048]{2,1,0:T(8,128)(2,1)S(1)}, bf16[4,64,2048]{2,1,0:T(8,128)(2,1)S(1)}, u32[]{:S(2)}, u32[]{:S(2)}) collective-permute-start(bf16[4,64,2048]{2,1,0:T(8,128)(2,1)S(1)} %collective-permute-done.7), channel_id=1, source_target_pairs={{0,4},{4,0},{8,12},{12,8},{1,5},{5,1},{9,13},{13,9},{2,6},{6,2},{1... | collective-permute-start | bytes 3145736 | tf_op jit(solution)/shard_map/ppermute | solution.py:169
  104.7 31.1 %collective-permute-start.8 = (bf16[4,64,2048]{2,1,0:T(8,128)(2,1)S(1)}, bf16[4,64,2048]{2,1,0:T(8,128)(2,1)}, u32[]{:S(2)}, u32[]{:S(2)}) collective-permute-start(bf16[4,64,2048]{2,1,0:T(8,128)(2,1)S(1)} %copy-done.8), channel_id=1, source_target_pairs={{0,8},{4,12},{8,0},{12,4},{1,9},{5,13},{9,1},{13,5},{2,10},{6,14},... | collective-permute-start | bytes 3145736 | tf_op jit(solution)/shard_map/ppermute | solution.py:184
  116.2 6.4 %collective-permute-start.12 = (f32[256,128]{1,0:T(8,128)S(1)}, f32[256,128]{1,0:T(8,128)S(1)}, u32[]{:S(2)}, u32[]{:S(2)}) collective-permute-start(f32[256,128]{1,0:T(8,128)S(1)} %pad_maximum_fusion), channel_id=1, source_target_pairs={{0,1},{1,0},{2,3},{3,2},{4,5},{5,4},{6,7},{7,6},{8,9},{9,8},{10,11... | collective-permute-start | bytes 393224 | tf_op jit(solution)/shard_map/ppermute | solution.py:241
  122.6 38.1 %copy-start.2 = (bf16[4,64,2048]{2,1,0:T(8,128)(2,1)S(1)}, bf16[4,64,2048]{2,1,0:T(8,128)(2,1)}, u32[]{:S(2)}) copy-start(bf16[4,64,2048]{2,1,0:T(8,128)(2,1)} %copy-done.1) | copy-start | bytes 3145732
  128.7 7.0 %collective-permute-start.16 = (f32[256,128]{1,0:T(8,128)S(1)}, f32[256,128]{1,0:T(8,128)S(1)}, u32[]{:S(2)}, u32[]{:S(2)}) collective-permute-start(f32[256,128]{1,0:T(8,128)S(1)} %fusion.31), channel_id=1, source_target_pairs={{1,2},{2,1},{5,6},{6,5},{9,10},{10,9},{13,14},{14,13},{17,18},{18,... | collective-permute-start | bytes 393224 | tf_op jit(solution)/shard_map/ppermute | solution.py:241
  135.8 24.3 %collective-permute-start.21 = (bf16[4,64,2048]{2,1,0:T(8,128)(2,1)}, bf16[4,64,2048]{2,1,0:T(8,128)(2,1)}, u32[]{:S(2)}, u32[]{:S(2)}) collective-permute-start(bf16[4,64,2048]{2,1,0:T(8,128)(2,1)} %collective-permute-done.8), channel_id=1, source_target_pairs={{0,16},{16,0},{1,17},{17,1},{2,18},{18,2},{3,19},{19,3},{4,20},{20... | collective-permute-start | bytes 3145736 | tf_op jit(solution)/shard_map/ppermute | solution.py:190
  136.4 48.3 %collective-permute-start.23 = (f16[512,2048]{1,0:T(8,128)(2,1)}, f16[512,2048]{1,0:T(8,128)(2,1)}, u32[]{:S(2)}, u32[]{:S(2)}) collective-permute-start(f16[512,2048]{1,0:T(8,128)(2,1)} %add_convert_fusion), channel_id=1, source_target_pairs={{1,2},{2,1},{5,6},{6,5},{9,10},{10,9},{13,14},{14,13},{17,18},{18,... | collective-permute-start | bytes 6291464 | tf_op jit(solution)/shard_map/ppermute | solution.py:241
  138.7 15.1 %collective-permute-start.18 = (f16[128,2048]{1,0:T(8,128)(2,1)}, f16[128,2048]{1,0:T(8,128)(2,1)S(1)}, u32[]{:S(2)}, u32[]{:S(2)}) collective-permute-start(f16[128,2048]{1,0:T(8,128)(2,1)} %add_convert_fusion.3), channel_id=1, source_target_pairs={{0,1},{1,0},{2,3},{3,2},{4,5},{5,4},{6,7},{7,6},{8,9},{9,8},{10,11... | collective-permute-start | bytes 1572872 | tf_op jit(solution)/shard_map/ppermute | solution.py:241
  138.8 14.0 %collective-permute-start.17 = (bf16[256,128]{1,0:T(8,128)(2,1)S(1)}, bf16[256,128]{1,0:T(8,128)(2,1)S(1)}, u32[]{:S(2)}, u32[]{:S(2)}) collective-permute-start(bf16[256,128]{1,0:T(8,128)(2,1)S(1)} %add.236), channel_id=1, source_target_pairs={{1,0},{2,3},{5,4},{6,7},{9,8},{10,11},{13,12},{14,15},{17,16},{18,... | collective-permute-start | bytes 196616 | tf_op jit(solution)/shard_map/ppermute | solution.py:241
  146.9 39.7 %collective-permute-start.24 = (f16[384,2048]{1,0:T(8,128)(2,1)}, f16[384,2048]{1,0:T(8,128)(2,1)}, u32[]{:S(2)}, u32[]{:S(2)}) collective-permute-start(f16[384,2048]{1,0:T(8,128)(2,1)} %add_convert_fusion.2), channel_id=1, source_target_pairs={{0,1},{1,0},{2,3},{3,2},{4,5},{5,4},{6,7},{7,6},{8,9},{9,8},{10,11... | collective-permute-start | bytes 4718600 | tf_op jit(solution)/shard_map/ppermute | solution.py:241
  153.9 0.8 copy-start.9
  154.7 6.0 %collective-permute-start.19 = (bf16[4,64,2048]{2,1,0:T(8,128)(2,1)}, bf16[4,64,2048]{2,1,0:T(8,128)(2,1)}, u32[]{:S(2)}, u32[]{:S(2)}) collective-permute-start(bf16[4,64,2048]{2,1,0:T(8,128)(2,1)} %collective-permute-done.8), channel_id=1, source_target_pairs={{0,4},{4,0},{8,12},{12,8},{1,5},{5,1},{9,13},{13,9},{2,6},{6,2},{1... | collective-permute-start | bytes 3145736 | tf_op jit(solution)/shard_map/ppermute | solution.py:169
  154.7 6.0 %collective-permute-start.20 = (bf16[4,64,2048]{2,1,0:T(8,128)(2,1)S(1)}, bf16[4,64,2048]{2,1,0:T(8,128)(2,1)}, u32[]{:S(2)}, u32[]{:S(2)}) collective-permute-start(bf16[4,64,2048]{2,1,0:T(8,128)(2,1)S(1)} %collective-permute-done.14), channel_id=1, source_target_pairs={{0,4},{4,0},{8,12},{12,8},{1,5},{5,1},{9,13},{13,9},{2,6},{6,2},{1... | collective-permute-start | bytes 3145736 | tf_op jit(solution)/shard_map/ppermute | solution.py:169
  160.1 13.9 %collective-permute-start.22 = (bf16[4,64,2048]{2,1,0:T(8,128)(2,1)}, bf16[4,64,2048]{2,1,0:T(8,128)(2,1)}, u32[]{:S(2)}, u32[]{:S(2)}) collective-permute-start(bf16[4,64,2048]{2,1,0:T(8,128)(2,1)} %collective-permute-done.21), channel_id=1, source_target_pairs={{0,4},{4,0},{8,12},{12,8},{1,5},{5,1},{9,13},{13,9},{2,6},{6,2},{1... | collective-permute-start | bytes 3145736 | tf_op jit(solution)/shard_map/ppermute | solution.py:169
  174.0 10.9 %copy-start.10 = (f16[128,2048]{1,0:T(8,128)(2,1)S(1)}, f16[128,2048]{1,0:T(8,128)(2,1)}, u32[]{:S(2)}) copy-start(f16[128,2048]{1,0:T(8,128)(2,1)} %copy-done.9) | copy-start | bytes 1572868
  180.6 7.2 %copy-start.3 = (f32[512,2048]{1,0:T(8,128)S(1)}, f32[512,2048]{1,0:T(8,128)}, u32[]{:S(2)}) copy-start(f32[512,2048]{1,0:T(8,128)} %shard_map.76) | copy-start | bytes 12582916
  186.5 1.3 copy-start.7

commit v4 on v3

--- a/solution.py
+++ b/solution.py
@@ -280,14 +280,12 @@
     part += hop(after(part, a2), both)
     c1 = [wire(unwire(part_of(third, span)) + unwire(part_of(b1, span))) for span in spans]
     b2 = wire(unwire(second) + unwire(a2))
-    part, c1[0], b2, home, u2, *seen = lax.optimization_barrier(
-        (part, c1[0], b2, home, u2, *[block for block, _ in ups])
-    )
+    part, c1[0], b2, home, *seen = lax.optimization_barrier((part, c1[0], b2, home, *[block for block, _ in ups]))
     ups = [(block, ids) for block, (_, ids) in zip(seen, ups)]
 
-    a3 = [hop(block, both) for block in c1]
+    a3 = [hop(after(block, u2), both) for block in c1]
     part += hop(part, inner)
-    b2 = hop(after(b2, part), inner)
+    b2 = hop(after(b2, part, u2), inner)
     u1 = after(u1, part)
     late = turn(u1, 1, 1)
     low = part.astype(jnp.bfloat16)

time: 192 us -> 188 us (0.979)
  waiting for transfers between devices: 64.1 us -> 57.3 us
  starting transfers between devices: 23.8 us -> 26 us
    ppermute x4, waiting for transfers between devices: 11 us -> 4.49 us  [turn(): lax.ppermute(block, 'groups', [(i, (i + step) % groups) for i in range(gr...]
  transfers between devices with their start and end apart: 25 -> 25, of which waited for: 11 -> 11; matrix products, arithmetic and copies ran while one was open for 31% -> 32% of each run, Pallas kernels for 19% -> 20%
where the time goes in v4:
time: 188 us; the launch traced here: 187 us
  waiting for transfers between devices  57.3 us (30%)
  matrix products  38.1 us (20%)
  Pallas kernels  36.5 us (19%)
  starting transfers between devices  26 us (14%)
  other arithmetic  18.6 us (10%)
  local copies, waits for them, and re-layouts  9.69 us (5%)
    ppermute x9, waiting for transfers between devices, hop(): return lax.ppermute(block, 'tensor', pairs)  41.4 us
    dot_general x4, matrix products, product(): jnp.dot(rows_of, block, preferred_element_type=jnp.float32)  38.1 us
    pallas_call x2, Pallas kernels, expand(): pl.pallas_call(functools.partial(expand_kernel, rank), out_shape=jax.Shap...  19.9 us
    ppermute x9, starting transfers between devices, hop(): return lax.ppermute(block, 'tensor', pairs)  16.8 us
    pallas_call x2, Pallas kernels, shrink(): pl.pallas_call(functools.partial(shrink_kernel, rank, steps), out_shape=j...  16.6 us
    convert_element_type x4, other arithmetic, wire(): return total.astype(jnp.float16)  11.4 us
    ppermute x4, waiting for transfers between devices, cross(): lax.ppermute(after(block, *gates), 'dp', [(i, (i + shift * CORES) % owner...  10.6 us
    dynamic_update_slice x2, other arithmetic, on_device(): lax.dynamic_update_slice(lax.optimization_barrier(out), total.astype(jnp....  5.57 us
  transfers between devices with their start and end apart: 25, of which 11 were waited for; matrix products, arithmetic and copies ran while one was open for 32% of the time, Pallas kernels for 20%

profile of v4, /device:TPU:10, one launch (start us, length us, event | category | flops | bytes accessed | tf_op | source)
XLA Modules:
  0.0 187.2 jit_solution(5989229392905065044)
XLA Ops:
  0.1 0.1 add.209
  0.2 0.8 squeeze.4
  0.9 0.8 select_reduce_fusion
  1.7 10.0 %fusion.15 = f16[512,2048]{1,0:T(8,128)(2,1)} fusion(bf16[512,2048]{1,0:T(8,128)(2,1)} %mine_ref.1, bf16[2048,8192]{1,0:T(8,128)(2,1)} %param.8, s32[]{:T(128)S(6)} %select_n.93), kind=kOutput, calls=%fused_computation.16 | convolution fusion | flops 4297064448 | bytes 12582916 | tf_op jit(solution)/shard_map/dot_general | solution.py:201
  11.7 0.5 collective-permute-start.2
  12.2 1.3 constant_dynamic-slice_fusion.1
  13.5 0.6 collective-permute-start.3
  14.1 0.6 dynamic_slice.32
  15.5 0.1 pad_add_fusion.2.ids_ref
  15.6 1.3 collective-permute-start.4
  16.9 2.3 %constant_dynamic-slice_fusion = bf16[4,64,2048]{2,1,0:T(8,128)(2,1)} fusion(bf16[16,64,2048]{2,1,0:T(8,128)(2,1)} %param.9, s32[]{:T(128)S(6)} %select_n.95), kind=kLoop, calls=%fused_computation.31 | loop fusion | bytes 2097156 | tf_op jit(solution)/shard_map/dynamic_slice | solution.py:183
  19.2 9.3 %multiply_convert_fusion.1 = f16[512,2048]{1,0:T(8,128)(2,1)} fusion(bf16[512,2048]{1,0:T(8,128)(2,1)S(1)} %copy-done, bf16[2048,8192]{1,0:T(8,128)(2,1)} %param.8, s32[]{:T(128)S(6)} %select_n.98), kind=kOutput, calls=%fused_computation.11 | convolution fusion | flops 4297064448 | bytes 12582916 | tf_op jit(solution)/shard_map/dot_general | solution.py:201
  28.5 10.3 %collective-permute-done.3 = bf16[4,64,2048]{2,1,0:T(8,128)(2,1)} collective-permute-done((bf16[4,64,2048]{2,1,0:T(8,128)(2,1)S(1)}, bf16[4,64,2048]{2,1,0:T(8,128)(2,1)}, u32[]{:S(2)}, u32[]{:S(2)}) %collective-permute-start.3) | collective-permute-done | bytes 1048608 | tf_op jit(solution)/shard_map/ppermute | solution.py:184
  38.8 1.5 collective-permute-start.6
  40.3 0.5 collective-permute-start.5
  40.8 1.6 constant_dynamic-slice_fusion.3
  42.4 0.2 copy.15.g_ref
  42.7 9.3 %multiply_convert_fusion = f16[512,2048]{1,0:T(8,128)(2,1)} fusion(bf16[512,2048]{1,0:T(8,128)(2,1)S(1)} %copy-done, bf16[2048,8192]{1,0:T(8,128)(2,1)} %param.8, s32[]{:T(128)S(6)} %select_n.100), kind=kOutput, calls=%fused_computation.10 | convolution fusion | flops 4297064448 | bytes 12582916 | tf_op jit(solution)/shard_map/dot_general | solution.py:201
  51.9 13.8 %collective-permute-done.4 = f16[512,2048]{1,0:T(8,128)(2,1)} collective-permute-done((f16[512,2048]{1,0:T(8,128)(2,1)}, f16[512,2048]{1,0:T(8,128)(2,1)}, u32[]{:S(2)}, u32[]{:S(2)}) %collective-permute-start.4) | collective-permute-done | bytes 2097184 | tf_op jit(solution)/shard_map/ppermute | solution.py:241
  65.8 1.3 collective-permute-start.11
  67.1 1.6 collective-permute-start.9
  68.7 2.8 %add_convert_fusion.1 = f16[512,2048]{1,0:T(8,128)(2,1)S(1)} fusion(f16[512,2048]{1,0:T(8,128)(2,1)} %collective-permute-done.4, f16[512,2048]{1,0:T(8,128)(2,1)S(1)} %copy-done.5), kind=kLoop, calls=%fused_computation.9 | loop fusion | flops 4194304 | bytes 6291456 | tf_op jit(solution)/shard_map/convert_element_type | solution.py:125
  71.5 3.7 %collective-permute-start.13 = (f16[512,2048]{1,0:T(8,128)(2,1)S(1)}, f16[512,2048]{1,0:T(8,128)(2,1)}, u32[]{:S(2)}, u32[]{:S(2)}) collective-permute-start(f16[512,2048]{1,0:T(8,128)(2,1)S(1)} %add_convert_fusion.1), channel_id=1, source_target_pairs={{1,2},{2,1},{5,6},{6,5},{9,10},{10,9},{13,14},{14,13},{17,18},{18,... | collective-permute-start | bytes 6291464 | tf_op jit(solution)/shard_map/ppermute | solution.py:241
  75.2 1.6 collective-permute-start.7
  76.7 8.3 %shard_map.73 = f32[1024,128]{1,0:T(8,128)S(1)} custom-call(s32[16]{0:T(128)S(1)} %iota_add_fusion.4.ids_ref, s32[1024,1]{1,0:T(8,128)S(1)} %copy.15.g_ref, bf16[512,2048]{1,0:T(8,128)(2,1)S(1)} %copy-done, bf16[512,2048]{1,0:T(8,128)(2,1)} %collective-permute-done.2.other_ref, bf16[1024,2048]{1,0:T(8,128)(2,1)} %bitcast.29), custom_call_target="tpu_custom_call" | custom-call | flops 1 | bytes 1 | tf_op jit(solution)/shard_map/pallas_call | solution.py:54
  85.0 9.5 %fusion.base_ref = f32[512,2048]{1,0:T(8,128)} fusion(bf16[512,2048]{1,0:T(8,128)(2,1)S(1)} %copy-done, bf16[2048,8192]{1,0:T(8,128)(2,1)} %param.8, s32[]{:T(128)S(6)} %select_n.101), kind=kOutput, calls=%fused_computation | convolution fusion | flops 4294967296 | bytes 14680068 | tf_op jit(solution)/shard_map/dot_general | solution.py:201
  94.5 8.3 %shard_map.74 = f32[1024,128]{1,0:T(8,128)S(1)} custom-call(s32[16]{0:T(128)S(1)} %pad_add_fusion.2.ids_ref, s32[1024,1]{1,0:T(8,128)S(1)} %copy.15.g_ref, bf16[512,2048]{1,0:T(8,128)(2,1)} %mine_ref.1, bf16[512,2048]{1,0:T(8,128)(2,1)} %collective-permute-done.2.other_ref, bf16[256,2048]{1,0:T(8,128)(2,1)} %bitcast.5.refs_0_, ...), custom_call_target="tpu_custom_call" | custom-call | flops 1 | bytes 1 | tf_op jit(solution)/shard_map/pallas_call | solution.py:54
  102.9 0.2 slice_add_fusion.2
  103.1 0.1 collective-permute-start.10
  103.2 0.6 collective-permute-start.16
  103.8 0.2 collective-permute-start.14
  104.0 0.8 collective-permute-done.10
  104.7 0.5 collective-permute-start.8
  105.3 0.1 pad_maximum_fusion
  105.4 9.5 %collective-permute-done.11 = f16[512,2048]{1,0:T(8,128)(2,1)S(1)} collective-permute-done((f16[512,2048]{1,0:T(8,128)(2,1)S(1)}, f16[512,2048]{1,0:T(8,128)(2,1)S(1)}, u32[]{:S(2)}, u32[]{:S(2)}) %collective-permute-start.11) | collective-permute-done | bytes 2097184 | tf_op jit(solution)/shard_map/ppermute | solution.py:241
  114.9 2.5 %add_convert_fusion = f16[512,2048]{1,0:T(8,128)(2,1)} fusion(f16[512,2048]{1,0:T(8,128)(2,1)S(1)} %collective-permute-done.11, f16[512,2048]{1,0:T(8,128)(2,1)S(1)} %copy-done.6), kind=kLoop, calls=%fused_computation.8 | loop fusion | flops 4194304 | bytes 6291456 | tf_op jit(solution)/shard_map/convert_element_type | solution.py:125
  117.5 3.0 %collective-permute-done.13 = f16[512,2048]{1,0:T(8,128)(2,1)} collective-permute-done((f16[512,2048]{1,0:T(8,128)(2,1)S(1)}, f16[512,2048]{1,0:T(8,128)(2,1)}, u32[]{:S(2)}, u32[]{:S(2)}) %collective-permute-start.13) | collective-permute-done | bytes 2097184 | tf_op jit(solution)/shard_map/ppermute | solution.py:241
  120.4 2.1 %add_convert_fusion.3 = f16[128,2048]{1,0:T(8,128)(2,1)} fusion(f16[512,2048]{1,0:T(8,128)(2,1)} %collective-permute-done.13, f16[512,2048]{1,0:T(8,128)(2,1)} %multiply_convert_fusion), kind=kLoop, calls=%fused_computation.20 | loop fusion | flops 1048576 | bytes 1572864 | tf_op jit(solution)/shard_map/convert_element_type | solution.py:125
  122.6 0.1 fusion.31
  122.7 3.6 %collective-permute-start.15 = (f32[256,128]{1,0:T(8,128)S(1)}, f32[256,128]{1,0:T(8,128)S(1)}, u32[]{:S(2)}, u32[]{:S(2)}) collective-permute-start(f32[256,128]{1,0:T(8,128)S(1)} %fusion.31), channel_id=1, source_target_pairs={{1,2},{2,1},{5,6},{6,5},{9,10},{10,9},{13,14},{14,13},{17,18},{18,... | collective-permute-start | bytes 393224 | tf_op jit(solution)/shard_map/ppermute | solution.py:241
  126.3 3.4 %collective-permute-done.15 = f32[256,128]{1,0:T(8,128)S(1)} collective-permute-done((f32[256,128]{1,0:T(8,128)S(1)}, f32[256,128]{1,0:T(8,128)S(1)}, u32[]{:S(2)}, u32[]{:S(2)}) %collective-permute-start.15) | collective-permute-done | bytes 131104 | tf_op jit(solution)/shard_map/ppermute | solution.py:241
  129.7 0.3 collective-permute-done.8
  130.0 1.0 collective-permute-start.21
  131.0 2.8 %collective-permute-start.23 = (f16[512,2048]{1,0:T(8,128)(2,1)}, f16[512,2048]{1,0:T(8,128)(2,1)}, u32[]{:S(2)}, u32[]{:S(2)}) collective-permute-start(f16[512,2048]{1,0:T(8,128)(2,1)} %add_convert_fusion), channel_id=1, source_target_pairs={{1,2},{2,1},{5,6},{6,5},{9,10},{10,9},{13,14},{14,13},{17,18},{18,... | collective-permute-start | bytes 6291464 | tf_op jit(solution)/shard_map/ppermute | solution.py:241
  133.8 0.2 collective-permute-start.18
  134.0 4.0 %collective-permute-start.17 = (bf16[256,128]{1,0:T(8,128)(2,1)S(1)}, bf16[256,128]{1,0:T(8,128)(2,1)S(1)}, u32[]{:S(2)}, u32[]{:S(2)}) collective-permute-start(bf16[256,128]{1,0:T(8,128)(2,1)S(1)} %add.236), channel_id=1, source_target_pairs={{1,0},{2,3},{5,4},{6,7},{9,8},{10,11},{13,12},{14,15},{17,16},{18,... | collective-permute-start | bytes 196616 | tf_op jit(solution)/shard_map/ppermute | solution.py:241
  138.0 3.9 %add_convert_fusion.2 = f16[384,2048]{1,0:T(8,128)(2,1)} fusion(f16[512,2048]{1,0:T(8,128)(2,1)} %collective-permute-done.13, f16[512,2048]{1,0:T(8,128)(2,1)} %multiply_convert_fusion), kind=kLoop, calls=%fused_computation.15 | loop fusion | flops 3145728 | bytes 4718592 | tf_op jit(solution)/shard_map/convert_element_type | solution.py:125
  142.0 6.0 %collective-permute-done.17 = bf16[256,128]{1,0:T(8,128)(2,1)S(1)} collective-permute-done((bf16[256,128]{1,0:T(8,128)(2,1)S(1)}, bf16[256,128]{1,0:T(8,128)(2,1)S(1)}, u32[]{:S(2)}, u32[]{:S(2)}) %collective-permute-start.17) | collective-permute-done | bytes 65568 | tf_op jit(solution)/shard_map/ppermute | solution.py:241
  148.0 0.9 collective-permute-done.18
  148.9 0.8 copy-done.9
  149.7 0.5 collective-permute-start.20
  150.2 4.5 %collective-permute-done.21 = bf16[4,64,2048]{2,1,0:T(8,128)(2,1)} collective-permute-done((bf16[4,64,2048]{2,1,0:T(8,128)(2,1)}, bf16[4,64,2048]{2,1,0:T(8,128)(2,1)}, u32[]{:S(2)}, u32[]{:S(2)}) %collective-permute-start.21) | collective-permute-done | bytes 1048608 | tf_op jit(solution)/shard_map/ppermute | solution.py:190
  154.8 0.1 concatenate.29.ids_ref
  154.8 0.1 pad_add_fusion.1.ids_ref
  154.9 0.1 copy.18.g_ref
  155.1 0.1 fusion.26
  155.2 0.1 maximum_maximum_fusion.low_ref
  155.3 13.3 %shard_map.75.base_ref = f32[512,2048]{1,0:T(8,128)} custom-call(s32[56]{0:T(128)S(1)} %concatenate.29.ids_ref, s32[512,1]{1,0:T(8,128)S(1)} %copy.18.g_ref, bf16[512,128]{1,0:T(8,128)(2,1)S(1)} %maximum_maximum_fusion.low_ref, f32[512,2048]{1,0:T(8,128)} %fusion.base_ref, bf16[1024,2048]{1,0:T(8,128)(2,1)} %bitcast.28, bf16[1024,2048]{1,0:T(8,128)(2,1)} %bitcast.10.refs_1_, ...), custom_call_target="tpu_custom_call" | custom-call | flops 1 | bytes 1 | tf_op jit(solution)/shard_map/pallas_call | solution.py:100
  168.6 6.6 %shard_map.76 = f32[512,2048]{1,0:T(8,128)} custom-call(s32[8]{0:T(128)S(1)} %pad_add_fusion.1.ids_ref, s32[512,1]{1,0:T(8,128)S(1)} %copy.18.g_ref, bf16[512,128]{1,0:T(8,128)(2,1)S(1)} %maximum_maximum_fusion.low_ref, f32[512,2048]{1,0:T(8,128)} %shard_map.75.base_ref, bf16[256,2048]{1,0:T(8,128)(2,1)} %bitcast.17.refs_0_, bf16[256,2048]{1,0:T(8,128)(2,1)} %bitcast.18.refs_1_), custom_call_target="tpu_custom_call" | custom-call | flops 1 | bytes 1 | tf_op jit(solution)/shard_map/pallas_call | solution.py:100
  175.3 4.7 %collective-permute-done.23 = f16[512,2048]{1,0:T(8,128)(2,1)} collective-permute-done((f16[512,2048]{1,0:T(8,128)(2,1)}, f16[512,2048]{1,0:T(8,128)(2,1)}, u32[]{:S(2)}, u32[]{:S(2)}) %collective-permute-start.23) | collective-permute-done | bytes 2097184 | tf_op jit(solution)/shard_map/ppermute | solution.py:241
  180.0 0.2 broadcast_in_dim.25
  180.3 1.6 fusion.20
  181.9 1.3 copy-done.7
  183.2 4.0 %fusion.18 = bf16[512,2048]{1,0:T(8,128)(2,1)} fusion(bf16[512,2048]{1,0:T(8,128)(2,1)} %copy-done.7, f16[384,2048]{1,0:T(8,128)(2,1)} %collective-permute-done.24, f32[512,2048]{1,0:T(8,128)S(1)} %copy-done.3, f16[512,2048]{1,0:T(8,128)(2,1)} %collective-permute-done.23), kind=kLoop, calls=%fused_computation.17 | loop fusion | flops 4718592 | bytes 7864320 | tf_op jit(solution)/shard_map/dynamic_update_slice | solution.py:301
  (60 shorter events, 0.4 us)
Async XLA Ops:
  0.0 11.7 %collective-permute-start = (bf16[16,64,2048]{2,1,0:T(8,128)(2,1)}, bf16[16,64,2048]{2,1,0:T(8,128)(2,1)}, u32[]{:S(2)}, u32[]{:S(2)}) collective-permute-start(bf16[16,64,2048]{2,1,0:T(8,128)(2,1)} %param.10), channel_id=1, source_target_pairs={{0,4},{4,0},{8,12},{12,8},{1,5},{5,1},{9,13},{13,9},{2,6},{6,2},{1... | collective-permute-start | bytes 12582920 | tf_op jit(solution)/shard_map/ppermute | solution.py:169
  1.7 10.0 %copy-start = (bf16[512,2048]{1,0:T(8,128)(2,1)S(1)}, bf16[512,2048]{1,0:T(8,128)(2,1)}, u32[]{:S(2)}) copy-start(bf16[512,2048]{1,0:T(8,128)(2,1)} %mine_ref.1) | copy-start | bytes 6291460
  1.7 12.4 %copy-start.11 = (s32[4]{0:T(128)S(1)}, s32[4]{0:T(128)}, u32[]{:S(2)}) copy-start(s32[4]{0:T(128)} %constant.101.clone) | copy-start | bytes 52
  11.7 7.5 %collective-permute-start.2 = (bf16[512,2048]{1,0:T(8,128)(2,1)S(1)}, bf16[512,2048]{1,0:T(8,128)(2,1)}, u32[]{:S(2)}, u32[]{:S(2)}) collective-permute-start(bf16[512,2048]{1,0:T(8,128)(2,1)S(1)} %copy-done), channel_id=1, source_target_pairs={{0,4},{4,0},{8,12},{12,8},{1,5},{5,1},{9,13},{13,9},{2,6},{6,2},{1... | collective-permute-start | bytes 6291464 | tf_op jit(solution)/shard_map/ppermute | solution.py:169
  13.5 25.3 %collective-permute-start.3 = (bf16[4,64,2048]{2,1,0:T(8,128)(2,1)S(1)}, bf16[4,64,2048]{2,1,0:T(8,128)(2,1)}, u32[]{:S(2)}, u32[]{:S(2)}) collective-permute-start(bf16[4,64,2048]{2,1,0:T(8,128)(2,1)S(1)} %constant_dynamic-slice_fusion.1), channel_id=1, source_target_pairs={{0,8},{4,12},{8,0},{12,4},{1,9},{5,13},{9,1},{13,5},{2,10},{6,14},... | collective-permute-start | bytes 3145736 | tf_op jit(solution)/shard_map/ppermute | solution.py:184
  15.5 3.6 %collective-permute-start.1 = (s32[512]{0:T(512)S(1)}, s32[512]{0:T(512)S(1)}, u32[]{:S(2)}, u32[]{:S(2)}) collective-permute-start(s32[512]{0:T(512)S(1)} %select_reduce_fusion), channel_id=1, source_target_pairs={{0,4},{4,0},{8,12},{12,8},{1,5},{5,1},{9,13},{13,9},{2,6},{6,2},{1... | collective-permute-start | bytes 6152 | tf_op jit(solution)/shard_map/ppermute | solution.py:169
  15.6 50.2 %collective-permute-start.4 = (f16[512,2048]{1,0:T(8,128)(2,1)}, f16[512,2048]{1,0:T(8,128)(2,1)}, u32[]{:S(2)}, u32[]{:S(2)}) collective-permute-start(f16[512,2048]{1,0:T(8,128)(2,1)} %fusion.15), channel_id=1, source_target_pairs={{0,1},{3,2},{4,5},{7,6},{8,9},{11,10},{12,13},{15,14},{16,17},{19,... | collective-permute-start | bytes 6291464 | tf_op jit(solution)/shard_map/ppermute | solution.py:241
  19.2 21.7 %copy-start.4 = (bf16[16,64,2048]{2,1,0:T(8,128)(2,1)S(1)}, bf16[16,64,2048]{2,1,0:T(8,128)(2,1)}, u32[]{:S(2)}) copy-start(bf16[16,64,2048]{2,1,0:T(8,128)(2,1)} %param.10) | copy-start | bytes 12582916
  38.8 27.0 %collective-permute-start.6 = (bf16[4,64,2048]{2,1,0:T(8,128)(2,1)}, bf16[4,64,2048]{2,1,0:T(8,128)(2,1)}, u32[]{:S(2)}, u32[]{:S(2)}) collective-permute-start(bf16[4,64,2048]{2,1,0:T(8,128)(2,1)} %collective-permute-done.3), channel_id=1, source_target_pairs={{0,16},{16,0},{1,17},{17,1},{2,18},{18,2},{3,19},{19,3},{4,20},{20... | collective-permute-start | bytes 3145736 | tf_op jit(solution)/shard_map/ppermute | solution.py:190
  40.3 25.5 %collective-permute-start.5 = (bf16[4,64,2048]{2,1,0:T(8,128)(2,1)}, bf16[4,64,2048]{2,1,0:T(8,128)(2,1)}, u32[]{:S(2)}, u32[]{:S(2)}) collective-permute-start(bf16[4,64,2048]{2,1,0:T(8,128)(2,1)} %constant_dynamic-slice_fusion), channel_id=1, source_target_pairs={{0,8},{4,12},{8,0},{12,4},{1,9},{5,13},{9,1},{13,5},{2,10},{6,14},... | collective-permute-start | bytes 3145736 | tf_op jit(solution)/shard_map/ppermute | solution.py:184
  42.6 23.1 %copy-start.6 = (f16[512,2048]{1,0:T(8,128)(2,1)S(1)}, f16[512,2048]{1,0:T(8,128)(2,1)}, u32[]{:S(2)}) copy-start(f16[512,2048]{1,0:T(8,128)(2,1)} %multiply_convert_fusion.1) | copy-start | bytes 6291460
  42.7 26.0 %copy-start.5 = (f16[512,2048]{1,0:T(8,128)(2,1)S(1)}, f16[512,2048]{1,0:T(8,128)(2,1)}, u32[]{:S(2)}) copy-start(f16[512,2048]{1,0:T(8,128)(2,1)} %fusion.15) | copy-start | bytes 6291460
  65.8 49.1 %collective-permute-start.11 = (f16[512,2048]{1,0:T(8,128)(2,1)S(1)}, f16[512,2048]{1,0:T(8,128)(2,1)S(1)}, u32[]{:S(2)}, u32[]{:S(2)}) collective-permute-start(f16[512,2048]{1,0:T(8,128)(2,1)S(1)} %copy-done.6), channel_id=1, source_target_pairs={{0,1},{3,2},{4,5},{7,6},{8,9},{11,10},{12,13},{15,14},{16,17},{19,... | collective-permute-start | bytes 6291464 | tf_op jit(solution)/shard_map/ppermute | solution.py:241
  67.1 27.4 %collective-permute-start.9 = (bf16[4,64,2048]{2,1,0:T(8,128)(2,1)}, bf16[4,64,2048]{2,1,0:T(8,128)(2,1)S(1)}, u32[]{:S(2)}, u32[]{:S(2)}) collective-permute-start(bf16[4,64,2048]{2,1,0:T(8,128)(2,1)} %collective-permute-done.5), channel_id=1, source_target_pairs={{0,16},{16,0},{1,17},{17,1},{2,18},{18,2},{3,19},{19,3},{4,20},{20... | collective-permute-start | bytes 3145736 | tf_op jit(solution)/shard_map/ppermute | solution.py:190
  71.5 49.0 %collective-permute-start.13 = (f16[512,2048]{1,0:T(8,128)(2,1)S(1)}, f16[512,2048]{1,0:T(8,128)(2,1)}, u32[]{:S(2)}, u32[]{:S(2)}) collective-permute-start(f16[512,2048]{1,0:T(8,128)(2,1)S(1)} %add_convert_fusion.1), channel_id=1, source_target_pairs={{1,2},{2,1},{5,6},{6,5},{9,10},{10,9},{13,14},{14,13},{17,18},{18,... | collective-permute-start | bytes 6291464 | tf_op jit(solution)/shard_map/ppermute | solution.py:241
  75.2 28.1 %collective-permute-start.7 = (bf16[4,64,2048]{2,1,0:T(8,128)(2,1)}, bf16[4,64,2048]{2,1,0:T(8,128)(2,1)S(1)}, u32[]{:S(2)}, u32[]{:S(2)}) collective-permute-start(bf16[4,64,2048]{2,1,0:T(8,128)(2,1)} %get-tuple-element.53), channel_id=1, source_target_pairs={{0,8},{4,12},{8,0},{12,4},{1,9},{5,13},{9,1},{13,5},{2,10},{6,14},... | collective-permute-start | bytes 3145736 | tf_op jit(solution)/shard_map/ppermute | solution.py:184
  102.8 1.9 %copy-start.8 = (bf16[4,64,2048]{2,1,0:T(8,128)(2,1)S(1)}, bf16[4,64,2048]{2,1,0:T(8,128)(2,1)}, u32[]{:S(2)}) copy-start(bf16[4,64,2048]{2,1,0:T(8,128)(2,1)} %get-tuple-element.57) | copy-start | bytes 3145732
  103.1 1.6 collective-permute-start.10
  103.2 14.3 %copy-start.1 = (bf16[4,64,2048]{2,1,0:T(8,128)(2,1)}, bf16[4,64,2048]{2,1,0:T(8,128)(2,1)S(1)}, u32[]{:S(2)}) copy-start(bf16[4,64,2048]{2,1,0:T(8,128)(2,1)S(1)} %collective-permute-done.7) | copy-start | bytes 3145732
  103.2 27.8 %collective-permute-start.16 = (bf16[4,64,2048]{2,1,0:T(8,128)(2,1)S(1)}, bf16[4,64,2048]{2,1,0:T(8,128)(2,1)S(1)}, u32[]{:S(2)}, u32[]{:S(2)}) collective-permute-start(bf16[4,64,2048]{2,1,0:T(8,128)(2,1)S(1)} %collective-permute-done.7), channel_id=1, source_target_pairs={{0,16},{16,0},{1,17},{17,1},{2,18},{18,2},{3,19},{19,3},{4,20},{20... | collective-permute-start | bytes 3145736 | tf_op jit(solution)/shard_map/ppermute | solution.py:190
  103.8 18.9 %collective-permute-start.14 = (bf16[4,64,2048]{2,1,0:T(8,128)(2,1)S(1)}, bf16[4,64,2048]{2,1,0:T(8,128)(2,1)S(1)}, u32[]{:S(2)}, u32[]{:S(2)}) collective-permute-start(bf16[4,64,2048]{2,1,0:T(8,128)(2,1)S(1)} %collective-permute-done.7), channel_id=1, source_target_pairs={{0,4},{4,0},{8,12},{12,8},{1,5},{5,1},{9,13},{13,9},{2,6},{6,2},{1... | collective-permute-start | bytes 3145736 | tf_op jit(solution)/shard_map/ppermute | solution.py:169
  104.7 25.3 %collective-permute-start.8 = (bf16[4,64,2048]{2,1,0:T(8,128)(2,1)S(1)}, bf16[4,64,2048]{2,1,0:T(8,128)(2,1)}, u32[]{:S(2)}, u32[]{:S(2)}) collective-permute-start(bf16[4,64,2048]{2,1,0:T(8,128)(2,1)S(1)} %copy-done.8), channel_id=1, source_target_pairs={{0,8},{4,12},{8,0},{12,4},{1,9},{5,13},{9,1},{13,5},{2,10},{6,14},... | collective-permute-start | bytes 3145736 | tf_op jit(solution)/shard_map/ppermute | solution.py:184
  114.9 7.6 %collective-permute-start.12 = (f32[256,128]{1,0:T(8,128)S(1)}, f32[256,128]{1,0:T(8,128)S(1)}, u32[]{:S(2)}, u32[]{:S(2)}) collective-permute-start(f32[256,128]{1,0:T(8,128)S(1)} %pad_maximum_fusion), channel_id=1, source_target_pairs={{0,1},{1,0},{2,3},{3,2},{4,5},{5,4},{6,7},{7,6},{8,9},{9,8},{10,11... | collective-permute-start | bytes 393224 | tf_op jit(solution)/shard_map/ppermute | solution.py:241
  122.7 32.6 %copy-start.2 = (bf16[4,64,2048]{2,1,0:T(8,128)(2,1)S(1)}, bf16[4,64,2048]{2,1,0:T(8,128)(2,1)}, u32[]{:S(2)}) copy-start(bf16[4,64,2048]{2,1,0:T(8,128)(2,1)} %copy-done.1) | copy-start | bytes 3145732
  122.7 7.0 %collective-permute-start.15 = (f32[256,128]{1,0:T(8,128)S(1)}, f32[256,128]{1,0:T(8,128)S(1)}, u32[]{:S(2)}, u32[]{:S(2)}) collective-permute-start(f32[256,128]{1,0:T(8,128)S(1)} %fusion.31), channel_id=1, source_target_pairs={{1,2},{2,1},{5,6},{6,5},{9,10},{10,9},{13,14},{14,13},{17,18},{18,... | collective-permute-start | bytes 393224 | tf_op jit(solution)/shard_map/ppermute | solution.py:241
  130.0 24.7 %collective-permute-start.21 = (bf16[4,64,2048]{2,1,0:T(8,128)(2,1)}, bf16[4,64,2048]{2,1,0:T(8,128)(2,1)}, u32[]{:S(2)}, u32[]{:S(2)}) collective-permute-start(bf16[4,64,2048]{2,1,0:T(8,128)(2,1)} %collective-permute-done.8), channel_id=1, source_target_pairs={{0,16},{16,0},{1,17},{17,1},{2,18},{18,2},{3,19},{19,3},{4,20},{20... | collective-permute-start | bytes 3145736 | tf_op jit(solution)/shard_map/ppermute | solution.py:190
  131.0 49.0 %collective-permute-start.23 = (f16[512,2048]{1,0:T(8,128)(2,1)}, f16[512,2048]{1,0:T(8,128)(2,1)}, u32[]{:S(2)}, u32[]{:S(2)}) collective-permute-start(f16[512,2048]{1,0:T(8,128)(2,1)} %add_convert_fusion), channel_id=1, source_target_pairs={{1,2},{2,1},{5,6},{6,5},{9,10},{10,9},{13,14},{14,13},{17,18},{18,... | collective-permute-start | bytes 6291464 | tf_op jit(solution)/shard_map/ppermute | solution.py:241
  133.8 15.1 %collective-permute-start.18 = (f16[128,2048]{1,0:T(8,128)(2,1)}, f16[128,2048]{1,0:T(8,128)(2,1)S(1)}, u32[]{:S(2)}, u32[]{:S(2)}) collective-permute-start(f16[128,2048]{1,0:T(8,128)(2,1)} %add_convert_fusion.3), channel_id=1, source_target_pairs={{0,1},{1,0},{2,3},{3,2},{4,5},{5,4},{6,7},{7,6},{8,9},{9,8},{10,11... | collective-permute-start | bytes 1572872 | tf_op jit(solution)/shard_map/ppermute | solution.py:241
  134.0 14.0 %collective-permute-start.17 = (bf16[256,128]{1,0:T(8,128)(2,1)S(1)}, bf16[256,128]{1,0:T(8,128)(2,1)S(1)}, u32[]{:S(2)}, u32[]{:S(2)}) collective-permute-start(bf16[256,128]{1,0:T(8,128)(2,1)S(1)} %add.236), channel_id=1, source_target_pairs={{1,0},{2,3},{5,4},{6,7},{9,8},{10,11},{13,12},{14,15},{17,16},{18,... | collective-permute-start | bytes 196616 | tf_op jit(solution)/shard_map/ppermute | solution.py:241
  142.0 39.9 %collective-permute-start.24 = (f16[384,2048]{1,0:T(8,128)(2,1)}, f16[384,2048]{1,0:T(8,128)(2,1)}, u32[]{:S(2)}, u32[]{:S(2)}) collective-permute-start(f16[384,2048]{1,0:T(8,128)(2,1)} %add_convert_fusion.2), channel_id=1, source_target_pairs={{0,1},{1,0},{2,3},{3,2},{4,5},{5,4},{6,7},{7,6},{8,9},{9,8},{10,11... | collective-permute-start | bytes 4718600 | tf_op jit(solution)/shard_map/ppermute | solution.py:241
  148.9 0.8 copy-start.9
  149.7 5.6 %collective-permute-start.19 = (bf16[4,64,2048]{2,1,0:T(8,128)(2,1)}, bf16[4,64,2048]{2,1,0:T(8,128)(2,1)}, u32[]{:S(2)}, u32[]{:S(2)}) collective-permute-start(bf16[4,64,2048]{2,1,0:T(8,128)(2,1)} %collective-permute-done.8), channel_id=1, source_target_pairs={{0,4},{4,0},{8,12},{12,8},{1,5},{5,1},{9,13},{13,9},{2,6},{6,2},{1... | collective-permute-start | bytes 3145736 | tf_op jit(solution)/shard_map/ppermute | solution.py:169
  149.7 5.6 %collective-permute-start.20 = (bf16[4,64,2048]{2,1,0:T(8,128)(2,1)S(1)}, bf16[4,64,2048]{2,1,0:T(8,128)(2,1)}, u32[]{:S(2)}, u32[]{:S(2)}) collective-permute-start(bf16[4,64,2048]{2,1,0:T(8,128)(2,1)S(1)} %collective-permute-done.16), channel_id=1, source_target_pairs={{0,4},{4,0},{8,12},{12,8},{1,5},{5,1},{9,13},{13,9},{2,6},{6,2},{1... | collective-permute-start | bytes 3145736 | tf_op jit(solution)/shard_map/ppermute | solution.py:169
  154.7 13.9 %collective-permute-start.22 = (bf16[4,64,2048]{2,1,0:T(8,128)(2,1)}, bf16[4,64,2048]{2,1,0:T(8,128)(2,1)}, u32[]{:S(2)}, u32[]{:S(2)}) collective-permute-start(bf16[4,64,2048]{2,1,0:T(8,128)(2,1)} %collective-permute-done.21), channel_id=1, source_target_pairs={{0,4},{4,0},{8,12},{12,8},{1,5},{5,1},{9,13},{13,9},{2,6},{6,2},{1... | collective-permute-start | bytes 3145736 | tf_op jit(solution)/shard_map/ppermute | solution.py:169
  168.6 11.6 %copy-start.10 = (f16[128,2048]{1,0:T(8,128)(2,1)S(1)}, f16[128,2048]{1,0:T(8,128)(2,1)}, u32[]{:S(2)}) copy-start(f16[128,2048]{1,0:T(8,128)(2,1)} %copy-done.9) | copy-start | bytes 1572868
  175.3 7.9 %copy-start.3 = (f32[512,2048]{1,0:T(8,128)S(1)}, f32[512,2048]{1,0:T(8,128)}, u32[]{:S(2)}) copy-start(f32[512,2048]{1,0:T(8,128)} %shard_map.76) | copy-start | bytes 12582916
  181.9 1.3 copy-start.7

commit v5 on v4

--- a/solution.py
+++ b/solution.py
@@ -290,10 +290,9 @@
     late = turn(u1, 1, 1)
     low = part.astype(jnp.bfloat16)
     low = jnp.where((z == 1) | (z == 2), low, hop(low, [(1, 0), (2, 3)]))
-    u1, u2, low = lax.optimization_barrier((u1, u2, low, a3[0]))[:3]
-    ups += shared([(u1, u1_ids), (u2, u2_ids)])
+    u1, u2, low = after(u1, a3[0]), after(u2, a3[0]), after(low, a3[0])
     adapted = update(home, low, ups)
-    adapted = update(adapted, low, shared(late))
+    adapted = update(adapted, low, shared([(u1, u1_ids), (u2, u2_ids)]) + shared(late))
     out = jnp.zeros((rows, width), jnp.bfloat16)
     for arrived, span in zip(a3, spans):
         wired = unwire(arrived) + unwire(part_of(b2, span))

time: 188 us -> 188 us (level)
  transfers between devices with their start and end apart: 25 -> 25, of which waited for: 11 -> 9; matrix products, arithmetic and copies ran while one was open for 32% -> 32% of each run, Pallas kernels for 20% -> 19%
where the time goes in v5:
time: 188 us; the launch traced here: 187 us
  waiting for transfers between devices  55.7 us (30%)
  matrix products  38.1 us (20%)
  Pallas kernels  36.4 us (19%)
  starting transfers between devices  26.1 us (14%)
  other arithmetic  18.6 us (10%)
  local copies, waits for them, and re-layouts  11.1 us (6%)
    ppermute x9, waiting for transfers between devices, hop(): return lax.ppermute(block, 'tensor', pairs)  40.5 us
    dot_general x4, matrix products, product(): jnp.dot(rows_of, block, preferred_element_type=jnp.float32)  38.1 us
    pallas_call x2, Pallas kernels, expand(): pl.pallas_call(functools.partial(expand_kernel, rank), out_shape=jax.Shap...  19.8 us
    ppermute x9, starting transfers between devices, hop(): return lax.ppermute(block, 'tensor', pairs)  17.4 us
    pallas_call x2, Pallas kernels, shrink(): pl.pallas_call(functools.partial(shrink_kernel, rank, steps), out_shape=j...  16.6 us
    convert_element_type x4, other arithmetic, wire(): return total.astype(jnp.float16)  11.4 us
    ppermute x4, waiting for transfers between devices, cross(): lax.ppermute(after(block, *gates), 'dp', [(i, (i + shift * CORES) % owner...  10.3 us
    dynamic_update_slice x2, other arithmetic, on_device(): lax.dynamic_update_slice(lax.optimization_barrier(out), total.astype(jnp....  5.57 us
  transfers between devices with their start and end apart: 25, of which 9 were waited for; matrix products, arithmetic and copies ran while one was open for 32% of the time, Pallas kernels for 19%

profile of v5, /device:TPU:10, one launch (start us, length us, event | category | flops | bytes accessed | tf_op | source)
XLA Modules:
  0.0 187.0 jit_solution(12213178498563012539)
XLA Ops:
  0.0 0.1 add.217
  0.1 0.1 add.218
  0.2 0.8 squeeze.4
  0.9 0.8 select_reduce_fusion
  1.7 10.0 %fusion.15 = f16[512,2048]{1,0:T(8,128)(2,1)} fusion(bf16[512,2048]{1,0:T(8,128)(2,1)} %mine_ref.1, bf16[2048,8192]{1,0:T(8,128)(2,1)} %param.8, s32[]{:T(128)S(6)} %select_n.93), kind=kOutput, calls=%fused_computation.16 | convolution fusion | flops 4297064448 | bytes 12582916 | tf_op jit(solution)/shard_map/dot_general | solution.py:201
  11.7 0.5 collective-permute-start.2
  12.2 1.3 constant_dynamic-slice_fusion.3
  13.5 0.6 collective-permute-start.3
  14.1 0.6 dynamic_slice.30
  15.4 0.1 pad_add_fusion.1.ids_ref
  15.5 1.3 collective-permute-start.4
  16.8 2.3 %constant_dynamic-slice_fusion.2 = bf16[4,64,2048]{2,1,0:T(8,128)(2,1)} fusion(bf16[16,64,2048]{2,1,0:T(8,128)(2,1)} %param.9, s32[]{:T(128)S(6)} %select_n.101), kind=kLoop, calls=%fused_computation.33 | loop fusion | bytes 2097156 | tf_op jit(solution)/shard_map/dynamic_slice | solution.py:183
  19.1 9.3 %multiply_convert_fusion.1 = f16[512,2048]{1,0:T(8,128)(2,1)} fusion(bf16[512,2048]{1,0:T(8,128)(2,1)S(1)} %copy-done, bf16[2048,8192]{1,0:T(8,128)(2,1)} %param.8, s32[]{:T(128)S(6)} %select_n.97), kind=kOutput, calls=%fused_computation.11 | convolution fusion | flops 4297064448 | bytes 12582916 | tf_op jit(solution)/shard_map/dot_general | solution.py:201
  28.5 10.3 %collective-permute-done.3 = bf16[4,64,2048]{2,1,0:T(8,128)(2,1)} collective-permute-done((bf16[4,64,2048]{2,1,0:T(8,128)(2,1)S(1)}, bf16[4,64,2048]{2,1,0:T(8,128)(2,1)}, u32[]{:S(2)}, u32[]{:S(2)}) %collective-permute-start.3) | collective-permute-done | bytes 1048608 | tf_op jit(solution)/shard_map/ppermute | solution.py:184
  38.8 1.5 collective-permute-start.6
  40.3 0.5 collective-permute-start.5
  40.8 1.6 constant_dynamic-slice_fusion
  42.4 0.2 copy.15.g_ref
  42.7 9.3 %multiply_convert_fusion = f16[512,2048]{1,0:T(8,128)(2,1)} fusion(bf16[512,2048]{1,0:T(8,128)(2,1)S(1)} %copy-done, bf16[2048,8192]{1,0:T(8,128)(2,1)} %param.8, s32[]{:T(128)S(6)} %select_n.100), kind=kOutput, calls=%fused_computation.10 | convolution fusion | flops 4297064448 | bytes 12582916 | tf_op jit(solution)/shard_map/dot_general | solution.py:201
  51.9 13.8 %collective-permute-done.4 = f16[512,2048]{1,0:T(8,128)(2,1)} collective-permute-done((f16[512,2048]{1,0:T(8,128)(2,1)}, f16[512,2048]{1,0:T(8,128)(2,1)}, u32[]{:S(2)}, u32[]{:S(2)}) %collective-permute-start.4) | collective-permute-done | bytes 2097184 | tf_op jit(solution)/shard_map/ppermute | solution.py:241
  65.7 1.3 collective-permute-start.9
  67.0 1.6 collective-permute-start.7
  68.6 2.8 %add_convert_fusion.1 = f16[512,2048]{1,0:T(8,128)(2,1)S(1)} fusion(f16[512,2048]{1,0:T(8,128)(2,1)} %collective-permute-done.4, f16[512,2048]{1,0:T(8,128)(2,1)S(1)} %copy-done.7), kind=kLoop, calls=%fused_computation.9 | loop fusion | flops 4194304 | bytes 6291456 | tf_op jit(solution)/shard_map/convert_element_type | solution.py:125
  71.4 3.7 %collective-permute-start.11 = (f16[512,2048]{1,0:T(8,128)(2,1)S(1)}, f16[512,2048]{1,0:T(8,128)(2,1)}, u32[]{:S(2)}, u32[]{:S(2)}) collective-permute-start(f16[512,2048]{1,0:T(8,128)(2,1)S(1)} %add_convert_fusion.1), channel_id=1, source_target_pairs={{1,2},{2,1},{5,6},{6,5},{9,10},{10,9},{13,14},{14,13},{17,18},{18,... | collective-permute-start | bytes 6291464 | tf_op jit(solution)/shard_map/ppermute | solution.py:241
  75.1 1.6 collective-permute-start.12
  76.7 8.3 %shard_map.73 = f32[1024,128]{1,0:T(8,128)S(1)} custom-call(s32[16]{0:T(128)S(1)} %iota_add_fusion.2.ids_ref, s32[1024,1]{1,0:T(8,128)S(1)} %copy.15.g_ref, bf16[512,2048]{1,0:T(8,128)(2,1)S(1)} %copy-done, bf16[512,2048]{1,0:T(8,128)(2,1)} %collective-permute-done.2.other_ref, bf16[1024,2048]{1,0:T(8,128)(2,1)} %bitcast.29), custom_call_target="tpu_custom_call" | custom-call | flops 1 | bytes 1 | tf_op jit(solution)/shard_map/pallas_call | solution.py:54
  84.9 9.5 %fusion.base_ref = f32[512,2048]{1,0:T(8,128)} fusion(bf16[512,2048]{1,0:T(8,128)(2,1)S(1)} %copy-done, bf16[2048,8192]{1,0:T(8,128)(2,1)} %param.8, s32[]{:T(128)S(6)} %select_n.102), kind=kOutput, calls=%fused_computation | convolution fusion | flops 4294967296 | bytes 14680068 | tf_op jit(solution)/shard_map/dot_general | solution.py:201
  94.4 8.3 %shard_map.74 = f32[1024,128]{1,0:T(8,128)S(1)} custom-call(s32[16]{0:T(128)S(1)} %pad_add_fusion.1.ids_ref, s32[1024,1]{1,0:T(8,128)S(1)} %copy.15.g_ref, bf16[512,2048]{1,0:T(8,128)(2,1)} %mine_ref.1, bf16[512,2048]{1,0:T(8,128)(2,1)} %collective-permute-done.2.other_ref, bf16[256,2048]{1,0:T(8,128)(2,1)} %bitcast.5.refs_0_, ...), custom_call_target="tpu_custom_call" | custom-call | flops 1 | bytes 1 | tf_op jit(solution)/shard_map/pallas_call | solution.py:54
  102.8 0.2 slice_add_fusion.2
  103.1 0.1 collective-permute-start.8
  103.2 0.6 collective-permute-start.16
  103.8 0.2 collective-permute-start.13
  103.9 0.8 collective-permute-done.8
  104.7 0.5 collective-permute-start.18
  105.3 0.1 pad_maximum_fusion
  105.4 9.5 %collective-permute-done.9 = f16[512,2048]{1,0:T(8,128)(2,1)S(1)} collective-permute-done((f16[512,2048]{1,0:T(8,128)(2,1)S(1)}, f16[512,2048]{1,0:T(8,128)(2,1)S(1)}, u32[]{:S(2)}, u32[]{:S(2)}) %collective-permute-start.9) | collective-permute-done | bytes 2097184 | tf_op jit(solution)/shard_map/ppermute | solution.py:241
  114.9 2.5 %add_convert_fusion = f16[512,2048]{1,0:T(8,128)(2,1)} fusion(f16[512,2048]{1,0:T(8,128)(2,1)S(1)} %collective-permute-done.9, f16[512,2048]{1,0:T(8,128)(2,1)S(1)} %copy-done.8), kind=kLoop, calls=%fused_computation.8 | loop fusion | flops 4194304 | bytes 6291456 | tf_op jit(solution)/shard_map/convert_element_type | solution.py:125
  117.4 3.0 %collective-permute-done.11 = f16[512,2048]{1,0:T(8,128)(2,1)} collective-permute-done((f16[512,2048]{1,0:T(8,128)(2,1)S(1)}, f16[512,2048]{1,0:T(8,128)(2,1)}, u32[]{:S(2)}, u32[]{:S(2)}) %collective-permute-start.11) | collective-permute-done | bytes 2097184 | tf_op jit(solution)/shard_map/ppermute | solution.py:241
  120.4 2.2 %add_convert_fusion.3 = f16[128,2048]{1,0:T(8,128)(2,1)} fusion(f16[512,2048]{1,0:T(8,128)(2,1)} %collective-permute-done.11, f16[512,2048]{1,0:T(8,128)(2,1)} %multiply_convert_fusion), kind=kLoop, calls=%fused_computation.20 | loop fusion | flops 1048576 | bytes 1572864 | tf_op jit(solution)/shard_map/convert_element_type | solution.py:125
  122.5 0.1 fusion.31
  122.7 1.0 copy-done.3
  123.7 3.5 %collective-permute-start.14 = (f32[256,128]{1,0:T(8,128)S(1)}, f32[256,128]{1,0:T(8,128)S(1)}, u32[]{:S(2)}, u32[]{:S(2)}) collective-permute-start(f32[256,128]{1,0:T(8,128)S(1)} %fusion.31), channel_id=1, source_target_pairs={{1,2},{2,1},{5,6},{6,5},{9,10},{10,9},{13,14},{14,13},{17,18},{18,... | collective-permute-start | bytes 393224 | tf_op jit(solution)/shard_map/ppermute | solution.py:241
  127.1 3.4 %collective-permute-done.14 = f32[256,128]{1,0:T(8,128)S(1)} collective-permute-done((f32[256,128]{1,0:T(8,128)S(1)}, f32[256,128]{1,0:T(8,128)S(1)}, u32[]{:S(2)}, u32[]{:S(2)}) %collective-permute-start.14) | collective-permute-done | bytes 131104 | tf_op jit(solution)/shard_map/ppermute | solution.py:241
  130.5 0.6 collective-permute-start.21
  131.1 3.5 %collective-permute-start.23 = (f16[512,2048]{1,0:T(8,128)(2,1)}, f16[512,2048]{1,0:T(8,128)(2,1)}, u32[]{:S(2)}, u32[]{:S(2)}) collective-permute-start(f16[512,2048]{1,0:T(8,128)(2,1)} %add_convert_fusion), channel_id=1, source_target_pairs={{1,2},{2,1},{5,6},{6,5},{9,10},{10,9},{13,14},{14,13},{17,18},{18,... | collective-permute-start | bytes 6291464 | tf_op jit(solution)/shard_map/ppermute | solution.py:241
  134.6 0.1 collective-permute-start.17
  134.7 4.1 %collective-permute-start.15 = (bf16[256,128]{1,0:T(8,128)(2,1)S(1)}, bf16[256,128]{1,0:T(8,128)(2,1)S(1)}, u32[]{:S(2)}, u32[]{:S(2)}) collective-permute-start(bf16[256,128]{1,0:T(8,128)(2,1)S(1)} %add.238), channel_id=1, source_target_pairs={{1,0},{2,3},{5,4},{6,7},{9,8},{10,11},{13,12},{14,15},{17,16},{18,... | collective-permute-start | bytes 196616 | tf_op jit(solution)/shard_map/ppermute | solution.py:241
  138.8 3.9 %add_convert_fusion.2 = f16[384,2048]{1,0:T(8,128)(2,1)} fusion(f16[512,2048]{1,0:T(8,128)(2,1)} %collective-permute-done.11, f16[512,2048]{1,0:T(8,128)(2,1)} %multiply_convert_fusion), kind=kLoop, calls=%fused_computation.15 | loop fusion | flops 3145728 | bytes 4718592 | tf_op jit(solution)/shard_map/convert_element_type | solution.py:125
  142.7 7.0 %collective-permute-done.17 = f16[128,2048]{1,0:T(8,128)(2,1)S(1)} collective-permute-done((f16[128,2048]{1,0:T(8,128)(2,1)}, f16[128,2048]{1,0:T(8,128)(2,1)S(1)}, u32[]{:S(2)}, u32[]{:S(2)}) %collective-permute-start.17) | collective-permute-done | bytes 524320 | tf_op jit(solution)/shard_map/ppermute | solution.py:241
  149.8 0.5 collective-permute-start.19
  150.3 4.1 %collective-permute-done.21 = bf16[4,64,2048]{2,1,0:T(8,128)(2,1)} collective-permute-done((bf16[4,64,2048]{2,1,0:T(8,128)(2,1)S(1)}, bf16[4,64,2048]{2,1,0:T(8,128)(2,1)}, u32[]{:S(2)}, u32[]{:S(2)}) %collective-permute-start.21) | collective-permute-done | bytes 1048608 | tf_op jit(solution)/shard_map/ppermute | solution.py:190
  154.4 0.1 concatenate.23.ids_ref
  154.5 0.1 pad_add_fusion.2.ids_ref
  154.6 0.1 copy.18.g_ref
  154.8 0.1 fusion.26
  154.8 0.1 maximum_maximum_fusion.low_ref
  155.0 1.2 copy-done.4
  156.2 11.1 %shard_map.75.base_ref = f32[512,2048]{1,0:T(8,128)} custom-call(s32[40]{0:T(128)S(1)} %pad_add_fusion.2.ids_ref, s32[512,1]{1,0:T(8,128)S(1)} %copy.18.g_ref, bf16[512,128]{1,0:T(8,128)(2,1)S(1)} %maximum_maximum_fusion.low_ref, f32[512,2048]{1,0:T(8,128)} %fusion.base_ref, bf16[1024,2048]{1,0:T(8,128)(2,1)} %bitcast.30, ...), custom_call_target="tpu_custom_call" | custom-call | flops 1 | bytes 1 | tf_op jit(solution)/shard_map/pallas_call | solution.py:100
  167.3 8.6 %shard_map.76 = f32[512,2048]{1,0:T(8,128)} custom-call(s32[24]{0:T(128)S(1)} %concatenate.23.ids_ref, s32[512,1]{1,0:T(8,128)S(1)} %copy.18.g_ref, bf16[512,128]{1,0:T(8,128)(2,1)S(1)} %maximum_maximum_fusion.low_ref, f32[512,2048]{1,0:T(8,128)} %shard_map.75.base_ref, bf16[256,2048]{1,0:T(8,128)(2,1)S(1)} %bitcast.26, bf16[256,2048]{1,0:T(8,128)(2,1)S(1)} %bitcast.25, ...), custom_call_target="tpu_custom_call" | custom-call | flops 1 | bytes 1 | tf_op jit(solution)/shard_map/pallas_call | solution.py:100
  176.0 3.9 %collective-permute-done.23 = f16[512,2048]{1,0:T(8,128)(2,1)} collective-permute-done((f16[512,2048]{1,0:T(8,128)(2,1)}, f16[512,2048]{1,0:T(8,128)(2,1)}, u32[]{:S(2)}, u32[]{:S(2)}) %collective-permute-start.23) | collective-permute-done | bytes 2097184 | tf_op jit(solution)/shard_map/ppermute | solution.py:241
  179.9 0.2 broadcast_in_dim.25
  180.1 1.6 fusion.20
  181.7 1.3 copy-done.9
  183.0 4.0 %fusion.18 = bf16[512,2048]{1,0:T(8,128)(2,1)} fusion(bf16[512,2048]{1,0:T(8,128)(2,1)} %copy-done.9, f16[384,2048]{1,0:T(8,128)(2,1)} %collective-permute-done.24, f32[512,2048]{1,0:T(8,128)S(1)} %copy-done.5, f16[512,2048]{1,0:T(8,128)(2,1)} %collective-permute-done.23), kind=kLoop, calls=%fused_computation.17 | loop fusion | flops 4718592 | bytes 7864320 | tf_op jit(solution)/shard_map/dynamic_update_slice | solution.py:300
  (64 shorter events, 0.3 us)
Async XLA Ops:
  0.0 11.7 %collective-permute-start = (bf16[16,64,2048]{2,1,0:T(8,128)(2,1)}, bf16[16,64,2048]{2,1,0:T(8,128)(2,1)}, u32[]{:S(2)}, u32[]{:S(2)}) collective-permute-start(bf16[16,64,2048]{2,1,0:T(8,128)(2,1)} %param.10), channel_id=1, source_target_pairs={{0,4},{4,0},{8,12},{12,8},{1,5},{5,1},{9,13},{13,9},{2,6},{6,2},{1... | collective-permute-start | bytes 12582920 | tf_op jit(solution)/shard_map/ppermute | solution.py:169
  1.7 10.0 %copy-start = (bf16[512,2048]{1,0:T(8,128)(2,1)S(1)}, bf16[512,2048]{1,0:T(8,128)(2,1)}, u32[]{:S(2)}) copy-start(bf16[512,2048]{1,0:T(8,128)(2,1)} %mine_ref.1) | copy-start | bytes 6291460
  1.7 12.4 %copy-start.13 = (s32[4]{0:T(128)S(1)}, s32[4]{0:T(128)}, u32[]{:S(2)}) copy-start(s32[4]{0:T(128)} %constant.101.clone) | copy-start | bytes 52
  11.7 7.4 %collective-permute-start.2 = (bf16[512,2048]{1,0:T(8,128)(2,1)S(1)}, bf16[512,2048]{1,0:T(8,128)(2,1)}, u32[]{:S(2)}, u32[]{:S(2)}) collective-permute-start(bf16[512,2048]{1,0:T(8,128)(2,1)S(1)} %copy-done), channel_id=1, source_target_pairs={{0,4},{4,0},{8,12},{12,8},{1,5},{5,1},{9,13},{13,9},{2,6},{6,2},{1... | collective-permute-start | bytes 6291464 | tf_op jit(solution)/shard_map/ppermute | solution.py:169
  13.5 25.3 %collective-permute-start.3 = (bf16[4,64,2048]{2,1,0:T(8,128)(2,1)S(1)}, bf16[4,64,2048]{2,1,0:T(8,128)(2,1)}, u32[]{:S(2)}, u32[]{:S(2)}) collective-permute-start(bf16[4,64,2048]{2,1,0:T(8,128)(2,1)S(1)} %constant_dynamic-slice_fusion.3), channel_id=1, source_target_pairs={{0,8},{4,12},{8,0},{12,4},{1,9},{5,13},{9,1},{13,5},{2,10},{6,14},... | collective-permute-start | bytes 3145736 | tf_op jit(solution)/shard_map/ppermute | solution.py:184
  15.5 3.6 %collective-permute-start.1 = (s32[512]{0:T(512)S(1)}, s32[512]{0:T(512)S(1)}, u32[]{:S(2)}, u32[]{:S(2)}) collective-permute-start(s32[512]{0:T(512)S(1)} %select_reduce_fusion), channel_id=1, source_target_pairs={{0,4},{4,0},{8,12},{12,8},{1,5},{5,1},{9,13},{13,9},{2,6},{6,2},{1... | collective-permute-start | bytes 6152 | tf_op jit(solution)/shard_map/ppermute | solution.py:169
  15.5 50.2 %collective-permute-start.4 = (f16[512,2048]{1,0:T(8,128)(2,1)}, f16[512,2048]{1,0:T(8,128)(2,1)}, u32[]{:S(2)}, u32[]{:S(2)}) collective-permute-start(f16[512,2048]{1,0:T(8,128)(2,1)} %fusion.15), channel_id=1, source_target_pairs={{0,1},{3,2},{4,5},{7,6},{8,9},{11,10},{12,13},{15,14},{16,17},{19,... | collective-permute-start | bytes 6291464 | tf_op jit(solution)/shard_map/ppermute | solution.py:241
  19.1 21.7 %copy-start.6 = (bf16[16,64,2048]{2,1,0:T(8,128)(2,1)S(1)}, bf16[16,64,2048]{2,1,0:T(8,128)(2,1)}, u32[]{:S(2)}) copy-start(bf16[16,64,2048]{2,1,0:T(8,128)(2,1)} %param.10) | copy-start | bytes 12582916
  38.8 27.0 %collective-permute-start.6 = (bf16[4,64,2048]{2,1,0:T(8,128)(2,1)}, bf16[4,64,2048]{2,1,0:T(8,128)(2,1)}, u32[]{:S(2)}, u32[]{:S(2)}) collective-permute-start(bf16[4,64,2048]{2,1,0:T(8,128)(2,1)} %collective-permute-done.3), channel_id=1, source_target_pairs={{0,16},{16,0},{1,17},{17,1},{2,18},{18,2},{3,19},{19,3},{4,20},{20... | collective-permute-start | bytes 3145736 | tf_op jit(solution)/shard_map/ppermute | solution.py:190
  40.3 25.4 %collective-permute-start.5 = (bf16[4,64,2048]{2,1,0:T(8,128)(2,1)}, bf16[4,64,2048]{2,1,0:T(8,128)(2,1)}, u32[]{:S(2)}, u32[]{:S(2)}) collective-permute-start(bf16[4,64,2048]{2,1,0:T(8,128)(2,1)} %constant_dynamic-slice_fusion.2), channel_id=1, source_target_pairs={{0,8},{4,12},{8,0},{12,4},{1,9},{5,13},{9,1},{13,5},{2,10},{6,14},... | collective-permute-start | bytes 3145736 | tf_op jit(solution)/shard_map/ppermute | solution.py:184
  42.7 23.1 %copy-start.8 = (f16[512,2048]{1,0:T(8,128)(2,1)S(1)}, f16[512,2048]{1,0:T(8,128)(2,1)}, u32[]{:S(2)}) copy-start(f16[512,2048]{1,0:T(8,128)(2,1)} %multiply_convert_fusion.1) | copy-start | bytes 6291460
  42.7 26.0 %copy-start.7 = (f16[512,2048]{1,0:T(8,128)(2,1)S(1)}, f16[512,2048]{1,0:T(8,128)(2,1)}, u32[]{:S(2)}) copy-start(f16[512,2048]{1,0:T(8,128)(2,1)} %fusion.15) | copy-start | bytes 6291460
  65.7 49.1 %collective-permute-start.9 = (f16[512,2048]{1,0:T(8,128)(2,1)S(1)}, f16[512,2048]{1,0:T(8,128)(2,1)S(1)}, u32[]{:S(2)}, u32[]{:S(2)}) collective-permute-start(f16[512,2048]{1,0:T(8,128)(2,1)S(1)} %copy-done.8), channel_id=1, source_target_pairs={{0,1},{3,2},{4,5},{7,6},{8,9},{11,10},{12,13},{15,14},{16,17},{19,... | collective-permute-start | bytes 6291464 | tf_op jit(solution)/shard_map/ppermute | solution.py:241
  67.0 27.4 %collective-permute-start.7 = (bf16[4,64,2048]{2,1,0:T(8,128)(2,1)}, bf16[4,64,2048]{2,1,0:T(8,128)(2,1)S(1)}, u32[]{:S(2)}, u32[]{:S(2)}) collective-permute-start(bf16[4,64,2048]{2,1,0:T(8,128)(2,1)} %collective-permute-done.5), channel_id=1, source_target_pairs={{0,16},{16,0},{1,17},{17,1},{2,18},{18,2},{3,19},{19,3},{4,20},{20... | collective-permute-start | bytes 3145736 | tf_op jit(solution)/shard_map/ppermute | solution.py:190
  71.4 49.0 %collective-permute-start.11 = (f16[512,2048]{1,0:T(8,128)(2,1)S(1)}, f16[512,2048]{1,0:T(8,128)(2,1)}, u32[]{:S(2)}, u32[]{:S(2)}) collective-permute-start(f16[512,2048]{1,0:T(8,128)(2,1)S(1)} %add_convert_fusion.1), channel_id=1, source_target_pairs={{1,2},{2,1},{5,6},{6,5},{9,10},{10,9},{13,14},{14,13},{17,18},{18,... | collective-permute-start | bytes 6291464 | tf_op jit(solution)/shard_map/ppermute | solution.py:241
  75.1 28.1 %collective-permute-start.12 = (bf16[4,64,2048]{2,1,0:T(8,128)(2,1)}, bf16[4,64,2048]{2,1,0:T(8,128)(2,1)S(1)}, u32[]{:S(2)}, u32[]{:S(2)}) collective-permute-start(bf16[4,64,2048]{2,1,0:T(8,128)(2,1)} %get-tuple-element.63), channel_id=1, source_target_pairs={{0,8},{4,12},{8,0},{12,4},{1,9},{5,13},{9,1},{13,5},{2,10},{6,14},... | collective-permute-start | bytes 3145736 | tf_op jit(solution)/shard_map/ppermute | solution.py:184
  102.8 1.9 %copy-start.10 = (bf16[4,64,2048]{2,1,0:T(8,128)(2,1)S(1)}, bf16[4,64,2048]{2,1,0:T(8,128)(2,1)}, u32[]{:S(2)}) copy-start(bf16[4,64,2048]{2,1,0:T(8,128)(2,1)} %get-tuple-element.74) | copy-start | bytes 3145732
  103.1 1.6 collective-permute-start.8
  103.2 14.2 %copy-start.1 = (bf16[4,64,2048]{2,1,0:T(8,128)(2,1)}, bf16[4,64,2048]{2,1,0:T(8,128)(2,1)S(1)}, u32[]{:S(2)}) copy-start(bf16[4,64,2048]{2,1,0:T(8,128)(2,1)S(1)} %collective-permute-done.12) | copy-start | bytes 3145732
  103.2 27.9 %collective-permute-start.16 = (bf16[4,64,2048]{2,1,0:T(8,128)(2,1)S(1)}, bf16[4,64,2048]{2,1,0:T(8,128)(2,1)S(1)}, u32[]{:S(2)}, u32[]{:S(2)}) collective-permute-start(bf16[4,64,2048]{2,1,0:T(8,128)(2,1)S(1)} %collective-permute-done.12), channel_id=1, source_target_pairs={{0,16},{16,0},{1,17},{17,1},{2,18},{18,2},{3,19},{19,3},{4,20},{20... | collective-permute-start | bytes 3145736 | tf_op jit(solution)/shard_map/ppermute | solution.py:190
  103.8 18.9 %collective-permute-start.13 = (bf16[4,64,2048]{2,1,0:T(8,128)(2,1)S(1)}, bf16[4,64,2048]{2,1,0:T(8,128)(2,1)S(1)}, u32[]{:S(2)}, u32[]{:S(2)}) collective-permute-start(bf16[4,64,2048]{2,1,0:T(8,128)(2,1)S(1)} %collective-permute-done.12), channel_id=1, source_target_pairs={{0,4},{4,0},{8,12},{12,8},{1,5},{5,1},{9,13},{13,9},{2,6},{6,2},{1... | collective-permute-start | bytes 3145736 | tf_op jit(solution)/shard_map/ppermute | solution.py:169
  104.7 25.8 %collective-permute-start.18 = (bf16[4,64,2048]{2,1,0:T(8,128)(2,1)S(1)}, bf16[4,64,2048]{2,1,0:T(8,128)(2,1)S(1)}, u32[]{:S(2)}, u32[]{:S(2)}) collective-permute-start(bf16[4,64,2048]{2,1,0:T(8,128)(2,1)S(1)} %copy-done.10), channel_id=1, source_target_pairs={{0,8},{4,12},{8,0},{12,4},{1,9},{5,13},{9,1},{13,5},{2,10},{6,14},... | collective-permute-start | bytes 3145736 | tf_op jit(solution)/shard_map/ppermute | solution.py:184
  114.9 7.7 %collective-permute-start.10 = (f32[256,128]{1,0:T(8,128)S(1)}, f32[256,128]{1,0:T(8,128)S(1)}, u32[]{:S(2)}, u32[]{:S(2)}) collective-permute-start(f32[256,128]{1,0:T(8,128)S(1)} %pad_maximum_fusion), channel_id=1, source_target_pairs={{0,1},{1,0},{2,3},{3,2},{4,5},{5,4},{6,7},{7,6},{8,9},{9,8},{10,11... | collective-permute-start | bytes 393224 | tf_op jit(solution)/shard_map/ppermute | solution.py:241
  122.6 32.3 %copy-start.2 = (bf16[4,64,2048]{2,1,0:T(8,128)(2,1)S(1)}, bf16[4,64,2048]{2,1,0:T(8,128)(2,1)}, u32[]{:S(2)}) copy-start(bf16[4,64,2048]{2,1,0:T(8,128)(2,1)} %copy-done.1) | copy-start | bytes 3145732
  122.7 1.0 copy-start.3
  123.7 6.8 %collective-permute-start.14 = (f32[256,128]{1,0:T(8,128)S(1)}, f32[256,128]{1,0:T(8,128)S(1)}, u32[]{:S(2)}, u32[]{:S(2)}) collective-permute-start(f32[256,128]{1,0:T(8,128)S(1)} %fusion.31), channel_id=1, source_target_pairs={{1,2},{2,1},{5,6},{6,5},{9,10},{10,9},{13,14},{14,13},{17,18},{18,... | collective-permute-start | bytes 393224 | tf_op jit(solution)/shard_map/ppermute | solution.py:241
  130.5 23.8 %collective-permute-start.21 = (bf16[4,64,2048]{2,1,0:T(8,128)(2,1)S(1)}, bf16[4,64,2048]{2,1,0:T(8,128)(2,1)}, u32[]{:S(2)}, u32[]{:S(2)}) collective-permute-start(bf16[4,64,2048]{2,1,0:T(8,128)(2,1)S(1)} %collective-permute-done.18), channel_id=1, source_target_pairs={{0,16},{16,0},{1,17},{17,1},{2,18},{18,2},{3,19},{19,3},{4,20},{20... | collective-permute-start | bytes 3145736 | tf_op jit(solution)/shard_map/ppermute | solution.py:190
  131.1 48.7 %collective-permute-start.23 = (f16[512,2048]{1,0:T(8,128)(2,1)}, f16[512,2048]{1,0:T(8,128)(2,1)}, u32[]{:S(2)}, u32[]{:S(2)}) collective-permute-start(f16[512,2048]{1,0:T(8,128)(2,1)} %add_convert_fusion), channel_id=1, source_target_pairs={{1,2},{2,1},{5,6},{6,5},{9,10},{10,9},{13,14},{14,13},{17,18},{18,... | collective-permute-start | bytes 6291464 | tf_op jit(solution)/shard_map/ppermute | solution.py:241
  134.6 15.1 %collective-permute-start.17 = (f16[128,2048]{1,0:T(8,128)(2,1)}, f16[128,2048]{1,0:T(8,128)(2,1)S(1)}, u32[]{:S(2)}, u32[]{:S(2)}) collective-permute-start(f16[128,2048]{1,0:T(8,128)(2,1)} %add_convert_fusion.3), channel_id=1, source_target_pairs={{0,1},{1,0},{2,3},{3,2},{4,5},{5,4},{6,7},{7,6},{8,9},{9,8},{10,11... | collective-permute-start | bytes 1572872 | tf_op jit(solution)/shard_map/ppermute | solution.py:241
  134.7 15.1 %collective-permute-start.15 = (bf16[256,128]{1,0:T(8,128)(2,1)S(1)}, bf16[256,128]{1,0:T(8,128)(2,1)S(1)}, u32[]{:S(2)}, u32[]{:S(2)}) collective-permute-start(bf16[256,128]{1,0:T(8,128)(2,1)S(1)} %add.238), channel_id=1, source_target_pairs={{1,0},{2,3},{5,4},{6,7},{9,8},{10,11},{13,12},{14,15},{17,16},{18,... | collective-permute-start | bytes 196616 | tf_op jit(solution)/shard_map/ppermute | solution.py:241
  142.7 39.0 %collective-permute-start.24 = (f16[384,2048]{1,0:T(8,128)(2,1)}, f16[384,2048]{1,0:T(8,128)(2,1)}, u32[]{:S(2)}, u32[]{:S(2)}) collective-permute-start(f16[384,2048]{1,0:T(8,128)(2,1)} %add_convert_fusion.2), channel_id=1, source_target_pairs={{0,1},{1,0},{2,3},{3,2},{4,5},{5,4},{6,7},{7,6},{8,9},{9,8},{10,11... | collective-permute-start | bytes 4718600 | tf_op jit(solution)/shard_map/ppermute | solution.py:241
  149.7 4.6 %copy-start.11 = (f16[128,2048]{1,0:T(8,128)(2,1)}, f16[128,2048]{1,0:T(8,128)(2,1)S(1)}, u32[]{:S(2)}) copy-start(f16[128,2048]{1,0:T(8,128)(2,1)S(1)} %collective-permute-done.17) | copy-start | bytes 1572868
  149.7 17.6 %collective-permute-start.20 = (bf16[4,64,2048]{2,1,0:T(8,128)(2,1)S(1)}, bf16[4,64,2048]{2,1,0:T(8,128)(2,1)}, u32[]{:S(2)}, u32[]{:S(2)}) collective-permute-start(bf16[4,64,2048]{2,1,0:T(8,128)(2,1)S(1)} %collective-permute-done.16), channel_id=1, source_target_pairs={{0,4},{4,0},{8,12},{12,8},{1,5},{5,1},{9,13},{13,9},{2,6},{6,2},{1... | collective-permute-start | bytes 3145736 | tf_op jit(solution)/shard_map/ppermute | solution.py:169
  149.8 17.6 %collective-permute-start.19 = (bf16[4,64,2048]{2,1,0:T(8,128)(2,1)S(1)}, bf16[4,64,2048]{2,1,0:T(8,128)(2,1)}, u32[]{:S(2)}, u32[]{:S(2)}) collective-permute-start(bf16[4,64,2048]{2,1,0:T(8,128)(2,1)S(1)} %collective-permute-done.18), channel_id=1, source_target_pairs={{0,4},{4,0},{8,12},{12,8},{1,5},{5,1},{9,13},{13,9},{2,6},{6,2},{1... | collective-permute-start | bytes 3145736 | tf_op jit(solution)/shard_map/ppermute | solution.py:169
  154.4 13.0 %collective-permute-start.22 = (bf16[4,64,2048]{2,1,0:T(8,128)(2,1)}, bf16[4,64,2048]{2,1,0:T(8,128)(2,1)}, u32[]{:S(2)}, u32[]{:S(2)}) collective-permute-start(bf16[4,64,2048]{2,1,0:T(8,128)(2,1)} %collective-permute-done.21), channel_id=1, source_target_pairs={{0,4},{4,0},{8,12},{12,8},{1,5},{5,1},{9,13},{13,9},{2,6},{6,2},{1... | collective-permute-start | bytes 3145736 | tf_op jit(solution)/shard_map/ppermute | solution.py:169
  155.0 1.2 copy-start.4
  167.3 12.8 %copy-start.12 = (f16[128,2048]{1,0:T(8,128)(2,1)S(1)}, f16[128,2048]{1,0:T(8,128)(2,1)}, u32[]{:S(2)}) copy-start(f16[128,2048]{1,0:T(8,128)(2,1)} %copy-done.11) | copy-start | bytes 1572868
  176.0 7.0 %copy-start.5 = (f32[512,2048]{1,0:T(8,128)S(1)}, f32[512,2048]{1,0:T(8,128)}, u32[]{:S(2)}) copy-start(f32[512,2048]{1,0:T(8,128)} %shard_map.76) | copy-start | bytes 12582916
  181.7 1.3 copy-start.9

commit v6 on v5

--- a/solution.py
+++ b/solution.py
@@ -285,7 +285,7 @@
 
     a3 = [hop(after(block, u2), both) for block in c1]
     part += hop(part, inner)
-    b2 = hop(after(b2, part, u2), inner)
+    b2 = hop(after(b2, part), inner)
     u1 = after(u1, part)
     late = turn(u1, 1, 1)
     low = part.astype(jnp.bfloat16)

time: 188 us -> 188 us (level)
  waiting for transfers between devices: 55.7 us -> 58.3 us
  local copies, waits for them, and re-layouts: 11.1 us -> 8.89 us
    unnamed x28 -> x22, local copies, waits for them, and re-layouts: 3.55 us -> 1.35 us
  transfers between devices with their start and end apart: 25 -> 25, of which waited for: 9 -> 10; matrix products, arithmetic and copies ran while one was open for 32% -> 32% of each run, Pallas kernels for 19% -> 19%
where the time goes in v6:
time: 188 us; the launch traced here: 187 us
  waiting for transfers between devices  58.3 us (31%)
  matrix products  38 us (20%)
  Pallas kernels  36.3 us (19%)
  starting transfers between devices  25.8 us (14%)
  other arithmetic  18.6 us (10%)
  local copies, waits for them, and re-layouts  8.89 us (5%)
    ppermute x9, waiting for transfers between devices, hop(): return lax.ppermute(block, 'tensor', pairs)  41.8 us
    dot_general x4, matrix products, product(): jnp.dot(rows_of, block, preferred_element_type=jnp.float32)  38 us
    pallas_call x2, Pallas kernels, expand(): pl.pallas_call(functools.partial(expand_kernel, rank), out_shape=jax.Shap...  19.7 us
    ppermute x9, starting transfers between devices, hop(): return lax.ppermute(block, 'tensor', pairs)  16.7 us
    pallas_call x2, Pallas kernels, shrink(): pl.pallas_call(functools.partial(shrink_kernel, rank, steps), out_shape=j...  16.6 us
    convert_element_type x4, other arithmetic, wire(): return total.astype(jnp.float16)  11.5 us
    ppermute x4, waiting for transfers between devices, cross(): lax.ppermute(after(block, *gates), 'dp', [(i, (i + shift * CORES) % owner...  10.6 us
    dynamic_update_slice x2, other arithmetic, on_device(): lax.dynamic_update_slice(lax.optimization_barrier(out), total.astype(jnp....  5.57 us
  transfers between devices with their start and end apart: 25, of which 10 were waited for; matrix products, arithmetic and copies ran while one was open for 32% of the time, Pallas kernels for 19%

profile of v6, /device:TPU:10, one launch (start us, length us, event | category | flops | bytes accessed | tf_op | source)
XLA Modules:
  0.0 187.1 jit_solution(13915406037200846159)
XLA Ops:
  0.0 0.1 add.217
  0.1 0.1 add.218
  0.2 0.8 squeeze.4
  0.9 0.8 select_reduce_fusion
  1.7 10.0 %fusion.15 = f16[512,2048]{1,0:T(8,128)(2,1)} fusion(bf16[512,2048]{1,0:T(8,128)(2,1)} %mine_ref.1, bf16[2048,8192]{1,0:T(8,128)(2,1)} %param.8, s32[]{:T(128)S(6)} %select_n.93), kind=kOutput, calls=%fused_computation.16 | convolution fusion | flops 4297064448 | bytes 12582916 | tf_op jit(solution)/shard_map/dot_general | solution.py:201
  11.7 0.5 collective-permute-start.2
  12.2 1.3 constant_dynamic-slice_fusion.3
  13.5 0.6 collective-permute-start.3
  14.1 0.6 dynamic_slice.30
  15.5 0.1 pad_add_fusion.1.ids_ref
  15.6 1.3 collective-permute-start.4
  16.9 2.3 %constant_dynamic-slice_fusion.2 = bf16[4,64,2048]{2,1,0:T(8,128)(2,1)} fusion(bf16[16,64,2048]{2,1,0:T(8,128)(2,1)} %param.9, s32[]{:T(128)S(6)} %select_n.101), kind=kLoop, calls=%fused_computation.33 | loop fusion | bytes 2097156 | tf_op jit(solution)/shard_map/dynamic_slice | solution.py:183
  19.2 9.3 %multiply_convert_fusion.1 = f16[512,2048]{1,0:T(8,128)(2,1)} fusion(bf16[512,2048]{1,0:T(8,128)(2,1)S(1)} %copy-done, bf16[2048,8192]{1,0:T(8,128)(2,1)} %param.8, s32[]{:T(128)S(6)} %select_n.97), kind=kOutput, calls=%fused_computation.11 | convolution fusion | flops 4297064448 | bytes 12582916 | tf_op jit(solution)/shard_map/dot_general | solution.py:201
  28.5 10.2 %collective-permute-done.3 = bf16[4,64,2048]{2,1,0:T(8,128)(2,1)} collective-permute-done((bf16[4,64,2048]{2,1,0:T(8,128)(2,1)S(1)}, bf16[4,64,2048]{2,1,0:T(8,128)(2,1)}, u32[]{:S(2)}, u32[]{:S(2)}) %collective-permute-start.3) | collective-permute-done | bytes 1048608 | tf_op jit(solution)/shard_map/ppermute | solution.py:184
  38.8 1.5 collective-permute-start.6
  40.3 0.5 collective-permute-start.5
  40.8 1.6 constant_dynamic-slice_fusion
  42.4 0.2 copy.15.g_ref
  42.7 9.3 %multiply_convert_fusion = f16[512,2048]{1,0:T(8,128)(2,1)} fusion(bf16[512,2048]{1,0:T(8,128)(2,1)S(1)} %copy-done, bf16[2048,8192]{1,0:T(8,128)(2,1)} %param.8, s32[]{:T(128)S(6)} %select_n.100), kind=kOutput, calls=%fused_computation.10 | convolution fusion | flops 4297064448 | bytes 12582916 | tf_op jit(solution)/shard_map/dot_general | solution.py:201
  51.9 13.9 %collective-permute-done.4 = f16[512,2048]{1,0:T(8,128)(2,1)} collective-permute-done((f16[512,2048]{1,0:T(8,128)(2,1)}, f16[512,2048]{1,0:T(8,128)(2,1)}, u32[]{:S(2)}, u32[]{:S(2)}) %collective-permute-start.4) | collective-permute-done | bytes 2097184 | tf_op jit(solution)/shard_map/ppermute | solution.py:241
  65.8 1.3 collective-permute-start.9
  67.1 1.6 collective-permute-start.7
  68.7 2.8 %add_convert_fusion.1 = f16[512,2048]{1,0:T(8,128)(2,1)S(1)} fusion(f16[512,2048]{1,0:T(8,128)(2,1)} %collective-permute-done.4, f16[512,2048]{1,0:T(8,128)(2,1)S(1)} %copy-done.3), kind=kLoop, calls=%fused_computation.9 | loop fusion | flops 4194304 | bytes 6291456 | tf_op jit(solution)/shard_map/convert_element_type | solution.py:125
  71.5 3.7 %collective-permute-start.11 = (f16[512,2048]{1,0:T(8,128)(2,1)S(1)}, f16[512,2048]{1,0:T(8,128)(2,1)}, u32[]{:S(2)}, u32[]{:S(2)}) collective-permute-start(f16[512,2048]{1,0:T(8,128)(2,1)S(1)} %add_convert_fusion.1), channel_id=1, source_target_pairs={{1,2},{2,1},{5,6},{6,5},{9,10},{10,9},{13,14},{14,13},{17,18},{18,... | collective-permute-start | bytes 6291464 | tf_op jit(solution)/shard_map/ppermute | solution.py:241
  75.2 1.6 collective-permute-start.12
  76.7 8.3 %shard_map.73 = f32[1024,128]{1,0:T(8,128)S(1)} custom-call(s32[16]{0:T(128)S(1)} %iota_add_fusion.2.ids_ref, s32[1024,1]{1,0:T(8,128)S(1)} %copy.15.g_ref, bf16[512,2048]{1,0:T(8,128)(2,1)S(1)} %copy-done, bf16[512,2048]{1,0:T(8,128)(2,1)} %collective-permute-done.2.other_ref, bf16[1024,2048]{1,0:T(8,128)(2,1)} %bitcast.28), custom_call_target="tpu_custom_call" | custom-call | flops 1 | bytes 1 | tf_op jit(solution)/shard_map/pallas_call | solution.py:54
  85.1 9.5 %fusion.base_ref = f32[512,2048]{1,0:T(8,128)} fusion(bf16[512,2048]{1,0:T(8,128)(2,1)S(1)} %copy-done, bf16[2048,8192]{1,0:T(8,128)(2,1)} %param.8, s32[]{:T(128)S(6)} %select_n.102), kind=kOutput, calls=%fused_computation | convolution fusion | flops 4294967296 | bytes 14680068 | tf_op jit(solution)/shard_map/dot_general | solution.py:201
  94.5 8.3 %shard_map.74 = f32[1024,128]{1,0:T(8,128)S(1)} custom-call(s32[16]{0:T(128)S(1)} %pad_add_fusion.1.ids_ref, s32[1024,1]{1,0:T(8,128)S(1)} %copy.15.g_ref, bf16[512,2048]{1,0:T(8,128)(2,1)} %mine_ref.1, bf16[512,2048]{1,0:T(8,128)(2,1)} %collective-permute-done.2.other_ref, bf16[256,2048]{1,0:T(8,128)(2,1)} %bitcast.5.refs_0_, ...), custom_call_target="tpu_custom_call" | custom-call | flops 1 | bytes 1 | tf_op jit(solution)/shard_map/pallas_call | solution.py:54
  102.9 0.1 add.231
  103.0 0.2 slice_add_fusion.2
  103.2 0.1 collective-permute-start.8
  103.3 0.6 collective-permute-start.16
  103.9 0.2 collective-permute-start.13
  104.0 0.8 collective-permute-done.8
  104.8 0.5 collective-permute-start.18
  105.4 0.1 pad_maximum_fusion
  105.5 9.5 %collective-permute-done.9 = f16[512,2048]{1,0:T(8,128)(2,1)S(1)} collective-permute-done((f16[512,2048]{1,0:T(8,128)(2,1)S(1)}, f16[512,2048]{1,0:T(8,128)(2,1)S(1)}, u32[]{:S(2)}, u32[]{:S(2)}) %collective-permute-start.9) | collective-permute-done | bytes 2097184 | tf_op jit(solution)/shard_map/ppermute | solution.py:241
  115.0 2.5 %add_convert_fusion = f16[512,2048]{1,0:T(8,128)(2,1)} fusion(f16[512,2048]{1,0:T(8,128)(2,1)S(1)} %collective-permute-done.9, f16[512,2048]{1,0:T(8,128)(2,1)S(1)} %copy-done.4), kind=kLoop, calls=%fused_computation.8 | loop fusion | flops 4194304 | bytes 6291456 | tf_op jit(solution)/shard_map/convert_element_type | solution.py:125
  117.5 3.0 %collective-permute-done.11 = f16[512,2048]{1,0:T(8,128)(2,1)} collective-permute-done((f16[512,2048]{1,0:T(8,128)(2,1)S(1)}, f16[512,2048]{1,0:T(8,128)(2,1)}, u32[]{:S(2)}, u32[]{:S(2)}) %collective-permute-start.11) | collective-permute-done | bytes 2097184 | tf_op jit(solution)/shard_map/ppermute | solution.py:241
  120.5 2.2 %add_convert_fusion.3 = f16[128,2048]{1,0:T(8,128)(2,1)} fusion(f16[512,2048]{1,0:T(8,128)(2,1)} %collective-permute-done.11, f16[512,2048]{1,0:T(8,128)(2,1)} %multiply_convert_fusion), kind=kLoop, calls=%fused_computation.20 | loop fusion | flops 1048576 | bytes 1572864 | tf_op jit(solution)/shard_map/convert_element_type | solution.py:125
  122.7 0.1 fusion.31
  122.8 3.5 %collective-permute-start.14 = (f32[256,128]{1,0:T(8,128)S(1)}, f32[256,128]{1,0:T(8,128)S(1)}, u32[]{:S(2)}, u32[]{:S(2)}) collective-permute-start(f32[256,128]{1,0:T(8,128)S(1)} %fusion.31), channel_id=1, source_target_pairs={{1,2},{2,1},{5,6},{6,5},{9,10},{10,9},{13,14},{14,13},{17,18},{18,... | collective-permute-start | bytes 393224 | tf_op jit(solution)/shard_map/ppermute | solution.py:241
  126.3 3.4 %collective-permute-done.14 = f32[256,128]{1,0:T(8,128)S(1)} collective-permute-done((f32[256,128]{1,0:T(8,128)S(1)}, f32[256,128]{1,0:T(8,128)S(1)}, u32[]{:S(2)}, u32[]{:S(2)}) %collective-permute-start.14) | collective-permute-done | bytes 131104 | tf_op jit(solution)/shard_map/ppermute | solution.py:241
  129.7 0.3 collective-permute-done.18
  130.0 1.0 collective-permute-start.21
  131.0 2.8 %collective-permute-start.23 = (f16[512,2048]{1,0:T(8,128)(2,1)}, f16[512,2048]{1,0:T(8,128)(2,1)}, u32[]{:S(2)}, u32[]{:S(2)}) collective-permute-start(f16[512,2048]{1,0:T(8,128)(2,1)} %add_convert_fusion), channel_id=1, source_target_pairs={{1,2},{2,1},{5,6},{6,5},{9,10},{10,9},{13,14},{14,13},{17,18},{18,... | collective-permute-start | bytes 6291464 | tf_op jit(solution)/shard_map/ppermute | solution.py:241
  133.7 0.2 collective-permute-start.17
  133.9 4.0 %collective-permute-start.15 = (bf16[256,128]{1,0:T(8,128)(2,1)S(1)}, bf16[256,128]{1,0:T(8,128)(2,1)S(1)}, u32[]{:S(2)}, u32[]{:S(2)}) collective-permute-start(bf16[256,128]{1,0:T(8,128)(2,1)S(1)} %add.238), channel_id=1, source_target_pairs={{1,0},{2,3},{5,4},{6,7},{9,8},{10,11},{13,12},{14,15},{17,16},{18,... | collective-permute-start | bytes 196616 | tf_op jit(solution)/shard_map/ppermute | solution.py:241
  138.0 3.9 %add_convert_fusion.2 = f16[384,2048]{1,0:T(8,128)(2,1)} fusion(f16[512,2048]{1,0:T(8,128)(2,1)} %collective-permute-done.11, f16[512,2048]{1,0:T(8,128)(2,1)} %multiply_convert_fusion), kind=kLoop, calls=%fused_computation.15 | loop fusion | flops 3145728 | bytes 4718592 | tf_op jit(solution)/shard_map/convert_element_type | solution.py:125
  141.9 7.0 %collective-permute-done.17 = f16[128,2048]{1,0:T(8,128)(2,1)S(1)} collective-permute-done((f16[128,2048]{1,0:T(8,128)(2,1)}, f16[128,2048]{1,0:T(8,128)(2,1)S(1)}, u32[]{:S(2)}, u32[]{:S(2)}) %collective-permute-start.17) | collective-permute-done | bytes 524320 | tf_op jit(solution)/shard_map/ppermute | solution.py:241
  148.9 0.5 collective-permute-start.19
  149.4 5.1 %collective-permute-done.21 = bf16[4,64,2048]{2,1,0:T(8,128)(2,1)} collective-permute-done((bf16[4,64,2048]{2,1,0:T(8,128)(2,1)S(1)}, bf16[4,64,2048]{2,1,0:T(8,128)(2,1)}, u32[]{:S(2)}, u32[]{:S(2)}) %collective-permute-start.21) | collective-permute-done | bytes 1048608 | tf_op jit(solution)/shard_map/ppermute | solution.py:190
  154.5 0.1 concatenate.23.ids_ref
  154.6 0.1 pad_add_fusion.2.ids_ref
  154.7 0.1 copy.18.g_ref
  154.9 0.1 fusion.26
  155.0 0.1 maximum_maximum_fusion.low_ref
  155.1 11.1 %shard_map.75.base_ref = f32[512,2048]{1,0:T(8,128)} custom-call(s32[40]{0:T(128)S(1)} %pad_add_fusion.2.ids_ref, s32[512,1]{1,0:T(8,128)S(1)} %copy.18.g_ref, bf16[512,128]{1,0:T(8,128)(2,1)S(1)} %maximum_maximum_fusion.low_ref, f32[512,2048]{1,0:T(8,128)} %fusion.base_ref, bf16[1024,2048]{1,0:T(8,128)(2,1)} %bitcast.29, ...), custom_call_target="tpu_custom_call" | custom-call | flops 1 | bytes 1 | tf_op jit(solution)/shard_map/pallas_call | solution.py:100
  166.2 8.6 %shard_map.76 = f32[512,2048]{1,0:T(8,128)} custom-call(s32[24]{0:T(128)S(1)} %concatenate.23.ids_ref, s32[512,1]{1,0:T(8,128)S(1)} %copy.18.g_ref, bf16[512,128]{1,0:T(8,128)(2,1)S(1)} %maximum_maximum_fusion.low_ref, f32[512,2048]{1,0:T(8,128)} %shard_map.75.base_ref, bf16[256,2048]{1,0:T(8,128)(2,1)S(1)} %bitcast.25, bf16[256,2048]{1,0:T(8,128)(2,1)S(1)} %bitcast.24, ...), custom_call_target="tpu_custom_call" | custom-call | flops 1 | bytes 1 | tf_op jit(solution)/shard_map/pallas_call | solution.py:100
  174.8 5.2 %collective-permute-done.23 = f16[512,2048]{1,0:T(8,128)(2,1)} collective-permute-done((f16[512,2048]{1,0:T(8,128)(2,1)}, f16[512,2048]{1,0:T(8,128)(2,1)}, u32[]{:S(2)}, u32[]{:S(2)}) %collective-permute-start.23) | collective-permute-done | bytes 2097184 | tf_op jit(solution)/shard_map/ppermute | solution.py:241
  180.0 0.2 broadcast_in_dim.25
  180.2 1.6 fusion.20
  181.8 1.3 copy-done.5
  183.1 4.0 %fusion.18 = bf16[512,2048]{1,0:T(8,128)(2,1)} fusion(bf16[512,2048]{1,0:T(8,128)(2,1)} %copy-done.5, f16[384,2048]{1,0:T(8,128)(2,1)} %collective-permute-done.24, f32[512,2048]{1,0:T(8,128)S(1)} %copy-done.1, f16[512,2048]{1,0:T(8,128)(2,1)} %collective-permute-done.23), kind=kLoop, calls=%fused_computation.17 | loop fusion | flops 4718592 | bytes 7864320 | tf_op jit(solution)/shard_map/dynamic_update_slice | solution.py:300
  (58 shorter events, 0.3 us)
Async XLA Ops:
  0.0 11.7 %collective-permute-start = (bf16[16,64,2048]{2,1,0:T(8,128)(2,1)}, bf16[16,64,2048]{2,1,0:T(8,128)(2,1)}, u32[]{:S(2)}, u32[]{:S(2)}) collective-permute-start(bf16[16,64,2048]{2,1,0:T(8,128)(2,1)} %param.10), channel_id=1, source_target_pairs={{0,4},{4,0},{8,12},{12,8},{1,5},{5,1},{9,13},{13,9},{2,6},{6,2},{1... | collective-permute-start | bytes 12582920 | tf_op jit(solution)/shard_map/ppermute | solution.py:169
  1.7 10.0 %copy-start = (bf16[512,2048]{1,0:T(8,128)(2,1)S(1)}, bf16[512,2048]{1,0:T(8,128)(2,1)}, u32[]{:S(2)}) copy-start(bf16[512,2048]{1,0:T(8,128)(2,1)} %mine_ref.1) | copy-start | bytes 6291460
  1.7 12.4 %copy-start.10 = (s32[4]{0:T(128)S(1)}, s32[4]{0:T(128)}, u32[]{:S(2)}) copy-start(s32[4]{0:T(128)} %constant.101.clone) | copy-start | bytes 52
  11.7 7.5 %collective-permute-start.2 = (bf16[512,2048]{1,0:T(8,128)(2,1)S(1)}, bf16[512,2048]{1,0:T(8,128)(2,1)}, u32[]{:S(2)}, u32[]{:S(2)}) collective-permute-start(bf16[512,2048]{1,0:T(8,128)(2,1)S(1)} %copy-done), channel_id=1, source_target_pairs={{0,4},{4,0},{8,12},{12,8},{1,5},{5,1},{9,13},{13,9},{2,6},{6,2},{1... | collective-permute-start | bytes 6291464 | tf_op jit(solution)/shard_map/ppermute | solution.py:169
  13.5 25.3 %collective-permute-start.3 = (bf16[4,64,2048]{2,1,0:T(8,128)(2,1)S(1)}, bf16[4,64,2048]{2,1,0:T(8,128)(2,1)}, u32[]{:S(2)}, u32[]{:S(2)}) collective-permute-start(bf16[4,64,2048]{2,1,0:T(8,128)(2,1)S(1)} %constant_dynamic-slice_fusion.3), channel_id=1, source_target_pairs={{0,8},{4,12},{8,0},{12,4},{1,9},{5,13},{9,1},{13,5},{2,10},{6,14},... | collective-permute-start | bytes 3145736 | tf_op jit(solution)/shard_map/ppermute | solution.py:184
  15.6 3.6 %collective-permute-start.1 = (s32[512]{0:T(512)S(1)}, s32[512]{0:T(512)S(1)}, u32[]{:S(2)}, u32[]{:S(2)}) collective-permute-start(s32[512]{0:T(512)S(1)} %select_reduce_fusion), channel_id=1, source_target_pairs={{0,4},{4,0},{8,12},{12,8},{1,5},{5,1},{9,13},{13,9},{2,6},{6,2},{1... | collective-permute-start | bytes 6152 | tf_op jit(solution)/shard_map/ppermute | solution.py:169
  15.6 50.2 %collective-permute-start.4 = (f16[512,2048]{1,0:T(8,128)(2,1)}, f16[512,2048]{1,0:T(8,128)(2,1)}, u32[]{:S(2)}, u32[]{:S(2)}) collective-permute-start(f16[512,2048]{1,0:T(8,128)(2,1)} %fusion.15), channel_id=1, source_target_pairs={{0,1},{3,2},{4,5},{7,6},{8,9},{11,10},{12,13},{15,14},{16,17},{19,... | collective-permute-start | bytes 6291464 | tf_op jit(solution)/shard_map/ppermute | solution.py:241
  19.2 21.6 %copy-start.2 = (bf16[16,64,2048]{2,1,0:T(8,128)(2,1)S(1)}, bf16[16,64,2048]{2,1,0:T(8,128)(2,1)}, u32[]{:S(2)}) copy-start(bf16[16,64,2048]{2,1,0:T(8,128)(2,1)} %param.10) | copy-start | bytes 12582916
  38.8 27.0 %collective-permute-start.6 = (bf16[4,64,2048]{2,1,0:T(8,128)(2,1)}, bf16[4,64,2048]{2,1,0:T(8,128)(2,1)}, u32[]{:S(2)}, u32[]{:S(2)}) collective-permute-start(bf16[4,64,2048]{2,1,0:T(8,128)(2,1)} %collective-permute-done.3), channel_id=1, source_target_pairs={{0,16},{16,0},{1,17},{17,1},{2,18},{18,2},{3,19},{19,3},{4,20},{20... | collective-permute-start | bytes 3145736 | tf_op jit(solution)/shard_map/ppermute | solution.py:190
  40.3 25.5 %collective-permute-start.5 = (bf16[4,64,2048]{2,1,0:T(8,128)(2,1)}, bf16[4,64,2048]{2,1,0:T(8,128)(2,1)}, u32[]{:S(2)}, u32[]{:S(2)}) collective-permute-start(bf16[4,64,2048]{2,1,0:T(8,128)(2,1)} %constant_dynamic-slice_fusion.2), channel_id=1, source_target_pairs={{0,8},{4,12},{8,0},{12,4},{1,9},{5,13},{9,1},{13,5},{2,10},{6,14},... | collective-permute-start | bytes 3145736 | tf_op jit(solution)/shard_map/ppermute | solution.py:184
  42.7 23.2 %copy-start.4 = (f16[512,2048]{1,0:T(8,128)(2,1)S(1)}, f16[512,2048]{1,0:T(8,128)(2,1)}, u32[]{:S(2)}) copy-start(f16[512,2048]{1,0:T(8,128)(2,1)} %multiply_convert_fusion.1) | copy-start | bytes 6291460
  42.7 26.0 %copy-start.3 = (f16[512,2048]{1,0:T(8,128)(2,1)S(1)}, f16[512,2048]{1,0:T(8,128)(2,1)}, u32[]{:S(2)}) copy-start(f16[512,2048]{1,0:T(8,128)(2,1)} %fusion.15) | copy-start | bytes 6291460
  51.9 23.3 %copy-start.7 = (bf16[4,64,2048]{2,1,0:T(8,128)(2,1)S(1)}, bf16[4,64,2048]{2,1,0:T(8,128)(2,1)}, u32[]{:S(2)}) copy-start(bf16[4,64,2048]{2,1,0:T(8,128)(2,1)} %get-tuple-element.63) | copy-start | bytes 3145732
  65.8 49.1 %collective-permute-start.9 = (f16[512,2048]{1,0:T(8,128)(2,1)S(1)}, f16[512,2048]{1,0:T(8,128)(2,1)S(1)}, u32[]{:S(2)}, u32[]{:S(2)}) collective-permute-start(f16[512,2048]{1,0:T(8,128)(2,1)S(1)} %copy-done.4), channel_id=1, source_target_pairs={{0,1},{3,2},{4,5},{7,6},{8,9},{11,10},{12,13},{15,14},{16,17},{19,... | collective-permute-start | bytes 6291464 | tf_op jit(solution)/shard_map/ppermute | solution.py:241
  67.1 27.4 %collective-permute-start.7 = (bf16[4,64,2048]{2,1,0:T(8,128)(2,1)}, bf16[4,64,2048]{2,1,0:T(8,128)(2,1)S(1)}, u32[]{:S(2)}, u32[]{:S(2)}) collective-permute-start(bf16[4,64,2048]{2,1,0:T(8,128)(2,1)} %collective-permute-done.5), channel_id=1, source_target_pairs={{0,16},{16,0},{1,17},{17,1},{2,18},{18,2},{3,19},{19,3},{4,20},{20... | collective-permute-start | bytes 3145736 | tf_op jit(solution)/shard_map/ppermute | solution.py:190
  71.5 49.0 %collective-permute-start.11 = (f16[512,2048]{1,0:T(8,128)(2,1)S(1)}, f16[512,2048]{1,0:T(8,128)(2,1)}, u32[]{:S(2)}, u32[]{:S(2)}) collective-permute-start(f16[512,2048]{1,0:T(8,128)(2,1)S(1)} %add_convert_fusion.1), channel_id=1, source_target_pairs={{1,2},{2,1},{5,6},{6,5},{9,10},{10,9},{13,14},{14,13},{17,18},{18,... | collective-permute-start | bytes 6291464 | tf_op jit(solution)/shard_map/ppermute | solution.py:241
  75.2 28.1 %collective-permute-start.12 = (bf16[4,64,2048]{2,1,0:T(8,128)(2,1)S(1)}, bf16[4,64,2048]{2,1,0:T(8,128)(2,1)}, u32[]{:S(2)}, u32[]{:S(2)}) collective-permute-start(bf16[4,64,2048]{2,1,0:T(8,128)(2,1)S(1)} %copy-done.7), channel_id=1, source_target_pairs={{0,8},{4,12},{8,0},{12,4},{1,9},{5,13},{9,1},{13,5},{2,10},{6,14},... | collective-permute-start | bytes 3145736 | tf_op jit(solution)/shard_map/ppermute | solution.py:184
  102.9 1.9 %copy-start.6 = (bf16[4,64,2048]{2,1,0:T(8,128)(2,1)S(1)}, bf16[4,64,2048]{2,1,0:T(8,128)(2,1)}, u32[]{:S(2)}) copy-start(bf16[4,64,2048]{2,1,0:T(8,128)(2,1)} %get-tuple-element.74) | copy-start | bytes 3145732
  103.2 1.6 collective-permute-start.8
  103.3 30.5 %collective-permute-start.16 = (bf16[4,64,2048]{2,1,0:T(8,128)(2,1)}, bf16[4,64,2048]{2,1,0:T(8,128)(2,1)S(1)}, u32[]{:S(2)}, u32[]{:S(2)}) collective-permute-start(bf16[4,64,2048]{2,1,0:T(8,128)(2,1)} %collective-permute-done.12), channel_id=1, source_target_pairs={{0,16},{16,0},{1,17},{17,1},{2,18},{18,2},{3,19},{19,3},{4,20},{20... | collective-permute-start | bytes 3145736 | tf_op jit(solution)/shard_map/ppermute | solution.py:190
  103.9 18.9 %collective-permute-start.13 = (bf16[4,64,2048]{2,1,0:T(8,128)(2,1)}, bf16[4,64,2048]{2,1,0:T(8,128)(2,1)S(1)}, u32[]{:S(2)}, u32[]{:S(2)}) collective-permute-start(bf16[4,64,2048]{2,1,0:T(8,128)(2,1)} %collective-permute-done.12), channel_id=1, source_target_pairs={{0,4},{4,0},{8,12},{12,8},{1,5},{5,1},{9,13},{13,9},{2,6},{6,2},{1... | collective-permute-start | bytes 3145736 | tf_op jit(solution)/shard_map/ppermute | solution.py:169
  104.8 25.2 %collective-permute-start.18 = (bf16[4,64,2048]{2,1,0:T(8,128)(2,1)S(1)}, bf16[4,64,2048]{2,1,0:T(8,128)(2,1)S(1)}, u32[]{:S(2)}, u32[]{:S(2)}) collective-permute-start(bf16[4,64,2048]{2,1,0:T(8,128)(2,1)S(1)} %copy-done.6), channel_id=1, source_target_pairs={{0,8},{4,12},{8,0},{12,4},{1,9},{5,13},{9,1},{13,5},{2,10},{6,14},... | collective-permute-start | bytes 3145736 | tf_op jit(solution)/shard_map/ppermute | solution.py:184
  115.0 7.7 %collective-permute-start.10 = (f32[256,128]{1,0:T(8,128)S(1)}, f32[256,128]{1,0:T(8,128)S(1)}, u32[]{:S(2)}, u32[]{:S(2)}) collective-permute-start(f32[256,128]{1,0:T(8,128)S(1)} %pad_maximum_fusion), channel_id=1, source_target_pairs={{0,1},{1,0},{2,3},{3,2},{4,5},{5,4},{6,7},{7,6},{8,9},{9,8},{10,11... | collective-permute-start | bytes 393224 | tf_op jit(solution)/shard_map/ppermute | solution.py:241
  122.8 6.9 %collective-permute-start.14 = (f32[256,128]{1,0:T(8,128)S(1)}, f32[256,128]{1,0:T(8,128)S(1)}, u32[]{:S(2)}, u32[]{:S(2)}) collective-permute-start(f32[256,128]{1,0:T(8,128)S(1)} %fusion.31), channel_id=1, source_target_pairs={{1,2},{2,1},{5,6},{6,5},{9,10},{10,9},{13,14},{14,13},{17,18},{18,... | collective-permute-start | bytes 393224 | tf_op jit(solution)/shard_map/ppermute | solution.py:241
  130.0 24.5 %collective-permute-start.21 = (bf16[4,64,2048]{2,1,0:T(8,128)(2,1)S(1)}, bf16[4,64,2048]{2,1,0:T(8,128)(2,1)}, u32[]{:S(2)}, u32[]{:S(2)}) collective-permute-start(bf16[4,64,2048]{2,1,0:T(8,128)(2,1)S(1)} %collective-permute-done.18), channel_id=1, source_target_pairs={{0,16},{16,0},{1,17},{17,1},{2,18},{18,2},{3,19},{19,3},{4,20},{20... | collective-permute-start | bytes 3145736 | tf_op jit(solution)/shard_map/ppermute | solution.py:190
  131.0 49.0 %collective-permute-start.23 = (f16[512,2048]{1,0:T(8,128)(2,1)}, f16[512,2048]{1,0:T(8,128)(2,1)}, u32[]{:S(2)}, u32[]{:S(2)}) collective-permute-start(f16[512,2048]{1,0:T(8,128)(2,1)} %add_convert_fusion), channel_id=1, source_target_pairs={{1,2},{2,1},{5,6},{6,5},{9,10},{10,9},{13,14},{14,13},{17,18},{18,... | collective-permute-start | bytes 6291464 | tf_op jit(solution)/shard_map/ppermute | solution.py:241
  133.7 15.1 %collective-permute-start.17 = (f16[128,2048]{1,0:T(8,128)(2,1)}, f16[128,2048]{1,0:T(8,128)(2,1)S(1)}, u32[]{:S(2)}, u32[]{:S(2)}) collective-permute-start(f16[128,2048]{1,0:T(8,128)(2,1)} %add_convert_fusion.3), channel_id=1, source_target_pairs={{0,1},{1,0},{2,3},{3,2},{4,5},{5,4},{6,7},{7,6},{8,9},{9,8},{10,11... | collective-permute-start | bytes 1572872 | tf_op jit(solution)/shard_map/ppermute | solution.py:241
  133.9 15.0 %collective-permute-start.15 = (bf16[256,128]{1,0:T(8,128)(2,1)S(1)}, bf16[256,128]{1,0:T(8,128)(2,1)S(1)}, u32[]{:S(2)}, u32[]{:S(2)}) collective-permute-start(bf16[256,128]{1,0:T(8,128)(2,1)S(1)} %add.238), channel_id=1, source_target_pairs={{1,0},{2,3},{5,4},{6,7},{9,8},{10,11},{13,12},{14,15},{17,16},{18,... | collective-permute-start | bytes 196616 | tf_op jit(solution)/shard_map/ppermute | solution.py:241
  141.9 39.9 %collective-permute-start.24 = (f16[384,2048]{1,0:T(8,128)(2,1)}, f16[384,2048]{1,0:T(8,128)(2,1)}, u32[]{:S(2)}, u32[]{:S(2)}) collective-permute-start(f16[384,2048]{1,0:T(8,128)(2,1)} %add_convert_fusion.2), channel_id=1, source_target_pairs={{0,1},{1,0},{2,3},{3,2},{4,5},{5,4},{6,7},{7,6},{8,9},{9,8},{10,11... | collective-permute-start | bytes 4718600 | tf_op jit(solution)/shard_map/ppermute | solution.py:241
  148.9 5.6 %copy-start.8 = (f16[128,2048]{1,0:T(8,128)(2,1)}, f16[128,2048]{1,0:T(8,128)(2,1)S(1)}, u32[]{:S(2)}) copy-start(f16[128,2048]{1,0:T(8,128)(2,1)S(1)} %collective-permute-done.17) | copy-start | bytes 1572868
  148.9 17.3 %collective-permute-start.20 = (bf16[4,64,2048]{2,1,0:T(8,128)(2,1)S(1)}, bf16[4,64,2048]{2,1,0:T(8,128)(2,1)}, u32[]{:S(2)}, u32[]{:S(2)}) collective-permute-start(bf16[4,64,2048]{2,1,0:T(8,128)(2,1)S(1)} %collective-permute-done.16), channel_id=1, source_target_pairs={{0,4},{4,0},{8,12},{12,8},{1,5},{5,1},{9,13},{13,9},{2,6},{6,2},{1... | collective-permute-start | bytes 3145736 | tf_op jit(solution)/shard_map/ppermute | solution.py:169
  148.9 17.3 %collective-permute-start.19 = (bf16[4,64,2048]{2,1,0:T(8,128)(2,1)S(1)}, bf16[4,64,2048]{2,1,0:T(8,128)(2,1)}, u32[]{:S(2)}, u32[]{:S(2)}) collective-permute-start(bf16[4,64,2048]{2,1,0:T(8,128)(2,1)S(1)} %collective-permute-done.18), channel_id=1, source_target_pairs={{0,4},{4,0},{8,12},{12,8},{1,5},{5,1},{9,13},{13,9},{2,6},{6,2},{1... | collective-permute-start | bytes 3145736 | tf_op jit(solution)/shard_map/ppermute | solution.py:169
  154.5 11.7 %collective-permute-start.22 = (bf16[4,64,2048]{2,1,0:T(8,128)(2,1)}, bf16[4,64,2048]{2,1,0:T(8,128)(2,1)}, u32[]{:S(2)}, u32[]{:S(2)}) collective-permute-start(bf16[4,64,2048]{2,1,0:T(8,128)(2,1)} %collective-permute-done.21), channel_id=1, source_target_pairs={{0,4},{4,0},{8,12},{12,8},{1,5},{5,1},{9,13},{13,9},{2,6},{6,2},{1... | collective-permute-start | bytes 3145736 | tf_op jit(solution)/shard_map/ppermute | solution.py:169
  166.2 14.0 %copy-start.9 = (f16[128,2048]{1,0:T(8,128)(2,1)S(1)}, f16[128,2048]{1,0:T(8,128)(2,1)}, u32[]{:S(2)}) copy-start(f16[128,2048]{1,0:T(8,128)(2,1)} %copy-done.8) | copy-start | bytes 1572868
  174.8 8.3 %copy-start.1 = (f32[512,2048]{1,0:T(8,128)S(1)}, f32[512,2048]{1,0:T(8,128)}, u32[]{:S(2)}) copy-start(f32[512,2048]{1,0:T(8,128)} %shard_map.76) | copy-start | bytes 12582916
  181.8 1.3 copy-start.5
